TPU v7x, 128 devices: a whole 4x4x4 slice. The times are simulated.
128 devices in a mesh: res: 32 (over z, y, core), col: 4 (over x).
Axes of the slice: x: 4, y: 4, z: 4, core: 2. Of those that a mesh axis runs over, the one named last changes fastest.
Arguments:
- homolog_embedding: bfloat16 [128, 1536, 256], P('res', 'col'), may hold values from -6 to 6
- sequence_row_mask: bfloat16 [128, 8], P('res'), may hold values from 0 to 1, as said below
- residue_chain_index: int32 [1536], P('col'), may hold values from 0 to 7, never falling along the last dimension, each value on 1 to 384 neighbouring positions
- standardize_factor: float32 [256], replicated, may hold values from 0.1 to 1.9
- standardize_shift: float32 [256], replicated, may hold values from -3 to 3
- first_projector_matrix: bfloat16 [256, 32], replicated, may hold values from -0.375 to 0.375
- second_projector_matrix: bfloat16 [256, 32], replicated, may hold values from -0.375 to 0.375
- output_weight: bfloat16 [1024, 128], replicated, may hold values from -1 to 1
Outputs:
- pair_update: bfloat16 [1536, 1536, 128], P('res', 'col')
Inputs may be any that keep to these rules, and one draw needn't show every extreme that they name: `sequence_row_mask`: row 0 is all ones. `residue_chain_index`: chain numbers never fall along the residues.
All inputs are finite; a program needn't handle non-finite values.
Results may differ from a plain program's by a relative error of at most 0.0063.
Values may be sent and summed in bfloat16 or wider, within the bound.
No kernel may reach another device: no remote copies, remote signals or barrier semaphores. Data moves between devices by JAX's collectives and lax.ppermute only.
A program may use at most 192 MiB of HBM per device.

v0:
```python
import math

import jax
import jax.numpy as jnp
from jax import lax
from jax.sharding import PartitionSpec as P


def apply_layer_norm(feats, standardize_factor, standardize_shift):
    wide = feats.astype(jnp.float32)
    centre = jnp.mean(wide, axis=-1, keepdims=True)
    shifted = wide - centre
    variance = jnp.mean(shifted * shifted, axis=-1, keepdims=True)
    return shifted * lax.rsqrt(variance + 1e-05) * standardize_factor + standardize_shift


def local(
    homolog_embedding,
    sequence_row_mask,
    residue_chain_index,
    standardize_factor,
    standardize_shift,
    first_projector_matrix,
    second_projector_matrix,
    output_weight,
):
    chain_count = sequence_row_mask.shape[1]
    onehot = (
        residue_chain_index[None, :] == jnp.arange(chain_count, dtype=jnp.int32)[:, None]
    ).astype(jnp.float32)
    seq_mask = jnp.dot(
        sequence_row_mask.astype(jnp.float32), onehot, precision=lax.Precision.HIGHEST
    )
    normalized_input = apply_layer_norm(
        homolog_embedding, standardize_factor, standardize_shift
    ).astype(jnp.bfloat16)

    def project(weight):
        moved = jnp.einsum(
            "src,ch->srh", normalized_input, weight, preferred_element_type=jnp.float32
        )
        return (moved * seq_mask[:, :, None]).astype(jnp.bfloat16)

    left_local = project(first_projector_matrix)
    right_local = project(second_projector_matrix)
    mask_local = seq_mask.astype(jnp.bfloat16)
    column_width = homolog_embedding.shape[1]
    left_every, right_every, mask_every = (
        lax.all_gather(left_local, "col", axis=1, tiled=True),
        lax.all_gather(right_local, "col", axis=1, tiled=True),
        lax.all_gather(mask_local, "col", axis=1, tiled=True),
    )
    left_rows, right_rows, mask_rows = (
        lax.all_to_all(left_every, "res", split_axis=1, concat_axis=0, tiled=True),
        lax.all_to_all(right_every, "res", split_axis=1, concat_axis=0, tiled=True),
        lax.all_to_all(mask_every, "res", split_axis=1, concat_axis=0, tiled=True),
    )
    right_all, mask_all = (
        lax.all_gather(right_rows, "res", axis=1, tiled=True),
        lax.all_gather(mask_rows, "res", axis=1, tiled=True),
    )
    offset = lax.axis_index("col") * column_width
    right_cols = lax.dynamic_slice_in_dim(right_all, offset, column_width, 1)
    mask_cols = lax.dynamic_slice_in_dim(mask_all, offset, column_width, 1)
    row_count = left_rows.shape[1]
    side_width = left_rows.shape[2]
    block_rows = math.gcd(row_count, 8)
    w_cube = output_weight.reshape(side_width, side_width, output_weight.shape[1])

    def one_block(row_start):
        left_part = lax.dynamic_slice_in_dim(left_rows, row_start, block_rows, 1)
        mask_part = lax.dynamic_slice_in_dim(mask_rows, row_start, block_rows, 1)
        outer_prod = jnp.einsum(
            "sip,sjq->ipjq", left_part, right_cols, preferred_element_type=jnp.float32
        ).astype(jnp.bfloat16)
        projected = jnp.einsum(
            "ipjq,pqz->ijz", outer_prod, w_cube, preferred_element_type=jnp.float32
        )
        counts = jnp.einsum("si,sj->ij", mask_part, mask_cols, preferred_element_type=jnp.float32)
        return (projected / (counts[:, :, None] + 0.001)).astype(jnp.bfloat16)

    starts = jnp.arange(row_count // block_rows, dtype=jnp.int32) * block_rows
    blocks = lax.map(one_block, starts)
    return blocks.reshape(row_count, column_width, output_weight.shape[1])


def solution(mesh):
    in_specs = (P("res", "col", None), P("res", None), P("col"), P(), P(), P(), P(), P())
    out_specs = P("res", "col", None)
    return jax.shard_map(local, mesh=mesh, in_specs=in_specs, out_specs=out_specs, check_vma=False)
```

profile of v0, /device:TPU:1, one launch (start us, length us, event | category | flops | bytes accessed | tf_op | source)
XLA Modules:
  0.0 340.0 jit_solution(8510652302373074275)
XLA Ops:
  6.6 1.5 convert_reduce_fusion
  8.1 1.6 fusion.11
  9.8 0.1 fusion.22
  9.9 0.6 fusion.16
  10.5 11.7 %all_gather.16 = bf16[4,1536,32]{1,2,0:T(8,128)(2,1)S(1)} all-gather(bf16[4,384,32]{1,2,0:T(8,128)(2,1)S(1)} %fusion.16), channel_id=1, replica_groups=mesh['res'=32,'col'=4] {'col'}, dimensions={1}, use_global_device_ids=true | all-gather | bytes 491520 | tf_op jit(solution)/shard_map/all_gather | solution.py:50
  22.2 1.0 copy.14
  23.3 1.5 reshape.37
  24.8 20.9 %all_to_all.55 = bf16[32,2,3072]{2,1,0:T(2,128)(2,1)S(1)} all-to-all(bf16[32,2,3072]{2,1,0:T(2,128)(2,1)S(1)} %reshape.37), channel_id=1, replica_groups=mesh['res'=32,'col'=4] {'res'}, dimensions={0} | all-to-all | bytes 786432 | tf_op jit(solution)/shard_map/all_to_all | solution.py:55
  45.7 0.7 reshape.38
  46.4 1.4 copy.15
  47.9 9.0 %all_gather.18 = bf16[4,1536]{1,0:T(4,128)(2,1)S(1)} all-gather(bf16[4,384]{1,0:T(4,128)(2,1)S(1)} %get-tuple-element.72), channel_id=1, replica_groups=mesh['res'=32,'col'=4] {'col'}, dimensions={1}, use_global_device_ids=true | all-gather | bytes 15360 | tf_op jit(solution)/shard_map/all_gather | solution.py:51
  56.9 0.1 all_to_all.48
  57.0 0.6 copy.16
  57.6 6.8 %all-to-all-start.2 = ((bf16[4,32,48]{2,0,1:T(4,128)(2,1)}), bf16[4,32,48]{2,0,1:T(4,128)(2,1)S(1)}, u32[]{:S(2)}, u32[]{:S(2)}) async-start(bf16[4,32,48]{2,0,1:T(4,128)(2,1)} %copy.16), calls=%async_computation.2 | async-start | bytes 65536 | tf_op jit(solution)/shard_map/all_to_all | solution.py:56
  64.4 0.6 fusion.15
  65.0 11.1 %all_gather.15 = bf16[4,1536,32]{1,2,0:T(8,128)(2,1)S(1)} all-gather(bf16[4,384,32]{1,2,0:T(8,128)(2,1)S(1)} %fusion.15), channel_id=1, replica_groups=mesh['res'=32,'col'=4] {'col'}, dimensions={1}, use_global_device_ids=true | all-gather | bytes 491520 | tf_op jit(solution)/shard_map/all_gather | solution.py:49
  76.1 1.0 copy.12
  77.2 2.2 reshape.35
  79.4 9.1 %all-to-all-start = ((bf16[32,2,3072]{2,1,0:T(2,128)(2,1)}), bf16[32,2,3072]{2,1,0:T(2,128)(2,1)S(1)}, u32[]{:S(2)}, u32[]{:S(2)}) async-start(bf16[32,2,3072]{2,1,0:T(2,128)(2,1)} %reshape.35), calls=%async_computation | async-start | bytes 786432 | tf_op jit(solution)/shard_map/all_to_all | solution.py:54
  88.5 0.1 copy.17
  88.6 26.9 %all_gather.19 = bf16[128,1536]{0,1:T(8,128)(2,1)S(1)} all-gather(bf16[128,48]{0,1:T(8,128)(2,1)S(1)} %copy.17), channel_id=1, replica_groups=mesh['res'=32,'col'=4] {'res'}, dimensions={1}, use_global_device_ids=true | all-gather | bytes 405504 | tf_op jit(solution)/shard_map/all_gather | solution.py:60
  115.5 0.1 copy.18
  115.6 0.7 reshape.36
  116.4 0.3 copy.13
  116.7 87.4 %all-gather.2.cloned.1.call-done = bf16[128,1536,32]{2,1,0:T(8,128)(2,1)} async-done(((bf16[128,48,32]{2,1,0:T(8,128)(2,1)}), bf16[128,1536,32]{2,1,0:T(8,128)(2,1)}) %all-gather.2.cloned.1.call-update) | async-done | bytes 12582928 | tf_op jit(solution)/shard_map/all_gather | solution.py:59
  204.1 12.0 %constant_dynamic-slice_fusion.1 = bf16[128,384,32]{2,1,0:T(8,128)(2,1)} fusion(bf16[128,1536,32]{2,1,0:T(8,128)(2,1)} %all-gather.2.cloned.1.call-done, s32[]{:T(128)S(6)} %select_n.8), kind=kLoop, calls=%fused_computation.34 | loop fusion | bytes 6291460 | tf_op jit(solution)/shard_map/dynamic_slice | solution.py:63
  216.1 116.4 %while.10 = (s32[]{:T(128)}, bf16[6,8,384,128]{3,2,1,0:T(8,128)(2,1)}, s32[6]{0:T(128)S(1)}, bf16[128,48,32]{2,1,0:T(8,128)(2,1)S(1)}, bf16[128,384,32]{2,1,0:T(...) while((s32[]{:T(128)}, ...), condition=%wide.region_3.4_spmd, body=%wide.region_2.3_spmd.sunk | while | flops 1612188672 | bytes 27595512 | solution.py:83
  216.1 0.7 dynamic_slice.28
  218.5 0.1 dynamic-slice_bitcast_fusion.2
  218.6 11.4 %copy.38 = bf16[128,384,32,1]{1,0,2,3:T(8,128)(2,1)S(1)} copy(bf16[128,384,32,1]{2,1,0,3:T(8,128)(2,1)} %bitcast.64) | data formatting | bytes 6291456 | tf_op jit(solution)/shard_map
  230.0 2.0 fusion.38
  232.1 0.2 convolution_add_fusion.2
  232.3 3.2 fusion.39
  235.5 0.7 dynamic_slice.28
  237.9 0.1 dynamic-slice_bitcast_fusion.2
  238.0 11.4 %copy.38 = bf16[128,384,32,1]{1,0,2,3:T(8,128)(2,1)S(1)} copy(bf16[128,384,32,1]{2,1,0,3:T(8,128)(2,1)} %bitcast.64) | data formatting | bytes 6291456 | tf_op jit(solution)/shard_map
  249.4 2.0 fusion.38
  251.5 0.2 convolution_add_fusion.2
  251.7 3.2 fusion.39
  254.9 0.7 dynamic_slice.28
  257.3 0.1 dynamic-slice_bitcast_fusion.2
  257.4 11.4 %copy.38 = bf16[128,384,32,1]{1,0,2,3:T(8,128)(2,1)S(1)} copy(bf16[128,384,32,1]{2,1,0,3:T(8,128)(2,1)} %bitcast.64) | data formatting | bytes 6291456 | tf_op jit(solution)/shard_map
  268.8 2.0 fusion.38
  270.9 0.2 convolution_add_fusion.2
  271.1 3.2 fusion.39
  274.3 0.7 dynamic_slice.28
  276.7 0.1 dynamic-slice_bitcast_fusion.2
  276.8 11.4 %copy.38 = bf16[128,384,32,1]{1,0,2,3:T(8,128)(2,1)S(1)} copy(bf16[128,384,32,1]{2,1,0,3:T(8,128)(2,1)} %bitcast.64) | data formatting | bytes 6291456 | tf_op jit(solution)/shard_map
  288.2 2.0 fusion.38
  290.2 0.2 convolution_add_fusion.2
  290.5 3.2 fusion.39
  293.7 0.7 dynamic_slice.28
  296.1 0.1 dynamic-slice_bitcast_fusion.2
  296.2 11.4 %copy.38 = bf16[128,384,32,1]{1,0,2,3:T(8,128)(2,1)S(1)} copy(bf16[128,384,32,1]{2,1,0,3:T(8,128)(2,1)} %bitcast.64) | data formatting | bytes 6291456 | tf_op jit(solution)/shard_map
  307.6 2.0 fusion.38
  309.6 0.2 convolution_add_fusion.2
  309.9 3.2 fusion.39
  313.1 0.7 dynamic_slice.28
  315.5 0.1 dynamic-slice_bitcast_fusion.2
  315.6 11.4 %copy.38 = bf16[128,384,32,1]{1,0,2,3:T(8,128)(2,1)S(1)} copy(bf16[128,384,32,1]{2,1,0,3:T(8,128)(2,1)} %bitcast.64) | data formatting | bytes 6291456 | tf_op jit(solution)/shard_map
  327.0 2.0 fusion.38
  329.0 0.2 convolution_add_fusion.2
  329.3 3.2 fusion.39
  332.5 0.7 copy-done.1
  (60 shorter events, 0.2 us)
Async XLA Ops:
  6.5 3.4 copy-start
  6.5 3.4 copy-start.4
  6.5 3.2 copy-start.6
  6.5 3.2 copy-start.5
  6.5 3.4 copy-start.10
  6.5 3.4 copy-start.9
  6.6 197.5 %all-gather.2.cloned.1.call-start = ((), (), s32[]{:S(2)}) async-start(), calls=%async_computation.3 | async-start | bytes 51904512 | tf_op jit(solution)/shard_map/all_gather | solution.py:59
  47.9 16.5 %copy-start.8 = (bf16[256,32]{0,1:T(8,128)(2,1)S(1)}, bf16[256,32]{0,1:T(8,128)(2,1)}, u32[]{:S(2)}) copy-start(bf16[256,32]{0,1:T(8,128)(2,1)} %param.15) | copy-start | bytes 49156
  57.6 21.8 %all-to-all-start.2 = ((bf16[4,32,48]{2,0,1:T(4,128)(2,1)}), bf16[4,32,48]{2,0,1:T(4,128)(2,1)S(1)}, u32[]{:S(2)}, u32[]{:S(2)}) async-start(bf16[4,32,48]{2,0,1:T(4,128)(2,1)} %copy.16), calls=%async_computation.2 | async-start | bytes 65536 | tf_op jit(solution)/shard_map/all_to_all | solution.py:56
  79.4 36.2 %all-to-all-start = ((bf16[32,2,3072]{2,1,0:T(2,128)(2,1)}), bf16[32,2,3072]{2,1,0:T(2,128)(2,1)S(1)}, u32[]{:S(2)}, u32[]{:S(2)}) async-start(bf16[32,2,3072]{2,1,0:T(2,128)(2,1)} %reshape.35), calls=%async_computation | async-start | bytes 786432 | tf_op jit(solution)/shard_map/all_to_all | solution.py:54
  216.1 2.5 copy-start.2
  230.0 2.3 copy-start.7
  232.3 3.2 copy-start.3
  235.5 2.5 copy-start.2
  249.4 2.3 copy-start.7
  251.7 3.2 copy-start.3
  254.9 2.5 copy-start.2
  268.8 2.3 copy-start.7
  271.1 3.2 copy-start.3
  274.3 2.5 copy-start.2
  288.2 2.3 copy-start.7
  290.5 3.2 copy-start.3
  293.7 2.5 copy-start.2
  307.6 2.3 copy-start.7
  309.9 3.2 copy-start.3
  313.1 2.5 copy-start.2
  327.0 2.3 copy-start.7
  329.3 3.2 copy-start.3
  332.5 0.7 copy-start.1
Sparse Core Ops, SparseCore 0:
  48.0 156.0 all-gather.1
where the time goes:
time: 342 us; the launch traced here: 340 us
  local copies, waits for them, and re-layouts  95.7 us (28%)
  waiting for transfers between devices  87.4 us (26%)
  blocking collectives  79.6 us (23%)
  matrix products  34.2 us (10%)
  starting transfers between devices  15.9 us (5%)
  between operations  13.6 us (4%)
  loops' own time  10.5 us (3%)
    all_gather x1, waiting for transfers between devices, local(): lax.all_gather(right_rows, 'res', axis=1, tiled=True)  87.4 us
    another operation x6, local copies, waits for them, and re-layouts  68.4 us
    all_gather x1, blocking collectives, local(): lax.all_gather(mask_rows, 'res', axis=1, tiled=True)  26.9 us
    all_to_all x1, blocking collectives, local(): lax.all_to_all(right_every, 'res', split_axis=1, concat_axis=0, tiled=True)  20.9 us
    dot_general x6, matrix products, one_block(): jnp.einsum('ipjq,pqz->ijz', outer_prod, w_cube, preferred_element_type=jn...  19.2 us
    dot_general x6, matrix products, one_block(): jnp.einsum('sip,sjq->ipjq', left_part, right_cols, preferred_element_type...  12.2 us
    dynamic_slice x1, local copies, waits for them, and re-layouts, local(): right_cols = lax.dynamic_slice_in_dim(right_all, offset, column_width, 1)  12 us
    all_gather x1, blocking collectives, local(): lax.all_gather(right_local, 'col', axis=1, tiled=True)  11.7 us
  transfers between devices with their start and end apart: 3, of which 1 were waited for; matrix products, arithmetic and copies ran while one was open for 2% of the time, Pallas kernels for 0%

commit v1 on v0

v1 whole, which is shorter than its diff:
```python
import functools

import jax
import jax.numpy as jnp
from jax import lax
from jax.experimental import pallas as pl
from jax.experimental.pallas import tpu as pltpu
from jax.sharding import PartitionSpec as P

RING = 4
CORES = 2
SEQS = 4
EMBED = 256
SIDE = 32
PAIR = 128
COLS = 384
ROWS = 48
PLANE = ROWS * CORES
GROUP = SEQS * RING
TOTAL = GROUP * RING * CORES
LANES = 128
RIGHT = (SIDE + 1) * COLS
LEFT = (SIDE + 1) * LANES
MEGA = 2**20
F32 = jnp.float32
BF16 = jnp.bfloat16


def position():
    res = lax.axis_index("res")
    return res // (RING * CORES), (res // CORES) % RING, res % CORES, lax.axis_index("col")


def res_shift(value, dz, dy, dc):
    pairs = []
    for r in range(RING * RING * CORES):
        z, y, c = r // (RING * CORES), (r // CORES) % RING, r % CORES
        to = (((z + dz) % RING) * RING + (y + dy) % RING) * CORES + (c + dc) % CORES
        pairs.append((r, to))
    return lax.ppermute(value, "res", pairs)


def row_owner_shift(value, k):
    pairs = []
    for z in range(RING):
        for y in range(RING):
            for c in range(CORES):
                for x in range(RING):
                    source = ((z * RING + y) * CORES + c) * RING + x
                    target = ((x * RING + y) * CORES + c) * RING + (z + k) % RING
                    pairs.append((source, target))
    return lax.ppermute(value, ("res", "col"), pairs)


def contract_last(a, b):
    return lax.dot_general(a, b, (((1,), (1,)), ((), ())), preferred_element_type=F32)


def project_kernel(emb, weights, chain, chain_parts, gain, shift, first, second, *rest):
    outs, (normed, right, left) = rest[:RING], rest[RING:]
    _, y, _, _ = position()
    first_t = first[...].astype(F32).T.astype(BF16)
    second_t = second[...].astype(F32).T.astype(BF16)
    chains = weights.shape[1]

    def mask_of(row):
        width = row.shape[1]
        ids = lax.broadcasted_iota(jnp.int32, (chains, width), 0)
        onehot = (jnp.broadcast_to(row, (chains, width)) == ids).astype(F32).astype(BF16)
        return jnp.dot(weights[...], onehot, preferred_element_type=F32)

    mask = mask_of(chain[...])
    for s in range(SEQS):
        wide = emb[s].astype(F32)
        shifted = wide - jnp.mean(wide, axis=-1, keepdims=True)
        variance = jnp.mean(shifted * shifted, axis=-1, keepdims=True)
        value = shifted * lax.rsqrt(variance + 1e-05) * gain[...] + shift[...]
        normed[s] = value.astype(BF16)
        right[s] = contract_last(second_t, normed[s]) * mask[s : s + 1]
    for q in range(SIDE):
        part = right[:, q, :].astype(BF16)
        for out in outs:
            out[:, q * COLS : (q + 1) * COLS] = part
    for out in outs:
        out[:, SIDE * COLS : RIGHT] = mask.astype(BF16)
    left[...] = jnp.zeros_like(left)
    for d, out in enumerate(outs):
        to = lax.rem(y + d, RING)
        row_mask = mask_of(chain_parts[pl.ds(to, 1), :])
        start = pl.multiple_of(to * PLANE, 16)
        for s in range(SEQS):
            part = contract_last(first_t, normed[s, pl.ds(start, PLANE), :])
            left[s, 0:SIDE, 0:PLANE] = part * row_mask[s : s + 1]
            left[s, SIDE : SIDE + 1, 0:PLANE] = row_mask[s : s + 1]
        for p in range(SIDE + 1):
            out[:, RIGHT + p * LANES : RIGHT + (p + 1) * LANES] = left[:, p, :].astype(BF16)


def project(emb, weights, chain, gain, shift, first, second):
    return pl.pallas_call(
        project_kernel,
        out_shape=[jax.ShapeDtypeStruct((SEQS, RIGHT + LEFT), BF16)] * RING,
        scratch_shapes=[
            pltpu.VMEM((SEQS, COLS, EMBED), BF16),
            pltpu.VMEM((SEQS, SIDE, COLS), F32),
            pltpu.VMEM((SEQS, SIDE + 8, LANES), F32),
        ],
        compiler_params=pltpu.CompilerParams(vmem_limit_bytes=32 * MEGA),
    )(
        emb,
        weights,
        chain.reshape(1, COLS),
        chain.reshape(RING, PLANE),
        gain.reshape(1, EMBED),
        shift.reshape(1, EMBED),
        first,
        second,
    )


def stack_kernel(*refs):
    parts, (right, left, wide) = refs[:RING], refs[RING:]
    step = 1408
    for at in range(0, RIGHT + LEFT, step):
        for d, part in enumerate(parts):
            wide[d * SEQS : (d + 1) * SEQS, :] = part[:, at : at + step].astype(F32)
        value = wide[...].astype(BF16)
        if at < RIGHT:
            right[:, at : at + step] = value
        else:
            left[:, at - RIGHT : at - RIGHT + step] = value


def stack(parts):
    return pl.pallas_call(
        stack_kernel,
        out_shape=[
            jax.ShapeDtypeStruct((GROUP, RIGHT), BF16),
            jax.ShapeDtypeStruct((GROUP, LEFT), BF16),
        ],
        scratch_shapes=[pltpu.VMEM((GROUP, 1408), F32)],
        compiler_params=pltpu.CompilerParams(vmem_limit_bytes=32 * MEGA),
    )(*parts)


def left_kernel(*refs):
    parts, (out, out_mask, wide, turned) = refs[: RING * CORES], refs[RING * CORES :]
    z, _, core, x = position()
    for c in range(CORES):
        for k in range(RING):
            group = lax.rem(z - x + k + RING, RING)
            start = pl.multiple_of((c * RING + group) * GROUP, GROUP)
            wide[pl.ds(start, GROUP), :] = parts[c * RING + k][...].astype(F32)
    for p in range(SIDE + 1):
        block = wide[:, p * LANES : (p + 1) * LANES].T
        turned[p * PLANE : (p + 1) * PLANE, :] = block[:PLANE]
    base = core * ROWS
    for i in range(ROWS):
        rows = turned[pl.ds(base + i, SIDE, stride=PLANE), :]
        out[i * SIDE : (i + 1) * SIDE, :] = rows.astype(BF16)
    start = pl.multiple_of(SIDE * PLANE + base, 8)
    out_mask[...] = turned[pl.ds(start, ROWS), :].astype(BF16)


def arrange_left(parts):
    return pl.pallas_call(
        left_kernel,
        out_shape=[
            jax.ShapeDtypeStruct((ROWS * SIDE, TOTAL), BF16),
            jax.ShapeDtypeStruct((ROWS, TOTAL), BF16),
        ],
        scratch_shapes=[
            pltpu.VMEM((TOTAL, LEFT), F32),
            pltpu.VMEM(((SIDE + 1) * PLANE, TOTAL), F32),
        ],
        compiler_params=pltpu.CompilerParams(vmem_limit_bytes=32 * MEGA),
    )(*parts)


def pair_kernel(block, left, left_mask, weight, *refs):
    parts, (out, right, outer, scale, sem) = refs[: RING * CORES], refs[RING * CORES :]

    @pl.when(pl.program_id(0) == 0)
    def _():
        copies = [
            pltpu.make_async_copy(part, right.at[pl.ds(k * GROUP, GROUP), :], sem.at[k])
            for k, part in enumerate(parts)
        ]
        for copy in copies:
            copy.start()
        for copy in copies:
            copy.wait()
        counts = jnp.dot(
            left_mask[...], right[:, SIDE * COLS : RIGHT], preferred_element_type=F32
        )
        scale[...] = 1.0 / (counts + 0.001)

    value = left[...]
    for q in range(SIDE):
        part = jnp.dot(
            value, right[:, q * COLS : (q + 1) * COLS], preferred_element_type=F32
        ).astype(BF16)
        for i in range(block):
            outer[i, q * SIDE : (q + 1) * SIDE, :] = part[i * SIDE : (i + 1) * SIDE]
    first = pl.multiple_of(pl.program_id(0) * block, block)
    scales = scale[pl.ds(first, block), :]
    for i in range(block):
        projected = jnp.dot(weight[...], outer[i], preferred_element_type=F32)
        out[i] = (projected * scales[i : i + 1]).T.astype(BF16)


def pair(left, left_mask, weight, parts):
    block = 8
    whole = lambda a: pl.BlockSpec(a.shape, lambda i: (0,) * a.ndim)
    return pl.pallas_call(
        functools.partial(pair_kernel, block),
        grid=(ROWS // block,),
        in_specs=[
            pl.BlockSpec((block * SIDE, TOTAL), lambda i: (i, 0)),
            whole(left_mask),
            whole(weight),
        ]
        + [pl.BlockSpec(memory_space=pl.ANY)] * len(parts),
        out_specs=pl.BlockSpec((block, COLS, PAIR), lambda i: (i, 0, 0)),
        out_shape=jax.ShapeDtypeStruct((ROWS, COLS, PAIR), BF16),
        scratch_shapes=[
            pltpu.VMEM((TOTAL, RIGHT), BF16),
            pltpu.VMEM((block, SIDE * SIDE, COLS), BF16),
            pltpu.VMEM((ROWS, COLS), F32),
            pltpu.SemaphoreType.DMA((RING * CORES,)),
        ],
        compiler_params=pltpu.CompilerParams(vmem_limit_bytes=48 * MEGA),
    )(left, left_mask, weight, *parts)


def local(
    homolog_embedding,
    sequence_row_mask,
    residue_chain_index,
    standardize_factor,
    standardize_shift,
    first_projector_matrix,
    second_projector_matrix,
    output_weight,
):
    weight = output_weight.reshape(SIDE, SIDE, PAIR).transpose(2, 1, 0).reshape(PAIR, SIDE * SIDE)
    own = project(
        homolog_embedding,
        sequence_row_mask,
        residue_chain_index,
        standardize_factor,
        standardize_shift,
        first_projector_matrix,
        second_projector_matrix,
    )
    along_y = [own[0]] + [res_shift(own[d], 0, d, 0) for d in range(1, RING)]
    right, left = stack(along_y)
    right_parts = [right] + [res_shift(right, d, 0, 0) for d in range(1, RING)]
    left_parts = [row_owner_shift(left, k) for k in range(RING)]
    left_parts = left_parts + [res_shift(part, 0, 0, 1) for part in left_parts]
    right_parts = right_parts + [res_shift(part, 0, 0, 1) for part in right_parts]
    left_all, left_mask = arrange_left(left_parts)
    return pair(left_all, left_mask, weight, right_parts)


def solution(mesh):
    in_specs = (P("res", "col", None), P("res", None), P("col"), P(), P(), P(), P(), P())
    out_specs = P("res", "col", None)
    return jax.shard_map(local, mesh=mesh, in_specs=in_specs, out_specs=out_specs, check_vma=False)
```

time: 342 us -> 95.4 us (0.28)
  the two profiles are of different devices: /device:TPU:1 before, /device:TPU:5 now
where the time goes in v1:
time: 95.4 us; the launch traced here: 94.9 us
  starting transfers between devices  28.2 us (30%)
  Pallas kernels  24.4 us (26%)
  waiting for transfers between devices  23.6 us (25%)
  local copies, waits for them, and re-layouts  18.5 us (19%)
    pallas_call x1, Pallas kernels, pair(): pl.pallas_call(functools.partial(pair_kernel, block), grid=(ROWS // block...  20.6 us
    ppermute x4, waiting for transfers between devices, row_owner_shift(): return lax.ppermute(value, ('res', 'col'), pairs)  17.6 us
    ppermute x14, starting transfers between devices, res_shift(): return lax.ppermute(value, 'res', pairs)  15.3 us
    unnamed x34, local copies, waits for them, and re-layouts  14.2 us
    ppermute x4, starting transfers between devices, row_owner_shift(): return lax.ppermute(value, ('res', 'col'), pairs)  13 us
    ppermute x14, waiting for transfers between devices, res_shift(): return lax.ppermute(value, 'res', pairs)  6.07 us
    pallas_call x1, Pallas kernels, arrange_left(): pl.pallas_call(left_kernel, out_shape=[jax.ShapeDtypeStruct((ROWS * SIDE,...  2.16 us
  transfers between devices with their start and end apart: 18, of which 5 were waited for; matrix products, arithmetic and copies ran while one was open for 3% of the time, Pallas kernels for 2%

profile of v1, /device:TPU:5, one launch (start us, length us, event | category | flops | bytes accessed | tf_op | source)
XLA Modules:
  0.0 94.9 jit_solution(16160718261849131715)
XLA Ops:
  0.0 0.7 reshape.18.chain
  0.7 0.8 reshape.19.chain_parts
  1.4 0.8 copy.15.first
  2.3 0.8 copy.16.second
  3.1 0.0 copy-start
  3.1 1.1 %copy-done = bf16[4,384,256]{2,1,0:T(8,128)(2,1)S(1)} copy-done((bf16[4,384,256]{2,1,0:T(8,128)(2,1)S(1)}, bf16[4,384,256]{2,1,0:T(8,128)(2,1)}, u32[]{:S(2)}) %copy-start) | copy-done | bytes 786456
  4.3 0.7 copy-done.13
  4.9 0.7 copy-done.14
  5.6 0.7 copy-done.15
  6.3 1.3 %shard_map.82 = (bf16[4,16896]{1,0:T(4,128)(2,1)S(1)}, bf16[4,16896]{1,0:T(4,128)(2,1)S(1)}, bf16[4,16896]{1,0:T(4,128)(2,1)S(1)}, bf16[4,16896]{1,0:T(4,128)(2,1)S(1)}) custom-call(bf16[4,384,256]{2,1,0:T(8,128)(2,1)S(1)} %copy-done, bf16[4,8]{1,0:T(4,128)(2,1)S(1)} %copy-done.13, s32[1,384]{1,0:T(1,128)S(1)} %reshape.18.chain, ...), custom_call_target="tpu_custom_call" | custom-call | tf_op jit(solution)/shard_map/pallas_call | solution.py:100
  7.6 1.4 %collective-permute-start = (bf16[4,16896]{1,0:T(4,128)(2,1)S(1)}, bf16[4,16896]{1,0:T(4,128)(2,1)S(1)}, u32[]{:S(2)}, u32[]{:S(2)}) collective-permute-start(bf16[4,16896]{1,0:T(4,128)(2,1)S(1)} %get-tuple-element.14), channel_id=1, source_target_pairs={{0,8},{4,12},{8,16},{12,20},{16,24},{20,28},{24,0},{28,4},{32,40},... | collective-permute-start | bytes 405512 | tf_op jit(solution)/shard_map/ppermute | solution.py:40
  9.0 2.6 %collective-permute-start.1 = (bf16[4,16896]{1,0:T(4,128)(2,1)S(1)}, bf16[4,16896]{1,0:T(4,128)(2,1)S(1)}, u32[]{:S(2)}, u32[]{:S(2)}) collective-permute-start(bf16[4,16896]{1,0:T(4,128)(2,1)S(1)} %get-tuple-element.15), channel_id=1, source_target_pairs={{0,16},{4,20},{8,24},{12,28},{16,0},{20,4},{24,8},{28,12},{32,48},... | collective-permute-start | bytes 405512 | tf_op jit(solution)/shard_map/ppermute | solution.py:40
  11.6 1.1 %collective-permute-start.2 = (bf16[4,16896]{1,0:T(4,128)(2,1)S(1)}, bf16[4,16896]{1,0:T(4,128)(2,1)S(1)}, u32[]{:S(2)}, u32[]{:S(2)}) collective-permute-start(bf16[4,16896]{1,0:T(4,128)(2,1)S(1)} %get-tuple-element.16), channel_id=1, source_target_pairs={{0,24},{4,28},{8,0},{12,4},{16,8},{20,12},{24,16},{28,20},{32,56},... | collective-permute-start | bytes 405512 | tf_op jit(solution)/shard_map/ppermute | solution.py:40
  12.7 0.8 collective-permute-done.refs_1_
  13.5 4.0 %collective-permute-done.1.refs_2_ = bf16[4,16896]{1,0:T(4,128)(2,1)S(1)} collective-permute-done((bf16[4,16896]{1,0:T(4,128)(2,1)S(1)}, bf16[4,16896]{1,0:T(4,128)(2,1)S(1)}, u32[]{:S(2)}, u32[]{:S(2)}) %collective-permute-start.1) | collective-permute-done | bytes 135200 | tf_op jit(solution)/shard_map/ppermute | solution.py:40
  17.5 0.0 collective-permute-done.2.refs_3_
  17.5 0.2 shard_map.83
  17.8 4.3 %collective-permute-start.6 = (bf16[16,4224]{1,0:T(8,128)(2,1)S(1)}, bf16[16,4224]{1,0:T(8,128)(2,1)S(1)}, u32[]{:S(2)}, u32[]{:S(2)}) collective-permute-start(bf16[16,4224]{1,0:T(8,128)(2,1)S(1)} %get-tuple-element.17), channel_id=1, source_target_pairs={{0,3},{1,35},{2,67},{3,99},{4,7},{5,39},{6,71},{7,103},{8,11},{9,4... | collective-permute-start | bytes 405512 | tf_op jit(solution)/shard_map/ppermute | solution.py:52
  22.0 0.0 collective-permute-start.13
  22.0 0.8 collective-permute-start.12
  22.8 0.7 collective-permute-start.11
  23.5 3.6 %collective-permute-start.5 = (bf16[16,4224]{1,0:T(8,128)(2,1)S(1)}, bf16[16,4224]{1,0:T(8,128)(2,1)S(1)}, u32[]{:S(2)}, u32[]{:S(2)}) collective-permute-start(bf16[16,4224]{1,0:T(8,128)(2,1)S(1)} %get-tuple-element.17), channel_id=1, source_target_pairs={{0,2},{1,34},{2,66},{3,98},{4,6},{5,38},{6,70},{7,102},{8,10},{9,4... | collective-permute-start | bytes 405512 | tf_op jit(solution)/shard_map/ppermute | solution.py:52
  27.1 0.0 collective-permute-done.6.refs_3_
  27.1 0.3 collective-permute-start.4
  27.3 16.7 %collective-permute-done.5.refs_2_ = bf16[16,4224]{1,0:T(8,128)(2,1)S(1)} collective-permute-done((bf16[16,4224]{1,0:T(8,128)(2,1)S(1)}, bf16[16,4224]{1,0:T(8,128)(2,1)S(1)}, u32[]{:S(2)}, u32[]{:S(2)}) %collective-permute-start.5) | collective-permute-done | bytes 135200 | tf_op jit(solution)/shard_map/ppermute | solution.py:52
  44.0 4.9 %collective-permute-start.3 = (bf16[16,4224]{1,0:T(8,128)(2,1)S(1)}, bf16[16,4224]{1,0:T(8,128)(2,1)}, u32[]{:S(2)}, u32[]{:S(2)}) collective-permute-start(bf16[16,4224]{1,0:T(8,128)(2,1)S(1)} %get-tuple-element.17), channel_id=1, source_target_pairs={{0,0},{1,32},{2,64},{3,96},{4,4},{5,36},{6,68},{7,100},{8,8},{9,40... | collective-permute-start | bytes 405512 | tf_op jit(solution)/shard_map/ppermute | solution.py:52
  48.9 0.0 collective-permute-done.4.refs_1_
  48.9 3.3 %collective-permute-start.10 = (bf16[16,4224]{1,0:T(8,128)(2,1)S(1)}, bf16[16,4224]{1,0:T(8,128)(2,1)S(1)}, u32[]{:S(2)}, u32[]{:S(2)}) collective-permute-start(bf16[16,4224]{1,0:T(8,128)(2,1)S(1)} %collective-permute-done.6.refs_3_), channel_id=1, source_target_pairs={{0,4},{4,0},{8,12},{12,8},{16,20},{20,16},{24,28},{28,24},{32,36},... | collective-permute-start | bytes 405512 | tf_op jit(solution)/shard_map/ppermute | solution.py:40
  52.3 0.7 copy-done.1
  52.9 0.9 collective-permute-done.3.refs_0_
  53.8 4.1 %collective-permute-start.9 = (bf16[16,4224]{1,0:T(8,128)(2,1)S(1)}, bf16[16,4224]{1,0:T(8,128)(2,1)S(1)}, u32[]{:S(2)}, u32[]{:S(2)}) collective-permute-start(bf16[16,4224]{1,0:T(8,128)(2,1)S(1)} %collective-permute-done.5.refs_2_), channel_id=1, source_target_pairs={{0,4},{4,0},{8,12},{12,8},{16,20},{20,16},{24,28},{28,24},{32,36},... | collective-permute-start | bytes 405512 | tf_op jit(solution)/shard_map/ppermute | solution.py:40
  57.9 0.7 copy-done.3
  58.6 0.0 collective-permute-done.10.refs_7_
  58.6 0.7 copy-done.7
  59.3 0.0 collective-permute-start.14
  59.3 0.0 collective-permute-done.13.refs_3_
  59.3 0.5 collective-permute-start.17
  59.8 0.0 collective-permute-done.12.refs_2_
  59.8 0.1 collective-permute-start.16
  59.9 0.0 collective-permute-done.11.refs_1_
  59.9 0.4 collective-permute-start.15
  60.3 0.0 collective-permute-done.9.refs_6_
  60.3 0.7 copy-done.9
  61.0 0.1 collective-permute-start.8
  61.0 0.7 copy-done.5
  61.7 1.2 %collective-permute-done.8.refs_5_ = bf16[16,4224]{1,0:T(8,128)(2,1)S(1)} collective-permute-done((bf16[16,4224]{1,0:T(8,128)(2,1)S(1)}, bf16[16,4224]{1,0:T(8,128)(2,1)S(1)}, u32[]{:S(2)}, u32[]{:S(2)}) %collective-permute-start.8) | collective-permute-done | bytes 135200 | tf_op jit(solution)/shard_map/ppermute | solution.py:40
  62.9 0.6 copy-done.11
  63.6 0.1 collective-permute-start.7
  63.7 1.8 %copy.17 = bf16[128,32,32]{0,2,1:T(8,128)(2,1)} copy(bf16[128,32,32]{0,1,2:T(8,128)(2,1)} %bitcast.9) | data formatting | bytes 524288 | tf_op jit(solution)/shard_map/transpose | solution.py:246
  65.5 1.1 %copy.18.weight = bf16[128,1024]{1,0:T(8,128)(2,1)S(1)} copy(bf16[128,1024]{0,1:T(8,128)(2,1)} %bitcast.8) | data formatting | bytes 524288 | tf_op jit(solution)/shard_map/reshape | solution.py:246
  66.6 0.0 collective-permute-done.7.refs_4_
  66.6 0.0 copy-start.2
  66.6 0.9 copy-done.2
  67.5 0.9 copy-done.4
  68.4 0.9 copy-done.6
  69.3 0.9 copy-done.8
  70.2 0.9 copy-done.10
  71.1 0.9 copy-done.12
  72.0 2.2 %shard_map.84 = (bf16[1536,128]{1,0:T(8,128)(2,1)S(1)}, bf16[48,128]{1,0:T(8,128)(2,1)S(1)}) custom-call(bf16[16,4224]{1,0:T(8,128)(2,1)} %collective-permute-done.3.refs_0_, bf16[16,4224]{1,0:T(8,128)(2,1)S(1)} %copy-done.6, bf16[16,4224]{1,0:T(8,128)(2,1)S(1)} %copy-done.4, bf16[16,4224]{1,0:T(8,128)(2,1)S(1)} %copy-done.2, ...), custom_call_target="tpu_custom_call" | custom-call | tf_op jit(solution)/shard_map/pallas_call | solution.py:166
  74.2 0.0 collective-permute-done.14.refs_4_
  74.2 0.0 collective-permute-done.17.refs_7_
  74.2 0.0 collective-permute-done.16.refs_6_
  74.2 0.0 collective-permute-done.15.refs_5_
  74.2 20.6 %shard_map.85 = bf16[48,384,128]{2,1,0:T(8,128)(2,1)} custom-call(bf16[1536,128]{1,0:T(8,128)(2,1)S(1)} %get-tuple-element.18.left, bf16[48,128]{1,0:T(8,128)(2,1)S(1)} %get-tuple-element.19.left_mask, bf16[128,1024]{1,0:T(8,128)(2,1)S(1)} %copy.18.weight, bf16[16,12672]{1,0:T(8,128)(2,1)S(1)} %get-tuple-element.20.refs_0_, ...), custom_call_target="tpu_custom_call" | custom-call | tf_op jit(solution)/shard_map/pallas_call | solution.py:215
  (14 shorter events, 0.0 us)
Async XLA Ops:
  3.1 1.1 %copy-start = (bf16[4,384,256]{2,1,0:T(8,128)(2,1)S(1)}, bf16[4,384,256]{2,1,0:T(8,128)(2,1)}, u32[]{:S(2)}) copy-start(bf16[4,384,256]{2,1,0:T(8,128)(2,1)} %emb.1) | copy-start | bytes 2359300
  4.3 0.7 copy-start.13
  4.9 0.7 copy-start.14
  5.6 0.7 copy-start.15
  7.6 5.9 %collective-permute-start = (bf16[4,16896]{1,0:T(4,128)(2,1)S(1)}, bf16[4,16896]{1,0:T(4,128)(2,1)S(1)}, u32[]{:S(2)}, u32[]{:S(2)}) collective-permute-start(bf16[4,16896]{1,0:T(4,128)(2,1)S(1)} %get-tuple-element.14), channel_id=1, source_target_pairs={{0,8},{4,12},{8,16},{12,20},{16,24},{20,28},{24,0},{28,4},{32,40},... | collective-permute-start | bytes 405512 | tf_op jit(solution)/shard_map/ppermute | solution.py:40
  9.0 8.5 %collective-permute-start.1 = (bf16[4,16896]{1,0:T(4,128)(2,1)S(1)}, bf16[4,16896]{1,0:T(4,128)(2,1)S(1)}, u32[]{:S(2)}, u32[]{:S(2)}) collective-permute-start(bf16[4,16896]{1,0:T(4,128)(2,1)S(1)} %get-tuple-element.15), channel_id=1, source_target_pairs={{0,16},{4,20},{8,24},{12,28},{16,0},{20,4},{24,8},{28,12},{32,48},... | collective-permute-start | bytes 405512 | tf_op jit(solution)/shard_map/ppermute | solution.py:40
  11.6 5.9 %collective-permute-start.2 = (bf16[4,16896]{1,0:T(4,128)(2,1)S(1)}, bf16[4,16896]{1,0:T(4,128)(2,1)S(1)}, u32[]{:S(2)}, u32[]{:S(2)}) collective-permute-start(bf16[4,16896]{1,0:T(4,128)(2,1)S(1)} %get-tuple-element.16), channel_id=1, source_target_pairs={{0,24},{4,28},{8,0},{12,4},{16,8},{20,12},{24,16},{28,20},{32,56},... | collective-permute-start | bytes 405512 | tf_op jit(solution)/shard_map/ppermute | solution.py:40
  17.8 9.3 %collective-permute-start.6 = (bf16[16,4224]{1,0:T(8,128)(2,1)S(1)}, bf16[16,4224]{1,0:T(8,128)(2,1)S(1)}, u32[]{:S(2)}, u32[]{:S(2)}) collective-permute-start(bf16[16,4224]{1,0:T(8,128)(2,1)S(1)} %get-tuple-element.17), channel_id=1, source_target_pairs={{0,3},{1,35},{2,67},{3,99},{4,7},{5,39},{6,71},{7,103},{8,11},{9,4... | collective-permute-start | bytes 405512 | tf_op jit(solution)/shard_map/ppermute | solution.py:52
  22.0 37.2 %collective-permute-start.13 = (bf16[16,12672]{1,0:T(8,128)(2,1)S(1)}, bf16[16,12672]{1,0:T(8,128)(2,1)S(1)}, u32[]{:S(2)}, u32[]{:S(2)}) collective-permute-start(bf16[16,12672]{1,0:T(8,128)(2,1)S(1)} %get-tuple-element.20.refs_0_), channel_id=1, source_target_pairs={{0,96},{4,100},{8,104},{12,108},{16,112},{20,116},{24,120},{28,124... | collective-permute-start | bytes 1216520 | tf_op jit(solution)/shard_map/ppermute | solution.py:40
  22.0 37.7 %collective-permute-start.12 = (bf16[16,12672]{1,0:T(8,128)(2,1)S(1)}, bf16[16,12672]{1,0:T(8,128)(2,1)S(1)}, u32[]{:S(2)}, u32[]{:S(2)}) collective-permute-start(bf16[16,12672]{1,0:T(8,128)(2,1)S(1)} %get-tuple-element.20.refs_0_), channel_id=1, source_target_pairs={{0,64},{4,68},{8,72},{12,76},{16,80},{20,84},{24,88},{28,92},{32,9... | collective-permute-start | bytes 1216520 | tf_op jit(solution)/shard_map/ppermute | solution.py:40
  22.8 37.1 %collective-permute-start.11 = (bf16[16,12672]{1,0:T(8,128)(2,1)S(1)}, bf16[16,12672]{1,0:T(8,128)(2,1)S(1)}, u32[]{:S(2)}, u32[]{:S(2)}) collective-permute-start(bf16[16,12672]{1,0:T(8,128)(2,1)S(1)} %get-tuple-element.20.refs_0_), channel_id=1, source_target_pairs={{0,32},{4,36},{8,40},{12,44},{16,48},{20,52},{24,56},{28,60},{32,6... | collective-permute-start | bytes 1216520 | tf_op jit(solution)/shard_map/ppermute | solution.py:40
  23.5 20.5 %collective-permute-start.5 = (bf16[16,4224]{1,0:T(8,128)(2,1)S(1)}, bf16[16,4224]{1,0:T(8,128)(2,1)S(1)}, u32[]{:S(2)}, u32[]{:S(2)}) collective-permute-start(bf16[16,4224]{1,0:T(8,128)(2,1)S(1)} %get-tuple-element.17), channel_id=1, source_target_pairs={{0,2},{1,34},{2,66},{3,98},{4,6},{5,38},{6,70},{7,102},{8,10},{9,4... | collective-permute-start | bytes 405512 | tf_op jit(solution)/shard_map/ppermute | solution.py:52
  27.1 21.8 %collective-permute-start.4 = (bf16[16,4224]{1,0:T(8,128)(2,1)S(1)}, bf16[16,4224]{1,0:T(8,128)(2,1)S(1)}, u32[]{:S(2)}, u32[]{:S(2)}) collective-permute-start(bf16[16,4224]{1,0:T(8,128)(2,1)S(1)} %get-tuple-element.17), channel_id=1, source_target_pairs={{0,1},{1,33},{2,65},{3,97},{4,5},{5,37},{6,69},{7,101},{8,9},{9,41... | collective-permute-start | bytes 405512 | tf_op jit(solution)/shard_map/ppermute | solution.py:52
  44.0 9.8 %collective-permute-start.3 = (bf16[16,4224]{1,0:T(8,128)(2,1)S(1)}, bf16[16,4224]{1,0:T(8,128)(2,1)}, u32[]{:S(2)}, u32[]{:S(2)}) collective-permute-start(bf16[16,4224]{1,0:T(8,128)(2,1)S(1)} %get-tuple-element.17), channel_id=1, source_target_pairs={{0,0},{1,32},{2,64},{3,96},{4,4},{5,36},{6,68},{7,100},{8,8},{9,40... | collective-permute-start | bytes 405512 | tf_op jit(solution)/shard_map/ppermute | solution.py:52
  48.9 9.7 %collective-permute-start.10 = (bf16[16,4224]{1,0:T(8,128)(2,1)S(1)}, bf16[16,4224]{1,0:T(8,128)(2,1)S(1)}, u32[]{:S(2)}, u32[]{:S(2)}) collective-permute-start(bf16[16,4224]{1,0:T(8,128)(2,1)S(1)} %collective-permute-done.6.refs_3_), channel_id=1, source_target_pairs={{0,4},{4,0},{8,12},{12,8},{16,20},{20,16},{24,28},{28,24},{32,36},... | collective-permute-start | bytes 405512 | tf_op jit(solution)/shard_map/ppermute | solution.py:40
  52.3 0.7 copy-start.1
  53.8 6.5 %collective-permute-start.9 = (bf16[16,4224]{1,0:T(8,128)(2,1)S(1)}, bf16[16,4224]{1,0:T(8,128)(2,1)S(1)}, u32[]{:S(2)}, u32[]{:S(2)}) collective-permute-start(bf16[16,4224]{1,0:T(8,128)(2,1)S(1)} %collective-permute-done.5.refs_2_), channel_id=1, source_target_pairs={{0,4},{4,0},{8,12},{12,8},{16,20},{20,16},{24,28},{28,24},{32,36},... | collective-permute-start | bytes 405512 | tf_op jit(solution)/shard_map/ppermute | solution.py:40
  57.9 0.7 copy-start.3
  58.6 0.7 copy-start.7
  59.3 14.9 %collective-permute-start.14 = (bf16[16,12672]{1,0:T(8,128)(2,1)S(1)}, bf16[16,12672]{1,0:T(8,128)(2,1)S(1)}, u32[]{:S(2)}, u32[]{:S(2)}) collective-permute-start(bf16[16,12672]{1,0:T(8,128)(2,1)S(1)} %get-tuple-element.20.refs_0_), channel_id=1, source_target_pairs={{0,4},{4,0},{8,12},{12,8},{16,20},{20,16},{24,28},{28,24},{32,36},... | collective-permute-start | bytes 1216520 | tf_op jit(solution)/shard_map/ppermute | solution.py:40
  59.3 14.9 %collective-permute-start.17 = (bf16[16,12672]{1,0:T(8,128)(2,1)S(1)}, bf16[16,12672]{1,0:T(8,128)(2,1)S(1)}, u32[]{:S(2)}, u32[]{:S(2)}) collective-permute-start(bf16[16,12672]{1,0:T(8,128)(2,1)S(1)} %collective-permute-done.13.refs_3_), channel_id=1, source_target_pairs={{0,4},{4,0},{8,12},{12,8},{16,20},{20,16},{24,28},{28,24},{32,36},... | collective-permute-start | bytes 1216520 | tf_op jit(solution)/shard_map/ppermute | solution.py:40
  59.8 14.4 %collective-permute-start.16 = (bf16[16,12672]{1,0:T(8,128)(2,1)S(1)}, bf16[16,12672]{1,0:T(8,128)(2,1)S(1)}, u32[]{:S(2)}, u32[]{:S(2)}) collective-permute-start(bf16[16,12672]{1,0:T(8,128)(2,1)S(1)} %collective-permute-done.12.refs_2_), channel_id=1, source_target_pairs={{0,4},{4,0},{8,12},{12,8},{16,20},{20,16},{24,28},{28,24},{32,36},... | collective-permute-start | bytes 1216520 | tf_op jit(solution)/shard_map/ppermute | solution.py:40
  59.9 14.3 %collective-permute-start.15 = (bf16[16,12672]{1,0:T(8,128)(2,1)S(1)}, bf16[16,12672]{1,0:T(8,128)(2,1)S(1)}, u32[]{:S(2)}, u32[]{:S(2)}) collective-permute-start(bf16[16,12672]{1,0:T(8,128)(2,1)S(1)} %collective-permute-done.11.refs_1_), channel_id=1, source_target_pairs={{0,4},{4,0},{8,12},{12,8},{16,20},{20,16},{24,28},{28,24},{32,36},... | collective-permute-start | bytes 1216520 | tf_op jit(solution)/shard_map/ppermute | solution.py:40
  60.3 0.7 copy-start.9
  61.0 2.0 %collective-permute-start.8 = (bf16[16,4224]{1,0:T(8,128)(2,1)S(1)}, bf16[16,4224]{1,0:T(8,128)(2,1)S(1)}, u32[]{:S(2)}, u32[]{:S(2)}) collective-permute-start(bf16[16,4224]{1,0:T(8,128)(2,1)S(1)} %collective-permute-done.4.refs_1_), channel_id=1, source_target_pairs={{0,4},{4,0},{8,12},{12,8},{16,20},{20,16},{24,28},{28,24},{32,36},... | collective-permute-start | bytes 405512 | tf_op jit(solution)/shard_map/ppermute | solution.py:40
  61.0 0.7 copy-start.5
  62.9 0.6 copy-start.11
  63.6 3.0 %collective-permute-start.7 = (bf16[16,4224]{1,0:T(8,128)(2,1)}, bf16[16,4224]{1,0:T(8,128)(2,1)}, u32[]{:S(2)}, u32[]{:S(2)}) collective-permute-start(bf16[16,4224]{1,0:T(8,128)(2,1)} %collective-permute-done.3.refs_0_), channel_id=1, source_target_pairs={{0,4},{4,0},{8,12},{12,8},{16,20},{20,16},{24,28},{28,24},{32,36},... | collective-permute-start | bytes 405512 | tf_op jit(solution)/shard_map/ppermute | solution.py:40
  66.6 0.9 copy-start.2
  67.5 0.9 copy-start.4
  68.4 0.9 copy-start.6
  69.3 0.9 copy-start.8
  70.2 0.9 copy-start.10
  71.1 0.9 copy-start.12

commit v2 on v1

v2 whole, which is shorter than its diff:
```python
import functools

import jax
import jax.numpy as jnp
from jax import lax
from jax.experimental import pallas as pl
from jax.experimental.pallas import tpu as pltpu
from jax.sharding import PartitionSpec as P

RING = 4
CORES = 2
SEQS = 4
EMBED = 256
SIDE = 32
PAIR = 128
COLS = 384
ROWS = 48
PLANE = ROWS * CORES
GROUP = SEQS * RING
CHIP = GROUP * CORES
TOTAL = CHIP * RING
LANES = 128
RIGHT = (SIDE + 1) * COLS
MAJOR, MINOR = 64, 32
LEFT = SIDE * PLANE + LANES
MEGA = 2**20
F32 = jnp.float32
BF16 = jnp.bfloat16


def position():
    res = lax.axis_index("res")
    return res // (RING * CORES), (res // CORES) % RING, res % CORES, lax.axis_index("col")


def res_shift(value, dz, dy, dc):
    pairs = []
    for r in range(RING * RING * CORES):
        z, y, c = r // (RING * CORES), (r // CORES) % RING, r % CORES
        to = (((z + dz) % RING) * RING + (y + dy) % RING) * CORES + (c + dc) % CORES
        pairs.append((r, to))
    return lax.ppermute(value, "res", pairs)


def core_swap(value):
    return res_shift(value, 0, 0, 1)


def both_ways(value):
    pairs = []
    for r in range(RING * RING * CORES):
        z, y, c = r // (RING * CORES), (r // CORES) % RING, r % CORES
        pairs.append((r, ((z + (-1 if c else 1)) % RING * RING + y) * CORES + c))
    return lax.ppermute(value, "res", pairs)


def to_row_owner(value, k):
    pairs = []
    for z in range(RING):
        for y in range(RING):
            for c in range(CORES):
                for x in range(RING):
                    source = ((z * RING + y) * CORES + c) * RING + x
                    target = ((x * RING + y) * CORES + c) * RING + (z + k + 2 * c) % RING
                    pairs.append((source, target))
    return lax.ppermute(value, ("res", "col"), pairs)


def contract_last(a, b):
    return lax.dot_general(a, b, (((1,), (1,)), ((), ())), preferred_element_type=F32)


def lanes_of(left, d, first, count, start, width):
    total = None
    lane = lax.broadcasted_iota(jnp.int32, (SEQS, LANES), 1)
    for at in range(count):
        row = left[:, d, first + at, :]
        move = (at * width - start) % LANES
        row = pltpu.roll(row, move, 1) if move else row
        if total is None:
            total = row
        else:
            total = jnp.where(lane >= at * width, row, total)
    return total


def project_kernel(emb, weights, chain, gain, shift, first, second, *rest):
    outs, (both, right, left) = rest[:RING], rest[RING:]
    _, y, _, _ = position()
    chains = weights.shape[1]
    ids = lax.broadcasted_iota(jnp.int32, (chains, COLS), 0)
    row = jnp.broadcast_to(chain[...].reshape(1, COLS), (chains, COLS))
    onehot = (row == ids).astype(F32).astype(BF16)
    mask = jnp.dot(weights[...], onehot, preferred_element_type=F32)
    both[0:SIDE] = first[...]
    both[SIDE:] = second[...]
    turn = lax.rem(RING - y, RING) * PLANE
    for s in range(SEQS):
        wide = emb[s].astype(F32)
        shifted = wide - jnp.mean(wide, axis=-1, keepdims=True)
        variance = jnp.mean(shifted * shifted, axis=-1, keepdims=True)
        value = shifted * lax.rsqrt(variance + 1e-05) * gain[...] + shift[...]
        sides = contract_last(both[...], value.astype(BF16)) * mask[s : s + 1]
        right[s] = sides[SIDE:]
        turned = pltpu.roll(sides[:SIDE], turn, 1)
        row = pltpu.roll(jnp.broadcast_to(mask[s : s + 1], (8, COLS)), turn, 1)
        for d in range(RING):
            left[s, d, 0:SIDE, 0:PLANE] = turned[:, d * PLANE : (d + 1) * PLANE]
            left[s, d, SIDE:, 0:PLANE] = row[:, d * PLANE : (d + 1) * PLANE]
            left[s, d, :, PLANE:] = jnp.zeros((SIDE + 8, LANES - PLANE), F32)
    for q in range(SIDE):
        part = right[:, q, :].astype(BF16)
        for out in outs:
            out[:, q * COLS : (q + 1) * COLS] = part
    for d, out in enumerate(outs):
        out[:, SIDE * COLS : RIGHT] = mask.astype(BF16)
        at = RIGHT
        for p in range(0, SIDE, 2):
            out[:, at : at + LANES] = lanes_of(left, d, p, 2, 0, MAJOR).astype(BF16)
            at += LANES
        for p in range(0, SIDE, 4):
            out[:, at : at + LANES] = lanes_of(left, d, p, 4, MAJOR, MINOR).astype(BF16)
            at += LANES
        out[:, at : at + LANES] = left[:, d, SIDE, :].astype(BF16)


def project(emb, weights, chain, gain, shift, first, second):
    vmem = pl.BlockSpec(memory_space=pltpu.VMEM)
    return pl.pallas_call(
        project_kernel,
        in_specs=[vmem] * 7,
        out_specs=[vmem] * RING,
        out_shape=[jax.ShapeDtypeStruct((SEQS, RIGHT + LEFT), BF16)] * RING,
        scratch_shapes=[
            pltpu.VMEM((2 * SIDE, EMBED), BF16),
            pltpu.VMEM((SEQS, SIDE, COLS), F32),
            pltpu.VMEM((SEQS, RING, SIDE + 8, LANES), F32),
        ],
        compiler_params=pltpu.CompilerParams(vmem_limit_bytes=60 * MEGA),
    )(
        emb,
        weights,
        chain,
        gain.reshape(1, EMBED),
        shift.reshape(1, EMBED),
        first.T,
        second.T,
    )


def stack_kernel(*refs):
    parts, (right, left, own_right, wide) = refs[: RING * CORES], refs[RING * CORES :]
    _, _, core, _ = position()
    step = 2 * COLS
    for at in [*range(0, RIGHT, step), *range(RIGHT, RIGHT + LEFT, step)]:
        out, start = (right, at) if at < RIGHT else (left, at - RIGHT)
        width = min(step, out.shape[1] - start)
        for c in range(CORES):
            base = pl.multiple_of(lax.rem(core + c, CORES) * GROUP, GROUP)
            half = wide.at[pl.ds(base, GROUP)]
            for d in range(RING):
                value = parts[c * RING + d][:, at : at + width].astype(F32)
                half[d * SEQS : (d + 1) * SEQS, :width] = value
            if c == 0 and out is right:
                own_right[:, start : start + width] = half[:, :width].astype(BF16)
        out[:, start : start + width] = wide[:, :width].astype(BF16)


def stack(parts):
    return pl.pallas_call(
        stack_kernel,
        out_shape=[
            jax.ShapeDtypeStruct((CHIP, RIGHT), BF16),
            jax.ShapeDtypeStruct((CHIP, LEFT), BF16),
            jax.ShapeDtypeStruct((GROUP, RIGHT), BF16),
        ],
        scratch_shapes=[pltpu.VMEM((CHIP, 2 * COLS), F32)],
        compiler_params=pltpu.CompilerParams(vmem_limit_bytes=16 * MEGA),
    )(*parts)


def left_kernel(weight, *refs):
    parts, refs = refs[:RING], refs[RING:]
    out, out_mask, out_weight, stacked, turned, wide_weight, sem = refs
    z, _, core, x = position()
    copies = []
    for at, part in enumerate(parts):
        group = lax.rem(z - x + at + 2 * core + RING, RING)
        start = pl.multiple_of(group * CHIP, CHIP)
        copies.append(pltpu.make_async_copy(part, stacked.at[pl.ds(start, CHIP), :], sem.at[at]))
    for copy in copies:
        copy.start()
    wide_weight[...] = weight[...].astype(F32)
    for q in range(0, SIDE, 4):
        rows = [wide_weight[pl.ds(q + at, SIDE, stride=SIDE), :] for at in range(4)]
        out_weight[:, q * SIDE : (q + 4) * SIDE] = jnp.concatenate(rows, 0).T.astype(BF16)
    for copy in copies:
        copy.wait()

    def block_at(at):
        return stacked[:, at : at + LANES].astype(F32).T

    at = 0
    for p in range(0, SIDE, 2):
        block = block_at(at)
        at += LANES
        for k in range(2):
            turned[(p + k) * PLANE : (p + k) * PLANE + MAJOR, :] = block[k * MAJOR : (k + 1) * MAJOR]
    for p in range(0, SIDE, 4):
        block = block_at(at)
        at += LANES
        for k in range(4):
            row = (p + k) * PLANE + MAJOR
            turned[row : row + MINOR, :] = block[k * MINOR : (k + 1) * MINOR]
    turned[SIDE * PLANE :, :] = block_at(at)[:PLANE]
    base = core * ROWS
    for i in range(ROWS):
        rows = turned[pl.ds(base + i, SIDE, stride=PLANE), :]
        out[i * SIDE : (i + 1) * SIDE, :] = rows.astype(BF16)
    start = pl.multiple_of(SIDE * PLANE + base, 8)
    out_mask[...] = turned[pl.ds(start, ROWS), :].astype(BF16)


def arrange_left(weight, parts):
    vmem = pl.BlockSpec(memory_space=pltpu.VMEM)
    return pl.pallas_call(
        left_kernel,
        in_specs=[vmem] + [pl.BlockSpec(memory_space=pl.ANY)] * len(parts),
        out_specs=[vmem] * 3,
        out_shape=[
            jax.ShapeDtypeStruct((ROWS * SIDE, TOTAL), BF16),
            jax.ShapeDtypeStruct((ROWS, TOTAL), BF16),
            jax.ShapeDtypeStruct((PAIR, SIDE * SIDE), BF16),
        ],
        scratch_shapes=[
            pltpu.VMEM((TOTAL, LEFT), BF16),
            pltpu.VMEM(((SIDE + 1) * PLANE, TOTAL), F32),
            pltpu.VMEM((SIDE * SIDE, PAIR), F32),
            pltpu.SemaphoreType.DMA((RING,)),
        ],
        compiler_params=pltpu.CompilerParams(vmem_limit_bytes=32 * MEGA),
    )(weight, *parts)


def pair_kernel(block, left, left_mask, weight, *refs):
    parts, (out, right, outer, scale, sem) = refs[: RING + 1], refs[RING + 1 :]
    _, _, core, _ = position()

    @pl.when(pl.program_id(0) == 0)
    def _():
        starts = [0, (1 + 2 * core) * CHIP, (3 - 2 * core) * CHIP]
        starts += [2 * CHIP + core * GROUP, 2 * CHIP + (1 - core) * GROUP]
        copies = []
        for k, part in enumerate(parts):
            rows = pl.ds(pl.multiple_of(starts[k], GROUP), part.shape[0])
            copies.append(pltpu.make_async_copy(part, right.at[rows, :], sem.at[k]))
        for copy in copies:
            copy.start()
        for copy in copies:
            copy.wait()
        counts = jnp.dot(
            left_mask[...], right[:, SIDE * COLS : (SIDE + 1) * COLS], preferred_element_type=F32
        )
        scale[...] = 1.0 / (counts + 0.001)

    value = left[...]
    for q in range(SIDE):
        part = jnp.dot(
            value, right[:, q * COLS : (q + 1) * COLS], preferred_element_type=F32
        ).astype(BF16)
        for i in range(block):
            outer[i, q * SIDE : (q + 1) * SIDE, :] = part[i * SIDE : (i + 1) * SIDE]
    first = pl.multiple_of(pl.program_id(0) * block, block)
    scales = scale[pl.ds(first, block), :]
    for i in range(block):
        projected = jnp.dot(weight[...], outer[i], preferred_element_type=F32)
        out[i] = (projected * scales[i : i + 1]).T.astype(BF16)


def pair(left, left_mask, weight, parts):
    block = 8
    whole = lambda a: pl.BlockSpec(a.shape, lambda i: (0,) * a.ndim)
    return pl.pallas_call(
        functools.partial(pair_kernel, block),
        grid=(ROWS // block,),
        in_specs=[
            pl.BlockSpec((block * SIDE, TOTAL), lambda i: (i, 0)),
            whole(left_mask),
            whole(weight),
        ]
        + [pl.BlockSpec(memory_space=pl.ANY)] * len(parts),
        out_specs=pl.BlockSpec((block, COLS, PAIR), lambda i: (i, 0, 0)),
        out_shape=jax.ShapeDtypeStruct((ROWS, COLS, PAIR), BF16),
        scratch_shapes=[
            pltpu.VMEM((TOTAL, RIGHT), BF16),
            pltpu.VMEM((block, SIDE * SIDE, COLS), BF16),
            pltpu.VMEM((ROWS, COLS), F32),
            pltpu.SemaphoreType.DMA((RING + 1,)),
        ],
        compiler_params=pltpu.CompilerParams(vmem_limit_bytes=48 * MEGA),
    )(left, left_mask, weight, *parts)


def local(
    homolog_embedding,
    sequence_row_mask,
    residue_chain_index,
    standardize_factor,
    standardize_shift,
    first_projector_matrix,
    second_projector_matrix,
    output_weight,
):
    own = project(
        homolog_embedding,
        sequence_row_mask,
        residue_chain_index,
        standardize_factor,
        standardize_shift,
        first_projector_matrix,
        second_projector_matrix,
    )
    along_y = [own[0]] + [res_shift(own[d], 0, d, 0) for d in range(1, RING)]
    right, left, own_right = stack(along_y + [core_swap(part) for part in along_y])
    left_parts = [to_row_owner(left, k) for k in range(2)]
    near, far = both_ways(right), res_shift(own_right, 2, 0, 0)
    prepared = arrange_left(output_weight, left_parts + [core_swap(part) for part in left_parts])
    prepared, near, far = lax.optimization_barrier((prepared, near, far))
    return pair(*prepared, [right, near, core_swap(near), far, core_swap(far)])


def solution(mesh):
    in_specs = (P("res", "col", None), P("res", None), P("col"), P(), P(), P(), P(), P())
    out_specs = P("res", "col", None)
    return jax.shard_map(local, mesh=mesh, in_specs=in_specs, out_specs=out_specs, check_vma=False)
```

time: 95.4 us -> 71.9 us (0.75)
  the two profiles are of different devices: /device:TPU:5 before, /device:TPU:7 now
where the time goes in v2:
time: 71.9 us; the launch traced here: 71.8 us
  Pallas kernels  26.5 us (37%)
  starting transfers between devices  22 us (31%)
  waiting for transfers between devices  21.4 us (30%)
  local copies, waits for them, and re-layouts  1.85 us (3%)
    pallas_call x1, Pallas kernels, pair(): pl.pallas_call(functools.partial(pair_kernel, block), grid=(ROWS // block...  20.1 us
    ppermute x12, starting transfers between devices, res_shift(): return lax.ppermute(value, 'res', pairs)  15.8 us
    ppermute x2, waiting for transfers between devices, to_row_owner(): return lax.ppermute(value, ('res', 'col'), pairs)  14.1 us
    ppermute x12, waiting for transfers between devices, res_shift(): return lax.ppermute(value, 'res', pairs)  7.31 us
    ppermute x1, starting transfers between devices, both_ways(): return lax.ppermute(value, 'res', pairs)  3.82 us
    pallas_call x1, Pallas kernels, project(): pl.pallas_call(project_kernel, in_specs=[vmem] * 7, out_specs=[vmem] * RI...  3.51 us
    ppermute x2, starting transfers between devices, to_row_owner(): return lax.ppermute(value, ('res', 'col'), pairs)  2.37 us
    pallas_call x1, Pallas kernels, arrange_left(): pl.pallas_call(left_kernel, in_specs=[vmem] + [pl.BlockSpec(memory_space=...  2.26 us
  transfers between devices with their start and end apart: 15, of which 7 were waited for; matrix products, arithmetic and copies ran while one was open for 0% of the time, Pallas kernels for 3%

profile of v2, /device:TPU:7, one launch (start us, length us, event | category | flops | bytes accessed | tf_op | source)
XLA Modules:
  0.0 71.8 jit_solution(14661750442171150001)
XLA Ops:
  0.0 3.5 %shard_map.82 = (bf16[4,15872]{1,0:T(4,128)(2,1)}, bf16[4,15872]{1,0:T(4,128)(2,1)}, bf16[4,15872]{1,0:T(4,128)(2,1)}, bf16[4,15872]{1,0:T(4,128)(2,1)}) custom-call(bf16[4,384,256]{2,1,0:T(8,128)(2,1)} %emb.1, bf16[4,8]{1,0:T(4,128)(2,1)} %weights.1, s32[384]{0:T(512)} %chain.1, f32[1,256]{1,0:T(1,128)} %bitcast.6, f32[1,256]{1,0:T(1,128)} %bitcast.7, ...), custom_call_target="tpu_custom_call" | custom-call | tf_op jit(solution)/shard_map/pallas_call | solution.py:129
  3.5 1.3 %collective-permute-start = (bf16[4,15872]{1,0:T(4,128)(2,1)}, bf16[4,15872]{1,0:T(4,128)(2,1)S(1)}, u32[]{:S(2)}, u32[]{:S(2)}) collective-permute-start(bf16[4,15872]{1,0:T(4,128)(2,1)} %get-tuple-element.21), channel_id=1, source_target_pairs={{0,8},{4,12},{8,16},{12,20},{16,24},{20,28},{24,0},{28,4},{32,40},... | collective-permute-start | bytes 380936 | tf_op jit(solution)/shard_map/ppermute | solution.py:42
  4.8 2.6 %collective-permute-start.1 = (bf16[4,15872]{1,0:T(4,128)(2,1)}, bf16[4,15872]{1,0:T(4,128)(2,1)S(1)}, u32[]{:S(2)}, u32[]{:S(2)}) collective-permute-start(bf16[4,15872]{1,0:T(4,128)(2,1)} %get-tuple-element.22), channel_id=1, source_target_pairs={{0,16},{4,20},{8,24},{12,28},{16,0},{20,4},{24,8},{28,12},{32,48},... | collective-permute-start | bytes 380936 | tf_op jit(solution)/shard_map/ppermute | solution.py:42
  7.4 1.1 %collective-permute-start.2 = (bf16[4,15872]{1,0:T(4,128)(2,1)}, bf16[4,15872]{1,0:T(4,128)(2,1)S(1)}, u32[]{:S(2)}, u32[]{:S(2)}) collective-permute-start(bf16[4,15872]{1,0:T(4,128)(2,1)} %get-tuple-element.23), channel_id=1, source_target_pairs={{0,24},{4,28},{8,0},{12,4},{16,8},{20,12},{24,16},{28,20},{32,56},... | collective-permute-start | bytes 380936 | tf_op jit(solution)/shard_map/ppermute | solution.py:42
  8.5 1.5 %collective-permute-start.3 = (bf16[4,15872]{1,0:T(4,128)(2,1)}, bf16[4,15872]{1,0:T(4,128)(2,1)S(1)}, u32[]{:S(2)}, u32[]{:S(2)}) collective-permute-start(bf16[4,15872]{1,0:T(4,128)(2,1)} %get-tuple-element.20.refs_0_), channel_id=1, source_target_pairs={{0,4},{4,0},{8,12},{12,8},{16,20},{20,16},{24,28},{28,24},{32,36},... | collective-permute-start | bytes 380936 | tf_op jit(solution)/shard_map/ppermute | solution.py:42
  10.0 0.0 collective-permute-done.refs_1_
  10.0 0.8 %collective-permute-start.4 = (bf16[4,15872]{1,0:T(4,128)(2,1)S(1)}, bf16[4,15872]{1,0:T(4,128)(2,1)S(1)}, u32[]{:S(2)}, u32[]{:S(2)}) collective-permute-start(bf16[4,15872]{1,0:T(4,128)(2,1)S(1)} %collective-permute-done.refs_1_), channel_id=1, source_target_pairs={{0,4},{4,0},{8,12},{12,8},{16,20},{20,16},{24,28},{28,24},{32,36},... | collective-permute-start | bytes 380936 | tf_op jit(solution)/shard_map/ppermute | solution.py:42
  10.8 2.3 %collective-permute-done.1.refs_2_ = bf16[4,15872]{1,0:T(4,128)(2,1)S(1)} collective-permute-done((bf16[4,15872]{1,0:T(4,128)(2,1)}, bf16[4,15872]{1,0:T(4,128)(2,1)S(1)}, u32[]{:S(2)}, u32[]{:S(2)}) %collective-permute-start.1) | collective-permute-done | bytes 127008 | tf_op jit(solution)/shard_map/ppermute | solution.py:42
  13.2 1.6 %collective-permute-start.5 = (bf16[4,15872]{1,0:T(4,128)(2,1)S(1)}, bf16[4,15872]{1,0:T(4,128)(2,1)S(1)}, u32[]{:S(2)}, u32[]{:S(2)}) collective-permute-start(bf16[4,15872]{1,0:T(4,128)(2,1)S(1)} %collective-permute-done.1.refs_2_), channel_id=1, source_target_pairs={{0,4},{4,0},{8,12},{12,8},{16,20},{20,16},{24,28},{28,24},{32,36},... | collective-permute-start | bytes 380936 | tf_op jit(solution)/shard_map/ppermute | solution.py:42
  14.7 0.0 collective-permute-done.2.refs_3_
  14.7 0.0 collective-permute-start.6
  14.7 0.0 collective-permute-done.3.refs_4_
  14.7 0.0 collective-permute-done.4.refs_5_
  14.7 1.0 %collective-permute-done.5.refs_6_ = bf16[4,15872]{1,0:T(4,128)(2,1)S(1)} collective-permute-done((bf16[4,15872]{1,0:T(4,128)(2,1)S(1)}, bf16[4,15872]{1,0:T(4,128)(2,1)S(1)}, u32[]{:S(2)}, u32[]{:S(2)}) %collective-permute-start.5) | collective-permute-done | bytes 127008 | tf_op jit(solution)/shard_map/ppermute | solution.py:42
  15.7 0.4 collective-permute-done.6.refs_7_
  16.1 0.0 copy-start.1
  16.1 0.9 %copy-done.1 = bf16[4,15872]{1,0:T(4,128)(2,1)S(1)} copy-done((bf16[4,15872]{1,0:T(4,128)(2,1)S(1)}, bf16[4,15872]{1,0:T(4,128)(2,1)}, u32[]{:S(2)}) %copy-start.1) | copy-done | bytes 127000
  17.0 0.6 shard_map.83
  17.6 3.8 %collective-permute-start.11 = (bf16[32,12672]{1,0:T(8,128)(2,1)S(1)}, bf16[32,12672]{1,0:T(8,128)(2,1)S(1)}, u32[]{:S(2)}, u32[]{:S(2)}) collective-permute-start(bf16[32,12672]{1,0:T(8,128)(2,1)S(1)} %get-tuple-element.28.refs_0_), channel_id=1, source_target_pairs={{0,32},{4,100},{8,40},{12,108},{16,48},{20,116},{24,56},{28,124},{... | collective-permute-start | bytes 2433032 | tf_op jit(solution)/shard_map/ppermute | solution.py:54
  21.4 0.1 collective-permute-start.8
  21.6 2.2 %collective-permute-start.7 = (bf16[32,3200]{1,0:T(8,128)(2,1)S(1)}, bf16[32,3200]{1,0:T(8,128)(2,1)S(1)}, u32[]{:S(2)}, u32[]{:S(2)}) collective-permute-start(bf16[32,3200]{1,0:T(8,128)(2,1)S(1)} %get-tuple-element.24), channel_id=1, source_target_pairs={{0,0},{1,32},{2,64},{3,96},{4,6},{5,38},{6,70},{7,102},{8,8},{9,40... | collective-permute-start | bytes 614408 | tf_op jit(solution)/shard_map/ppermute | solution.py:66
  23.8 5.8 %collective-permute-start.12 = (bf16[16,12672]{1,0:T(8,128)(2,1)S(1)}, bf16[16,12672]{1,0:T(8,128)(2,1)S(1)}, u32[]{:S(2)}, u32[]{:S(2)}) collective-permute-start(bf16[16,12672]{1,0:T(8,128)(2,1)S(1)} %get-tuple-element.29), channel_id=1, source_target_pairs={{0,64},{4,68},{8,72},{12,76},{16,80},{20,84},{24,88},{28,92},{32,9... | collective-permute-start | bytes 1216520 | tf_op jit(solution)/shard_map/ppermute | solution.py:42
  29.7 14.1 %collective-permute-done.8.refs_1_ = bf16[32,3200]{1,0:T(8,128)(2,1)S(1)} collective-permute-done((bf16[32,3200]{1,0:T(8,128)(2,1)S(1)}, bf16[32,3200]{1,0:T(8,128)(2,1)S(1)}, u32[]{:S(2)}, u32[]{:S(2)}) %collective-permute-start.8) | collective-permute-done | bytes 204832 | tf_op jit(solution)/shard_map/ppermute | solution.py:66
  43.7 0.0 collective-permute-start.10
  43.7 0.0 collective-permute-done.7.refs_0_
  43.7 0.5 collective-permute-start.9
  44.2 0.9 %collective-permute-done.10.refs_3_ = bf16[32,3200]{1,0:T(8,128)(2,1)S(1)} collective-permute-done((bf16[32,3200]{1,0:T(8,128)(2,1)S(1)}, bf16[32,3200]{1,0:T(8,128)(2,1)S(1)}, u32[]{:S(2)}, u32[]{:S(2)}) %collective-permute-start.10) | collective-permute-done | bytes 204832 | tf_op jit(solution)/shard_map/ppermute | solution.py:42
  45.2 0.3 collective-permute-done.9.refs_2_
  45.5 0.0 copy-start
  45.5 0.9 %copy-done = bf16[1024,128]{1,0:T(8,128)(2,1)S(1)} copy-done((bf16[1024,128]{1,0:T(8,128)(2,1)S(1)}, bf16[1024,128]{1,0:T(8,128)(2,1)}, u32[]{:S(2)}) %copy-start) | copy-done | bytes 262168
  46.4 2.3 %shard_map.84 = (bf16[1536,128]{1,0:T(8,128)(2,1)S(1)}, bf16[48,128]{1,0:T(8,128)(2,1)S(1)}, bf16[128,1024]{1,0:T(8,128)(2,1)S(1)}) custom-call(bf16[1024,128]{1,0:T(8,128)(2,1)S(1)} %copy-done, bf16[32,3200]{1,0:T(8,128)(2,1)S(1)} %collective-permute-done.7.refs_0_, bf16[32,3200]{1,0:T(8,128)(2,1)S(1)} %collective-permute-done.8.refs_1_, ...), custom_call_target="tpu_custom_call" | custom-call | tf_op jit(solution)/shard_map/pallas_call | solution.py:226
  48.7 0.0 collective-permute-done.12.refs_3_
  48.7 0.0 collective-permute-done.11.refs_1_
  48.7 0.3 collective-permute-start.13
  49.0 0.3 collective-permute-start.14
  49.3 2.4 %collective-permute-done.14.refs_4_ = bf16[16,12672]{1,0:T(8,128)(2,1)S(1)} collective-permute-done((bf16[16,12672]{1,0:T(8,128)(2,1)S(1)}, bf16[16,12672]{1,0:T(8,128)(2,1)S(1)}, u32[]{:S(2)}, u32[]{:S(2)}) %collective-permute-start.14) | collective-permute-done | bytes 405536 | tf_op jit(solution)/shard_map/ppermute | solution.py:42
  51.7 0.0 collective-permute-done.13.refs_2_
  51.7 20.1 %shard_map.85 = bf16[48,384,128]{2,1,0:T(8,128)(2,1)} custom-call(bf16[1536,128]{1,0:T(8,128)(2,1)S(1)} %get-tuple-element.30.left, bf16[48,128]{1,0:T(8,128)(2,1)S(1)} %get-tuple-element.31.left_mask, bf16[128,1024]{1,0:T(8,128)(2,1)S(1)} %get-tuple-element.32.weight, bf16[32,12672]{1,0:T(8,128)(2,1)S(1)} %get-tuple-element.28.refs_0_, ...), custom_call_target="tpu_custom_call" | custom-call | tf_op jit(solution)/shard_map/pallas_call | solution.py:283
Async XLA Ops:
  3.5 6.5 %collective-permute-start = (bf16[4,15872]{1,0:T(4,128)(2,1)}, bf16[4,15872]{1,0:T(4,128)(2,1)S(1)}, u32[]{:S(2)}, u32[]{:S(2)}) collective-permute-start(bf16[4,15872]{1,0:T(4,128)(2,1)} %get-tuple-element.21), channel_id=1, source_target_pairs={{0,8},{4,12},{8,16},{12,20},{16,24},{20,28},{24,0},{28,4},{32,40},... | collective-permute-start | bytes 380936 | tf_op jit(solution)/shard_map/ppermute | solution.py:42
  4.8 8.4 %collective-permute-start.1 = (bf16[4,15872]{1,0:T(4,128)(2,1)}, bf16[4,15872]{1,0:T(4,128)(2,1)S(1)}, u32[]{:S(2)}, u32[]{:S(2)}) collective-permute-start(bf16[4,15872]{1,0:T(4,128)(2,1)} %get-tuple-element.22), channel_id=1, source_target_pairs={{0,16},{4,20},{8,24},{12,28},{16,0},{20,4},{24,8},{28,12},{32,48},... | collective-permute-start | bytes 380936 | tf_op jit(solution)/shard_map/ppermute | solution.py:42
  7.4 7.3 %collective-permute-start.2 = (bf16[4,15872]{1,0:T(4,128)(2,1)}, bf16[4,15872]{1,0:T(4,128)(2,1)S(1)}, u32[]{:S(2)}, u32[]{:S(2)}) collective-permute-start(bf16[4,15872]{1,0:T(4,128)(2,1)} %get-tuple-element.23), channel_id=1, source_target_pairs={{0,24},{4,28},{8,0},{12,4},{16,8},{20,12},{24,16},{28,20},{32,56},... | collective-permute-start | bytes 380936 | tf_op jit(solution)/shard_map/ppermute | solution.py:42
  8.5 6.2 %collective-permute-start.3 = (bf16[4,15872]{1,0:T(4,128)(2,1)}, bf16[4,15872]{1,0:T(4,128)(2,1)S(1)}, u32[]{:S(2)}, u32[]{:S(2)}) collective-permute-start(bf16[4,15872]{1,0:T(4,128)(2,1)} %get-tuple-element.20.refs_0_), channel_id=1, source_target_pairs={{0,4},{4,0},{8,12},{12,8},{16,20},{20,16},{24,28},{28,24},{32,36},... | collective-permute-start | bytes 380936 | tf_op jit(solution)/shard_map/ppermute | solution.py:42
  10.0 4.7 %collective-permute-start.4 = (bf16[4,15872]{1,0:T(4,128)(2,1)S(1)}, bf16[4,15872]{1,0:T(4,128)(2,1)S(1)}, u32[]{:S(2)}, u32[]{:S(2)}) collective-permute-start(bf16[4,15872]{1,0:T(4,128)(2,1)S(1)} %collective-permute-done.refs_1_), channel_id=1, source_target_pairs={{0,4},{4,0},{8,12},{12,8},{16,20},{20,16},{24,28},{28,24},{32,36},... | collective-permute-start | bytes 380936 | tf_op jit(solution)/shard_map/ppermute | solution.py:42
  13.2 2.5 %collective-permute-start.5 = (bf16[4,15872]{1,0:T(4,128)(2,1)S(1)}, bf16[4,15872]{1,0:T(4,128)(2,1)S(1)}, u32[]{:S(2)}, u32[]{:S(2)}) collective-permute-start(bf16[4,15872]{1,0:T(4,128)(2,1)S(1)} %collective-permute-done.1.refs_2_), channel_id=1, source_target_pairs={{0,4},{4,0},{8,12},{12,8},{16,20},{20,16},{24,28},{28,24},{32,36},... | collective-permute-start | bytes 380936 | tf_op jit(solution)/shard_map/ppermute | solution.py:42
  14.7 1.3 %collective-permute-start.6 = (bf16[4,15872]{1,0:T(4,128)(2,1)S(1)}, bf16[4,15872]{1,0:T(4,128)(2,1)S(1)}, u32[]{:S(2)}, u32[]{:S(2)}) collective-permute-start(bf16[4,15872]{1,0:T(4,128)(2,1)S(1)} %collective-permute-done.2.refs_3_), channel_id=1, source_target_pairs={{0,4},{4,0},{8,12},{12,8},{16,20},{20,16},{24,28},{28,24},{32,36},... | collective-permute-start | bytes 380936 | tf_op jit(solution)/shard_map/ppermute | solution.py:42
  16.1 0.9 %copy-start.1 = (bf16[4,15872]{1,0:T(4,128)(2,1)S(1)}, bf16[4,15872]{1,0:T(4,128)(2,1)}, u32[]{:S(2)}) copy-start(bf16[4,15872]{1,0:T(4,128)(2,1)} %get-tuple-element.20.refs_0_) | copy-start | bytes 380932
  17.6 31.1 %collective-permute-start.11 = (bf16[32,12672]{1,0:T(8,128)(2,1)S(1)}, bf16[32,12672]{1,0:T(8,128)(2,1)S(1)}, u32[]{:S(2)}, u32[]{:S(2)}) collective-permute-start(bf16[32,12672]{1,0:T(8,128)(2,1)S(1)} %get-tuple-element.28.refs_0_), channel_id=1, source_target_pairs={{0,32},{4,100},{8,40},{12,108},{16,48},{20,116},{24,56},{28,124},{... | collective-permute-start | bytes 2433032 | tf_op jit(solution)/shard_map/ppermute | solution.py:54
  21.4 22.3 %collective-permute-start.8 = (bf16[32,3200]{1,0:T(8,128)(2,1)S(1)}, bf16[32,3200]{1,0:T(8,128)(2,1)S(1)}, u32[]{:S(2)}, u32[]{:S(2)}) collective-permute-start(bf16[32,3200]{1,0:T(8,128)(2,1)S(1)} %get-tuple-element.24), channel_id=1, source_target_pairs={{0,1},{1,33},{2,65},{3,97},{4,7},{5,39},{6,71},{7,103},{8,9},{9,41... | collective-permute-start | bytes 614408 | tf_op jit(solution)/shard_map/ppermute | solution.py:66
  21.6 22.2 %collective-permute-start.7 = (bf16[32,3200]{1,0:T(8,128)(2,1)S(1)}, bf16[32,3200]{1,0:T(8,128)(2,1)S(1)}, u32[]{:S(2)}, u32[]{:S(2)}) collective-permute-start(bf16[32,3200]{1,0:T(8,128)(2,1)S(1)} %get-tuple-element.24), channel_id=1, source_target_pairs={{0,0},{1,32},{2,64},{3,96},{4,6},{5,38},{6,70},{7,102},{8,8},{9,40... | collective-permute-start | bytes 614408 | tf_op jit(solution)/shard_map/ppermute | solution.py:66
  23.8 24.9 %collective-permute-start.12 = (bf16[16,12672]{1,0:T(8,128)(2,1)S(1)}, bf16[16,12672]{1,0:T(8,128)(2,1)S(1)}, u32[]{:S(2)}, u32[]{:S(2)}) collective-permute-start(bf16[16,12672]{1,0:T(8,128)(2,1)S(1)} %get-tuple-element.29), channel_id=1, source_target_pairs={{0,64},{4,68},{8,72},{12,76},{16,80},{20,84},{24,88},{28,92},{32,9... | collective-permute-start | bytes 1216520 | tf_op jit(solution)/shard_map/ppermute | solution.py:42
  43.7 1.5 %collective-permute-start.10 = (bf16[32,3200]{1,0:T(8,128)(2,1)S(1)}, bf16[32,3200]{1,0:T(8,128)(2,1)S(1)}, u32[]{:S(2)}, u32[]{:S(2)}) collective-permute-start(bf16[32,3200]{1,0:T(8,128)(2,1)S(1)} %collective-permute-done.8.refs_1_), channel_id=1, source_target_pairs={{0,4},{4,0},{8,12},{12,8},{16,20},{20,16},{24,28},{28,24},{32,36},... | collective-permute-start | bytes 614408 | tf_op jit(solution)/shard_map/ppermute | solution.py:42
  43.7 1.7 %collective-permute-start.9 = (bf16[32,3200]{1,0:T(8,128)(2,1)S(1)}, bf16[32,3200]{1,0:T(8,128)(2,1)S(1)}, u32[]{:S(2)}, u32[]{:S(2)}) collective-permute-start(bf16[32,3200]{1,0:T(8,128)(2,1)S(1)} %collective-permute-done.7.refs_0_), channel_id=1, source_target_pairs={{0,4},{4,0},{8,12},{12,8},{16,20},{20,16},{24,28},{28,24},{32,36},... | collective-permute-start | bytes 614408 | tf_op jit(solution)/shard_map/ppermute | solution.py:42
  45.5 1.0 %copy-start = (bf16[1024,128]{1,0:T(8,128)(2,1)S(1)}, bf16[1024,128]{1,0:T(8,128)(2,1)}, u32[]{:S(2)}) copy-start(bf16[1024,128]{1,0:T(8,128)(2,1)} %weight.1) | copy-start | bytes 786436
  48.7 3.0 %collective-permute-start.13 = (bf16[32,12672]{1,0:T(8,128)(2,1)S(1)}, bf16[32,12672]{1,0:T(8,128)(2,1)S(1)}, u32[]{:S(2)}, u32[]{:S(2)}) collective-permute-start(bf16[32,12672]{1,0:T(8,128)(2,1)S(1)} %collective-permute-done.11.refs_1_), channel_id=1, source_target_pairs={{0,4},{4,0},{8,12},{12,8},{16,20},{20,16},{24,28},{28,24},{32,36},... | collective-permute-start | bytes 2433032 | tf_op jit(solution)/shard_map/ppermute | solution.py:42
  49.0 2.7 %collective-permute-start.14 = (bf16[16,12672]{1,0:T(8,128)(2,1)S(1)}, bf16[16,12672]{1,0:T(8,128)(2,1)S(1)}, u32[]{:S(2)}, u32[]{:S(2)}) collective-permute-start(bf16[16,12672]{1,0:T(8,128)(2,1)S(1)} %collective-permute-done.12.refs_3_), channel_id=1, source_target_pairs={{0,4},{4,0},{8,12},{12,8},{16,20},{20,16},{24,28},{28,24},{32,36},... | collective-permute-start | bytes 1216520 | tf_op jit(solution)/shard_map/ppermute | solution.py:42

commit v3 on v2

v3 whole, which is shorter than its diff:
```python
import functools

import jax
import jax.numpy as jnp
from jax import lax
from jax.experimental import pallas as pl
from jax.experimental.pallas import tpu as pltpu
from jax.sharding import PartitionSpec as P

RING = 4
CORES = 2
SEQS = 4
EMBED = 256
SIDE = 32
PAIR = 128
COLS = 384
ROWS = 48
PLANE = ROWS * CORES
GROUP = SEQS * RING
CHIP = GROUP * CORES
TOTAL = CHIP * RING
LANES = 128
RIGHT = (SIDE + 1) * COLS
MAJOR, MINOR = 64, 32
LEFT = SIDE * PLANE + LANES
MEGA = 2**20
F32 = jnp.float32
BF16 = jnp.bfloat16


def position():
    res = lax.axis_index("res")
    return res // (RING * CORES), (res // CORES) % RING, res % CORES, lax.axis_index("col")


def res_shift(value, dz, dy, dc):
    pairs = []
    for r in range(RING * RING * CORES):
        z, y, c = r // (RING * CORES), (r // CORES) % RING, r % CORES
        to = (((z + dz) % RING) * RING + (y + dy) % RING) * CORES + (c + dc) % CORES
        pairs.append((r, to))
    return lax.ppermute(value, "res", pairs)


def core_swap(value):
    return res_shift(value, 0, 0, 1)


def both_ways(value, dz, dy):
    pairs = []
    for r in range(RING * RING * CORES):
        z, y, c = r // (RING * CORES), (r // CORES) % RING, r % CORES
        way = -1 if c else 1
        z, y = (z + way * dz) % RING, (y + way * dy) % RING
        pairs.append((r, (z * RING + y) * CORES + c))
    return lax.ppermute(value, "res", pairs)


def to_row_owner(value, k):
    pairs = []
    for z in range(RING):
        for y in range(RING):
            for c in range(CORES):
                for x in range(RING):
                    source = ((z * RING + y) * CORES + c) * RING + x
                    target = ((x * RING + y) * CORES + c) * RING + (z + k + 2 * c) % RING
                    pairs.append((source, target))
    return lax.ppermute(value, ("res", "col"), pairs)


def contract_last(a, b):
    return lax.dot_general(a, b, (((1,), (1,)), ((), ())), preferred_element_type=F32)


def side_by_side(value, count, start, width):
    rows = value.shape[0] // count
    lane = lax.broadcasted_iota(jnp.int32, (rows, LANES), 1)
    total = None
    for at in range(count):
        part = value[at * rows : (at + 1) * rows]
        move = (at * width - start) % LANES
        part = pltpu.roll(part, move, 1) if move else part
        total = part if total is None else jnp.where(lane >= at * width, part, total)
    return total


def project_kernel(*refs):
    arguments, outs = refs[:7], refs[7 : 8 + RING]
    emb, weights, chain, gain, shift, first, second = arguments
    both, right, left = refs[8 + RING :]
    _, y, _, _ = position()
    chains = weights.shape[1]
    ids = lax.broadcasted_iota(jnp.int32, (chains, COLS), 0)
    row = jnp.broadcast_to(chain[...].reshape(1, COLS), (chains, COLS))
    onehot = (row == ids).astype(F32).astype(BF16)
    mask = jnp.dot(weights[...], onehot, preferred_element_type=F32)
    both[0:SIDE] = first[...]
    both[SIDE:] = second[...]
    turn = lax.rem(RING - y, RING) * PLANE
    for s in range(SEQS):
        wide = emb[s].astype(F32)
        shifted = wide - jnp.mean(wide, axis=-1, keepdims=True)
        variance = jnp.mean(shifted * shifted, axis=-1, keepdims=True)
        value = shifted * lax.rsqrt(variance + 1e-05) * gain[...].reshape(1, EMBED)
        value = (value + shift[...].reshape(1, EMBED)).astype(BF16)
        sides = contract_last(both[...], value) * mask[s : s + 1]
        right[s] = sides[SIDE:]
        turned = pltpu.roll(sides[:SIDE], turn, 1)
        row = pltpu.roll(jnp.broadcast_to(mask[s : s + 1], (8, COLS)), turn, 1)
        fill = jnp.zeros((SIDE, LANES - PLANE), F32)
        for d in range(RING):
            part = jnp.concatenate([turned[:, d * PLANE : (d + 1) * PLANE], fill], 1)
            left[s, d, 0 : SIDE // 2] = side_by_side(part, 2, 0, MAJOR)
            left[s, d, SIDE // 2 : 3 * SIDE // 4] = side_by_side(part, 4, MAJOR, MINOR)
            part = jnp.concatenate([row[:, d * PLANE : (d + 1) * PLANE], fill[:8]], 1)
            left[s, d, 3 * SIDE // 4 :] = part
    for q in range(SIDE):
        part = right[:, q, :].astype(BF16)
        for out in outs:
            out[:, q * COLS : (q + 1) * COLS] = part
    for out in outs:
        out[:, SIDE * COLS : RIGHT] = mask.astype(BF16)
    for d, out in enumerate(outs[:RING]):
        for at in range(LEFT // LANES):
            to = RIGHT + at * LANES
            out[:, to : to + LANES] = left[:, d, at, :].astype(BF16)


def project(emb, weights, chain, gain, shift, first, second):
    arguments = (emb, weights, chain, gain, shift, first.T, second.T)
    return pl.pallas_call(
        project_kernel,
        in_specs=[pl.BlockSpec(memory_space=pltpu.VMEM)] * len(arguments),
        out_specs=[pl.BlockSpec(memory_space=pltpu.VMEM)] * (RING + 1),
        out_shape=[jax.ShapeDtypeStruct((SEQS, RIGHT + LEFT), BF16)] * RING
        + [jax.ShapeDtypeStruct((SEQS, RIGHT), BF16)],
        scratch_shapes=[
            pltpu.VMEM((2 * SIDE, EMBED), BF16),
            pltpu.VMEM((SEQS, SIDE, COLS), F32),
            pltpu.VMEM((SEQS, RING, LEFT // LANES + 7, LANES), F32),
        ],
        compiler_params=pltpu.CompilerParams(vmem_limit_bytes=60 * MEGA),
    )(*arguments)


def weight_kernel(weight_hbm, out, weight, wide, sem):
    copy = pltpu.make_async_copy(weight_hbm, weight, sem)
    copy.start()
    copy.wait()
    wide[...] = weight[...].astype(F32)
    for q in range(0, SIDE, 4):
        rows = [wide[pl.ds(q + at, SIDE, stride=SIDE), :] for at in range(4)]
        out[:, q * SIDE : (q + 4) * SIDE] = jnp.concatenate(rows, 0).T.astype(BF16)


def arrange_weight(weight):
    return pl.pallas_call(
        weight_kernel,
        in_specs=[pl.BlockSpec(memory_space=pl.ANY)],
        out_specs=pl.BlockSpec(memory_space=pltpu.VMEM),
        out_shape=jax.ShapeDtypeStruct((PAIR, SIDE * SIDE), BF16),
        scratch_shapes=[
            pltpu.VMEM((SIDE * SIDE, PAIR), BF16),
            pltpu.VMEM((SIDE * SIDE, PAIR), F32),
            pltpu.SemaphoreType.DMA,
        ],
        compiler_params=pltpu.CompilerParams(vmem_limit_bytes=16 * MEGA),
    )(weight)


def chunks(width):
    return [(at, min(2 * COLS, width - at)) for at in range(0, width, 2 * COLS)]


def by_core(core, own, other):
    return jnp.where(core == 0, own, other), jnp.where(core == 0, other, own)


def stack_kernel(*refs):
    parts, (far, far_other, right, left, far_chip, wide) = refs[: RING * CORES], refs[RING * CORES :]
    _, _, core, _ = position()
    for out, base in ((right, 0), (left, RIGHT)):
        for at, width in chunks(out.shape[1]):
            lanes = slice(base + at, base + at + width)
            for c in range(CORES):
                start = pl.multiple_of(lax.rem(core + c, CORES) * GROUP, GROUP)
                half = wide.at[pl.ds(start, GROUP)]
                for d in range(RING):
                    half[d * SEQS : (d + 1) * SEQS, :width] = parts[c * RING + d][:, lanes].astype(F32)
            out[:, at : at + width] = wide[:, :width].astype(BF16)
    for at, width in chunks(RIGHT):
        lanes = slice(at, at + width)
        values = by_core(core, far[:, lanes].astype(F32), far_other[:, lanes].astype(F32))
        for c in range(CORES):
            wide[c * SEQS : (c + 1) * SEQS, :width] = values[c]
        far_chip[:, lanes] = wide[: CORES * SEQS, :width].astype(BF16)


def stack(parts, far, far_other):
    return pl.pallas_call(
        stack_kernel,
        out_shape=[
            jax.ShapeDtypeStruct((CHIP, RIGHT), BF16),
            jax.ShapeDtypeStruct((CHIP, LEFT), BF16),
            jax.ShapeDtypeStruct((CORES * SEQS, RIGHT), BF16),
        ],
        scratch_shapes=[pltpu.VMEM((CHIP, 2 * COLS), F32)],
        compiler_params=pltpu.CompilerParams(vmem_limit_bytes=16 * MEGA),
    )(*parts, far, far_other)


def far_kernel(own, near, near_other, far, far_other, out, wide):
    _, _, core, _ = position()
    for at, width in chunks(RIGHT):
        lanes = slice(at, at + width)
        below, above = by_core(core, near[:, lanes].astype(F32), near_other[:, lanes].astype(F32))
        opposite = by_core(core, far[:, lanes].astype(F32), far_other[:, lanes].astype(F32))
        here = own[:, lanes].astype(F32)
        for c in range(CORES):
            rows = slice(c * SEQS, (c + 1) * SEQS)
            for d, value in enumerate((here[rows], below[rows], opposite[c], above[rows])):
                start = c * GROUP + d * SEQS
                wide[start : start + SEQS, :width] = value
        out[:, lanes] = wide[:, :width].astype(BF16)


def stack_far(*parts):
    return pl.pallas_call(
        far_kernel,
        out_shape=jax.ShapeDtypeStruct((CHIP, RIGHT), BF16),
        scratch_shapes=[pltpu.VMEM((CHIP, 2 * COLS), F32)],
        compiler_params=pltpu.CompilerParams(vmem_limit_bytes=16 * MEGA),
    )(*parts)


def left_kernel(*refs):
    parts, (out, out_mask, stacked, turned, sem) = refs[:RING], refs[RING:]
    z, _, core, x = position()
    copies = []
    for at, part in enumerate(parts):
        group = lax.rem(z - x + at + 2 * core + RING, RING)
        start = pl.multiple_of(group * CHIP, CHIP)
        copies.append(pltpu.make_async_copy(part, stacked.at[pl.ds(start, CHIP), :], sem.at[at]))
    for copy in copies:
        copy.start()
    for copy in copies:
        copy.wait()

    def block_at(at):
        return stacked[:, at * LANES : (at + 1) * LANES].astype(F32).T

    for p in range(SIDE // 2):
        block = block_at(p)
        for k in range(2):
            row = (p + k * SIDE // 2) * PLANE
            turned[row : row + MAJOR, :] = block[k * MAJOR : (k + 1) * MAJOR]
    for p in range(SIDE // 4):
        block = block_at(SIDE // 2 + p)
        for k in range(4):
            row = (p + k * SIDE // 4) * PLANE + MAJOR
            turned[row : row + MINOR, :] = block[k * MINOR : (k + 1) * MINOR]
    turned[SIDE * PLANE :, :] = block_at(3 * SIDE // 4)[:PLANE]
    base = core * ROWS
    for i in range(ROWS):
        rows = turned[pl.ds(base + i, SIDE, stride=PLANE), :]
        out[i * SIDE : (i + 1) * SIDE, :] = rows.astype(BF16)
    start = pl.multiple_of(SIDE * PLANE + base, 8)
    out_mask[...] = turned[pl.ds(start, ROWS), :].astype(BF16)


def arrange_left(parts):
    return pl.pallas_call(
        left_kernel,
        in_specs=[pl.BlockSpec(memory_space=pl.ANY)] * len(parts),
        out_specs=[pl.BlockSpec(memory_space=pltpu.VMEM)] * 2,
        out_shape=[
            jax.ShapeDtypeStruct((ROWS * SIDE, TOTAL), BF16),
            jax.ShapeDtypeStruct((ROWS, TOTAL), BF16),
        ],
        scratch_shapes=[
            pltpu.VMEM((TOTAL, LEFT), BF16),
            pltpu.VMEM(((SIDE + 1) * PLANE, TOTAL), F32),
            pltpu.SemaphoreType.DMA((RING,)),
        ],
        compiler_params=pltpu.CompilerParams(vmem_limit_bytes=16 * MEGA),
    )(*parts)


def pair_kernel(block, beside, left, left_mask, weight, *refs):
    parts, (out, right, outer, scale, sem) = refs[:RING], refs[RING:]
    _, _, core, _ = position()

    @pl.when(pl.program_id(0) == 0)
    def _():
        copies = []
        for k, slot in enumerate((0, 1 + 2 * core, 3 - 2 * core, 2)):
            rows = pl.ds(pl.multiple_of(slot * CHIP, CHIP), CHIP)
            copies.append(pltpu.make_async_copy(parts[k], right.at[rows, :], sem.at[k]))
        for copy in copies:
            copy.start()
        for copy in copies:
            copy.wait()
        counts = jnp.dot(left_mask[...], right[:, SIDE * COLS :], preferred_element_type=F32)
        scale[...] = 1.0 / (counts + 0.001)

    value = left[...]
    for q in range(SIDE):
        part = jnp.dot(
            value, right[:, q * COLS : (q + 1) * COLS], preferred_element_type=F32
        ).astype(BF16)
        for i in range(block):
            at = i % beside * COLS
            outer[i // beside, q * SIDE : (q + 1) * SIDE, at : at + COLS] = part[
                i * SIDE : (i + 1) * SIDE
            ]
    first = pl.multiple_of(pl.program_id(0) * block, block)
    scales = scale[pl.ds(first, block), :]
    for i in range(0, block, beside):
        projected = jnp.dot(weight[...], outer[i // beside], preferred_element_type=F32)
        for k in range(beside):
            value = projected[:, k * COLS : (k + 1) * COLS] * scales[i + k : i + k + 1]
            out[i + k] = value.T.astype(BF16)


def pair(left, left_mask, weight, parts):
    block, beside = 8, 2
    whole = lambda a: pl.BlockSpec(a.shape, lambda i: (0,) * a.ndim)
    return pl.pallas_call(
        functools.partial(pair_kernel, block, beside),
        grid=(ROWS // block,),
        in_specs=[
            pl.BlockSpec((block * SIDE, TOTAL), lambda i: (i, 0)),
            whole(left_mask),
            whole(weight),
        ]
        + [pl.BlockSpec(memory_space=pl.ANY)] * len(parts),
        out_specs=pl.BlockSpec((block, COLS, PAIR), lambda i: (i, 0, 0)),
        out_shape=jax.ShapeDtypeStruct((ROWS, COLS, PAIR), BF16),
        scratch_shapes=[
            pltpu.VMEM((TOTAL, RIGHT), BF16),
            pltpu.VMEM((block // beside, SIDE * SIDE, beside * COLS), BF16),
            pltpu.VMEM((ROWS, COLS), F32),
            pltpu.SemaphoreType.DMA((RING,)),
        ],
        compiler_params=pltpu.CompilerParams(vmem_limit_bytes=40 * MEGA),
    )(left, left_mask, weight, *parts)


def local(
    homolog_embedding,
    sequence_row_mask,
    residue_chain_index,
    standardize_factor,
    standardize_shift,
    first_projector_matrix,
    second_projector_matrix,
    output_weight,
):
    own = project(
        homolog_embedding,
        sequence_row_mask,
        residue_chain_index,
        standardize_factor,
        standardize_shift,
        first_projector_matrix,
        second_projector_matrix,
    )
    along_y = [own[0]] + [res_shift(own[d], 0, d, 0) for d in range(1, RING)]
    far = res_shift(own[RING], 2, 0, 0)
    weight = arrange_weight(output_weight)
    along_y[2], weight = lax.optimization_barrier((along_y[2], weight))
    right, left, far_chip = stack(along_y + [core_swap(part) for part in along_y], far, core_swap(far))
    near = both_ways(right, 1, 0)
    left_parts = [to_row_owner(left, k) for k in range(2)]
    far_parts = [both_ways(far_chip, 0, 1), res_shift(far, 0, 2, 0)]
    left_parts, far_parts = lax.optimization_barrier((left_parts, far_parts))
    sides = arrange_left(left_parts + [core_swap(part) for part in left_parts])
    far_right = stack_far(
        far_chip, far_parts[0], core_swap(far_parts[0]), far_parts[1], core_swap(far_parts[1])
    )
    sides, far_right, near = lax.optimization_barrier((sides, far_right, near))
    return pair(*sides, weight, [right, near, core_swap(near), far_right])


def solution(mesh):
    in_specs = (P("res", "col", None), P("res", None), P("col"), P(), P(), P(), P(), P())
    out_specs = P("res", "col", None)
    return jax.shard_map(local, mesh=mesh, in_specs=in_specs, out_specs=out_specs, check_vma=False)
```

time: 71.9 us -> 64.5 us (0.90)
  the two profiles are of different devices: /device:TPU:7 before, /device:TPU:1 now
where the time goes in v3:
time: 64.5 us; the launch traced here: 64.3 us
  Pallas kernels  24.8 us (38%)
  starting transfers between devices  24.4 us (38%)
  waiting for transfers between devices  12.9 us (20%)
  local copies, waits for them, and re-layouts  1.85 us (3%)
    pallas_call x1, Pallas kernels, pair(): pl.pallas_call(functools.partial(pair_kernel, block, beside), grid=(ROWS...  17.8 us
    ppermute x15, starting transfers between devices, res_shift(): return lax.ppermute(value, 'res', pairs)  15.3 us
    ppermute x15, waiting for transfers between devices, res_shift(): return lax.ppermute(value, 'res', pairs)  8.65 us
    ppermute x2, starting transfers between devices, to_row_owner(): return lax.ppermute(value, ('res', 'col'), pairs)  5.2 us
    ppermute x2, waiting for transfers between devices, to_row_owner(): return lax.ppermute(value, ('res', 'col'), pairs)  4.26 us
    ppermute x2, starting transfers between devices, both_ways(): return lax.ppermute(value, 'res', pairs)  3.93 us
    pallas_call x1, Pallas kernels, project(): pl.pallas_call(project_kernel, in_specs=[pl.BlockSpec(memory_space=pltpu....  3.68 us
    pallas_call x1, Pallas kernels, arrange_left(): pl.pallas_call(left_kernel, in_specs=[pl.BlockSpec(memory_space=pl.ANY)]...  1.95 us
  transfers between devices with their start and end apart: 19, of which 6 were waited for; matrix products, arithmetic and copies ran while one was open for 0% of the time, Pallas kernels for 4%

profile of v3, /device:TPU:1, one launch (start us, length us, event | category | flops | bytes accessed | tf_op | source)
XLA Modules:
  0.0 64.3 jit_solution(10059656432055665292)
XLA Ops:
  0.0 3.7 %shard_map.82 = (bf16[4,15872]{1,0:T(4,128)(2,1)}, bf16[4,15872]{1,0:T(4,128)(2,1)}, bf16[4,15872]{1,0:T(4,128)(2,1)}, bf16[4,15872]{1,0:T(4,128)(2,1)}, bf16[4,12672]{1,0:T(4,128)(2,1)}) custom-call(bf16[4,384,256]{2,1,0:T(8,128)(2,1)} %refs_0_.1, bf16[4,8]{1,0:T(4,128)(2,1)} %refs_1_.1, s32[384]{0:T(512)} %refs_2_.1, f32[256]{0:T(256)} %refs_3_.1, ...), custom_call_target="tpu_custom_call" | custom-call | tf_op jit(solution)/shard_map/pallas_call | solution.py:131
  3.7 3.7 %collective-permute-start.1 = (bf16[4,15872]{1,0:T(4,128)(2,1)}, bf16[4,15872]{1,0:T(4,128)(2,1)S(1)}, u32[]{:S(2)}, u32[]{:S(2)}) collective-permute-start(bf16[4,15872]{1,0:T(4,128)(2,1)} %get-tuple-element.27), channel_id=1, source_target_pairs={{0,16},{4,20},{8,24},{12,28},{16,0},{20,4},{24,8},{28,12},{32,48},... | collective-permute-start | bytes 380936 | tf_op jit(solution)/shard_map/ppermute | solution.py:42
  7.4 0.4 collective-permute-start
  7.8 2.3 %collective-permute-start.2 = (bf16[4,15872]{1,0:T(4,128)(2,1)}, bf16[4,15872]{1,0:T(4,128)(2,1)S(1)}, u32[]{:S(2)}, u32[]{:S(2)}) collective-permute-start(bf16[4,15872]{1,0:T(4,128)(2,1)} %get-tuple-element.29), channel_id=1, source_target_pairs={{0,24},{4,28},{8,0},{12,4},{16,8},{20,12},{24,16},{28,20},{32,56},... | collective-permute-start | bytes 380936 | tf_op jit(solution)/shard_map/ppermute | solution.py:42
  10.1 3.6 %collective-permute-start.7 = (bf16[4,12672]{1,0:T(4,128)(2,1)}, bf16[4,12672]{1,0:T(4,128)(2,1)S(1)}, u32[]{:S(2)}, u32[]{:S(2)}) collective-permute-start(bf16[4,12672]{1,0:T(4,128)(2,1)} %get-tuple-element.30), channel_id=1, source_target_pairs={{0,64},{4,68},{8,72},{12,76},{16,80},{20,84},{24,88},{28,92},{32,9... | collective-permute-start | bytes 304136 | tf_op jit(solution)/shard_map/ppermute | solution.py:42
  13.7 1.8 %collective-permute-start.3 = (bf16[4,15872]{1,0:T(4,128)(2,1)}, bf16[4,15872]{1,0:T(4,128)(2,1)S(1)}, u32[]{:S(2)}, u32[]{:S(2)}) collective-permute-start(bf16[4,15872]{1,0:T(4,128)(2,1)} %get-tuple-element.25.refs_0_), channel_id=1, source_target_pairs={{0,4},{4,0},{8,12},{12,8},{16,20},{20,16},{24,28},{28,24},{32,36},... | collective-permute-start | bytes 380936 | tf_op jit(solution)/shard_map/ppermute | solution.py:42
  15.5 0.0 copy-start
  15.5 0.9 %copy-done = bf16[1024,128]{1,0:T(8,128)(2,1)S(1)} copy-done((bf16[1024,128]{1,0:T(8,128)(2,1)S(1)}, bf16[1024,128]{1,0:T(8,128)(2,1)}, u32[]{:S(2)}) %copy-start) | copy-done | bytes 262168
  16.4 0.4 shard_map.83.weight
  16.9 0.0 collective-permute-done.1.refs_2_
  16.9 0.1 collective-permute-start.5
  17.0 0.0 collective-permute-done.refs_1_
  17.0 0.5 collective-permute-start.4
  17.5 0.0 collective-permute-done.2.refs_3_
  17.5 0.1 collective-permute-start.6
  17.6 0.0 collective-permute-done.7.refs_8_
  17.6 0.7 %collective-permute-start.8 = (bf16[4,12672]{1,0:T(4,128)(2,1)S(1)}, bf16[4,12672]{1,0:T(4,128)(2,1)S(1)}, u32[]{:S(2)}, u32[]{:S(2)}) collective-permute-start(bf16[4,12672]{1,0:T(4,128)(2,1)S(1)} %collective-permute-done.7.refs_8_), channel_id=1, source_target_pairs={{0,4},{4,0},{8,12},{12,8},{16,20},{20,16},{24,28},{28,24},{32,36},... | collective-permute-start | bytes 304136 | tf_op jit(solution)/shard_map/ppermute | solution.py:42
  18.3 0.0 collective-permute-done.3.refs_4_
  18.3 0.9 %collective-permute-done.8.refs_9_ = bf16[4,12672]{1,0:T(4,128)(2,1)S(1)} collective-permute-done((bf16[4,12672]{1,0:T(4,128)(2,1)S(1)}, bf16[4,12672]{1,0:T(4,128)(2,1)S(1)}, u32[]{:S(2)}, u32[]{:S(2)}) %collective-permute-start.8) | collective-permute-done | bytes 101408 | tf_op jit(solution)/shard_map/ppermute | solution.py:42
  19.3 0.0 collective-permute-done.4.refs_5_
  19.3 0.0 collective-permute-done.5.refs_6_
  19.3 0.0 collective-permute-done.6.refs_7_
  19.3 0.0 copy-start.1
  19.3 0.9 %copy-done.1 = bf16[4,15872]{1,0:T(4,128)(2,1)S(1)} copy-done((bf16[4,15872]{1,0:T(4,128)(2,1)S(1)}, bf16[4,15872]{1,0:T(4,128)(2,1)}, u32[]{:S(2)}) %copy-start.1) | copy-done | bytes 127000
  20.2 0.6 shard_map.84
  20.8 3.5 %collective-permute-start.17 = (bf16[32,12672]{1,0:T(8,128)(2,1)S(1)}, bf16[32,12672]{1,0:T(8,128)(2,1)S(1)}, u32[]{:S(2)}, u32[]{:S(2)}) collective-permute-start(bf16[32,12672]{1,0:T(8,128)(2,1)S(1)} %get-tuple-element.39.refs_0_), channel_id=1, source_target_pairs={{0,32},{4,100},{8,40},{12,108},{16,48},{20,116},{24,56},{28,124},{... | collective-permute-start | bytes 2433032 | tf_op jit(solution)/shard_map/ppermute | solution.py:56
  24.3 2.5 %collective-permute-start.10 = (bf16[32,3200]{1,0:T(8,128)(2,1)S(1)}, bf16[32,3200]{1,0:T(8,128)(2,1)S(1)}, u32[]{:S(2)}, u32[]{:S(2)}) collective-permute-start(bf16[32,3200]{1,0:T(8,128)(2,1)S(1)} %get-tuple-element.31), channel_id=1, source_target_pairs={{0,1},{1,33},{2,65},{3,97},{4,7},{5,39},{6,71},{7,103},{8,9},{9,41... | collective-permute-start | bytes 614408 | tf_op jit(solution)/shard_map/ppermute | solution.py:68
  26.8 2.7 %collective-permute-start.9 = (bf16[32,3200]{1,0:T(8,128)(2,1)S(1)}, bf16[32,3200]{1,0:T(8,128)(2,1)S(1)}, u32[]{:S(2)}, u32[]{:S(2)}) collective-permute-start(bf16[32,3200]{1,0:T(8,128)(2,1)S(1)} %get-tuple-element.31), channel_id=1, source_target_pairs={{0,0},{1,32},{2,64},{3,96},{4,6},{5,38},{6,70},{7,102},{8,8},{9,40... | collective-permute-start | bytes 614408 | tf_op jit(solution)/shard_map/ppermute | solution.py:68
  29.5 0.5 collective-permute-start.11
  30.0 0.6 collective-permute-start.12
  30.5 4.4 %collective-permute-done.12.far = bf16[4,12672]{1,0:T(4,128)(2,1)S(1)} collective-permute-done((bf16[4,12672]{1,0:T(4,128)(2,1)S(1)}, bf16[4,12672]{1,0:T(4,128)(2,1)S(1)}, u32[]{:S(2)}, u32[]{:S(2)}) %collective-permute-start.12) | collective-permute-done | bytes 101408 | tf_op jit(solution)/shard_map/ppermute | solution.py:42
  35.0 0.0 collective-permute-done.11.near
  35.0 1.7 %collective-permute-done.10.refs_1_ = bf16[32,3200]{1,0:T(8,128)(2,1)S(1)} collective-permute-done((bf16[32,3200]{1,0:T(8,128)(2,1)S(1)}, bf16[32,3200]{1,0:T(8,128)(2,1)S(1)}, u32[]{:S(2)}, u32[]{:S(2)}) %collective-permute-start.10) | collective-permute-done | bytes 204832 | tf_op jit(solution)/shard_map/ppermute | solution.py:68
  36.7 2.5 %collective-permute-done.9.refs_0_ = bf16[32,3200]{1,0:T(8,128)(2,1)S(1)} collective-permute-done((bf16[32,3200]{1,0:T(8,128)(2,1)S(1)}, bf16[32,3200]{1,0:T(8,128)(2,1)S(1)}, u32[]{:S(2)}, u32[]{:S(2)}) %collective-permute-start.9) | collective-permute-done | bytes 204832 | tf_op jit(solution)/shard_map/ppermute | solution.py:68
  39.2 0.0 collective-permute-start.13
  39.2 0.5 collective-permute-start.14
  39.7 0.0 collective-permute-start.15
  39.7 0.5 collective-permute-start.16
  40.2 1.2 %collective-permute-done.16.far_other = bf16[4,12672]{1,0:T(4,128)(2,1)S(1)} collective-permute-done((bf16[4,12672]{1,0:T(4,128)(2,1)S(1)}, bf16[4,12672]{1,0:T(4,128)(2,1)S(1)}, u32[]{:S(2)}, u32[]{:S(2)}) %collective-permute-start.16) | collective-permute-done | bytes 101408 | tf_op jit(solution)/shard_map/ppermute | solution.py:42
  41.4 0.0 collective-permute-done.15.near_other
  41.4 0.4 shard_map.86.refs_3_
  41.8 0.0 collective-permute-done.13.refs_2_
  41.8 0.0 collective-permute-done.14.refs_3_
  41.8 1.9 %shard_map.85 = (bf16[1536,128]{1,0:T(8,128)(2,1)S(1)}, bf16[48,128]{1,0:T(8,128)(2,1)S(1)}) custom-call(bf16[32,3200]{1,0:T(8,128)(2,1)S(1)} %collective-permute-done.9.refs_0_, bf16[32,3200]{1,0:T(8,128)(2,1)S(1)} %collective-permute-done.10.refs_1_, bf16[32,3200]{1,0:T(8,128)(2,1)S(1)} %collective-permute-done.13.refs_2_, ...), custom_call_target="tpu_custom_call" | custom-call | tf_op jit(solution)/shard_map/pallas_call | solution.py:272
  43.8 0.0 collective-permute-done.17.refs_1_
  43.8 0.5 collective-permute-start.18
  44.2 2.1 %collective-permute-done.18.refs_2_ = bf16[32,12672]{1,0:T(8,128)(2,1)S(1)} collective-permute-done((bf16[32,12672]{1,0:T(8,128)(2,1)S(1)}, bf16[32,12672]{1,0:T(8,128)(2,1)S(1)}, u32[]{:S(2)}, u32[]{:S(2)}) %collective-permute-start.18) | collective-permute-done | bytes 811040 | tf_op jit(solution)/shard_map/ppermute | solution.py:42
  46.3 17.8 %shard_map.87 = bf16[48,384,128]{2,1,0:T(8,128)(2,1)} custom-call(bf16[1536,128]{1,0:T(8,128)(2,1)S(1)} %get-tuple-element.40.left, bf16[48,128]{1,0:T(8,128)(2,1)S(1)} %get-tuple-element.41.left_mask, bf16[128,1024]{1,0:T(8,128)(2,1)S(1)} %shard_map.83.weight, bf16[32,12672]{1,0:T(8,128)(2,1)S(1)} %get-tuple-element.39.refs_0_, ...), custom_call_target="tpu_custom_call" | custom-call | tf_op jit(solution)/shard_map/pallas_call | solution.py:328
Async XLA Ops:
  3.7 13.2 %collective-permute-start.1 = (bf16[4,15872]{1,0:T(4,128)(2,1)}, bf16[4,15872]{1,0:T(4,128)(2,1)S(1)}, u32[]{:S(2)}, u32[]{:S(2)}) collective-permute-start(bf16[4,15872]{1,0:T(4,128)(2,1)} %get-tuple-element.27), channel_id=1, source_target_pairs={{0,16},{4,20},{8,24},{12,28},{16,0},{20,4},{24,8},{28,12},{32,48},... | collective-permute-start | bytes 380936 | tf_op jit(solution)/shard_map/ppermute | solution.py:42
  7.4 9.6 %collective-permute-start = (bf16[4,15872]{1,0:T(4,128)(2,1)}, bf16[4,15872]{1,0:T(4,128)(2,1)S(1)}, u32[]{:S(2)}, u32[]{:S(2)}) collective-permute-start(bf16[4,15872]{1,0:T(4,128)(2,1)} %get-tuple-element.26), channel_id=1, source_target_pairs={{0,8},{4,12},{8,16},{12,20},{16,24},{20,28},{24,0},{28,4},{32,40},... | collective-permute-start | bytes 380936 | tf_op jit(solution)/shard_map/ppermute | solution.py:42
  7.8 9.7 %collective-permute-start.2 = (bf16[4,15872]{1,0:T(4,128)(2,1)}, bf16[4,15872]{1,0:T(4,128)(2,1)S(1)}, u32[]{:S(2)}, u32[]{:S(2)}) collective-permute-start(bf16[4,15872]{1,0:T(4,128)(2,1)} %get-tuple-element.29), channel_id=1, source_target_pairs={{0,24},{4,28},{8,0},{12,4},{16,8},{20,12},{24,16},{28,20},{32,56},... | collective-permute-start | bytes 380936 | tf_op jit(solution)/shard_map/ppermute | solution.py:42
  10.1 7.5 %collective-permute-start.7 = (bf16[4,12672]{1,0:T(4,128)(2,1)}, bf16[4,12672]{1,0:T(4,128)(2,1)S(1)}, u32[]{:S(2)}, u32[]{:S(2)}) collective-permute-start(bf16[4,12672]{1,0:T(4,128)(2,1)} %get-tuple-element.30), channel_id=1, source_target_pairs={{0,64},{4,68},{8,72},{12,76},{16,80},{20,84},{24,88},{28,92},{32,9... | collective-permute-start | bytes 304136 | tf_op jit(solution)/shard_map/ppermute | solution.py:42
  13.7 4.6 %collective-permute-start.3 = (bf16[4,15872]{1,0:T(4,128)(2,1)}, bf16[4,15872]{1,0:T(4,128)(2,1)S(1)}, u32[]{:S(2)}, u32[]{:S(2)}) collective-permute-start(bf16[4,15872]{1,0:T(4,128)(2,1)} %get-tuple-element.25.refs_0_), channel_id=1, source_target_pairs={{0,4},{4,0},{8,12},{12,8},{16,20},{20,16},{24,28},{28,24},{32,36},... | collective-permute-start | bytes 380936 | tf_op jit(solution)/shard_map/ppermute | solution.py:42
  15.5 0.9 %copy-start = (bf16[1024,128]{1,0:T(8,128)(2,1)S(1)}, bf16[1024,128]{1,0:T(8,128)(2,1)}, u32[]{:S(2)}) copy-start(bf16[1024,128]{1,0:T(8,128)(2,1)} %weight_hbm.1) | copy-start | bytes 786436
  16.9 2.4 %collective-permute-start.5 = (bf16[4,15872]{1,0:T(4,128)(2,1)S(1)}, bf16[4,15872]{1,0:T(4,128)(2,1)S(1)}, u32[]{:S(2)}, u32[]{:S(2)}) collective-permute-start(bf16[4,15872]{1,0:T(4,128)(2,1)S(1)} %collective-permute-done.1.refs_2_), channel_id=1, source_target_pairs={{0,4},{4,0},{8,12},{12,8},{16,20},{20,16},{24,28},{28,24},{32,36},... | collective-permute-start | bytes 380936 | tf_op jit(solution)/shard_map/ppermute | solution.py:42
  17.0 2.3 %collective-permute-start.4 = (bf16[4,15872]{1,0:T(4,128)(2,1)S(1)}, bf16[4,15872]{1,0:T(4,128)(2,1)S(1)}, u32[]{:S(2)}, u32[]{:S(2)}) collective-permute-start(bf16[4,15872]{1,0:T(4,128)(2,1)S(1)} %collective-permute-done.refs_1_), channel_id=1, source_target_pairs={{0,4},{4,0},{8,12},{12,8},{16,20},{20,16},{24,28},{28,24},{32,36},... | collective-permute-start | bytes 380936 | tf_op jit(solution)/shard_map/ppermute | solution.py:42
  17.5 1.8 %collective-permute-start.6 = (bf16[4,15872]{1,0:T(4,128)(2,1)S(1)}, bf16[4,15872]{1,0:T(4,128)(2,1)S(1)}, u32[]{:S(2)}, u32[]{:S(2)}) collective-permute-start(bf16[4,15872]{1,0:T(4,128)(2,1)S(1)} %collective-permute-done.2.refs_3_), channel_id=1, source_target_pairs={{0,4},{4,0},{8,12},{12,8},{16,20},{20,16},{24,28},{28,24},{32,36},... | collective-permute-start | bytes 380936 | tf_op jit(solution)/shard_map/ppermute | solution.py:42
  17.6 1.7 %collective-permute-start.8 = (bf16[4,12672]{1,0:T(4,128)(2,1)S(1)}, bf16[4,12672]{1,0:T(4,128)(2,1)S(1)}, u32[]{:S(2)}, u32[]{:S(2)}) collective-permute-start(bf16[4,12672]{1,0:T(4,128)(2,1)S(1)} %collective-permute-done.7.refs_8_), channel_id=1, source_target_pairs={{0,4},{4,0},{8,12},{12,8},{16,20},{20,16},{24,28},{28,24},{32,36},... | collective-permute-start | bytes 304136 | tf_op jit(solution)/shard_map/ppermute | solution.py:42
  19.3 0.9 %copy-start.1 = (bf16[4,15872]{1,0:T(4,128)(2,1)S(1)}, bf16[4,15872]{1,0:T(4,128)(2,1)}, u32[]{:S(2)}) copy-start(bf16[4,15872]{1,0:T(4,128)(2,1)} %get-tuple-element.25.refs_0_) | copy-start | bytes 380932
  20.8 22.9 %collective-permute-start.17 = (bf16[32,12672]{1,0:T(8,128)(2,1)S(1)}, bf16[32,12672]{1,0:T(8,128)(2,1)S(1)}, u32[]{:S(2)}, u32[]{:S(2)}) collective-permute-start(bf16[32,12672]{1,0:T(8,128)(2,1)S(1)} %get-tuple-element.39.refs_0_), channel_id=1, source_target_pairs={{0,32},{4,100},{8,40},{12,108},{16,48},{20,116},{24,56},{28,124},{... | collective-permute-start | bytes 2433032 | tf_op jit(solution)/shard_map/ppermute | solution.py:56
  24.3 12.4 %collective-permute-start.10 = (bf16[32,3200]{1,0:T(8,128)(2,1)S(1)}, bf16[32,3200]{1,0:T(8,128)(2,1)S(1)}, u32[]{:S(2)}, u32[]{:S(2)}) collective-permute-start(bf16[32,3200]{1,0:T(8,128)(2,1)S(1)} %get-tuple-element.31), channel_id=1, source_target_pairs={{0,1},{1,33},{2,65},{3,97},{4,7},{5,39},{6,71},{7,103},{8,9},{9,41... | collective-permute-start | bytes 614408 | tf_op jit(solution)/shard_map/ppermute | solution.py:68
  26.8 12.4 %collective-permute-start.9 = (bf16[32,3200]{1,0:T(8,128)(2,1)S(1)}, bf16[32,3200]{1,0:T(8,128)(2,1)S(1)}, u32[]{:S(2)}, u32[]{:S(2)}) collective-permute-start(bf16[32,3200]{1,0:T(8,128)(2,1)S(1)} %get-tuple-element.31), channel_id=1, source_target_pairs={{0,0},{1,32},{2,64},{3,96},{4,6},{5,38},{6,70},{7,102},{8,8},{9,40... | collective-permute-start | bytes 614408 | tf_op jit(solution)/shard_map/ppermute | solution.py:68
  29.5 5.5 %collective-permute-start.11 = (bf16[8,12672]{1,0:T(8,128)(2,1)S(1)}, bf16[8,12672]{1,0:T(8,128)(2,1)S(1)}, u32[]{:S(2)}, u32[]{:S(2)}) collective-permute-start(bf16[8,12672]{1,0:T(8,128)(2,1)S(1)} %get-tuple-element.32.own), channel_id=1, source_target_pairs={{0,8},{4,28},{8,16},{12,4},{16,24},{20,12},{24,0},{28,20},{32,40},... | collective-permute-start | bytes 608264 | tf_op jit(solution)/shard_map/ppermute | solution.py:56
  30.0 5.0 %collective-permute-start.12 = (bf16[4,12672]{1,0:T(4,128)(2,1)S(1)}, bf16[4,12672]{1,0:T(4,128)(2,1)S(1)}, u32[]{:S(2)}, u32[]{:S(2)}) collective-permute-start(bf16[4,12672]{1,0:T(4,128)(2,1)S(1)} %collective-permute-done.7.refs_8_), channel_id=1, source_target_pairs={{0,16},{4,20},{8,24},{12,28},{16,0},{20,4},{24,8},{28,12},{32,48},... | collective-permute-start | bytes 304136 | tf_op jit(solution)/shard_map/ppermute | solution.py:42
  39.2 2.6 %collective-permute-start.13 = (bf16[32,3200]{1,0:T(8,128)(2,1)S(1)}, bf16[32,3200]{1,0:T(8,128)(2,1)S(1)}, u32[]{:S(2)}, u32[]{:S(2)}) collective-permute-start(bf16[32,3200]{1,0:T(8,128)(2,1)S(1)} %collective-permute-done.9.refs_0_), channel_id=1, source_target_pairs={{0,4},{4,0},{8,12},{12,8},{16,20},{20,16},{24,28},{28,24},{32,36},... | collective-permute-start | bytes 614408 | tf_op jit(solution)/shard_map/ppermute | solution.py:42
  39.2 2.6 %collective-permute-start.14 = (bf16[32,3200]{1,0:T(8,128)(2,1)S(1)}, bf16[32,3200]{1,0:T(8,128)(2,1)S(1)}, u32[]{:S(2)}, u32[]{:S(2)}) collective-permute-start(bf16[32,3200]{1,0:T(8,128)(2,1)S(1)} %collective-permute-done.10.refs_1_), channel_id=1, source_target_pairs={{0,4},{4,0},{8,12},{12,8},{16,20},{20,16},{24,28},{28,24},{32,36},... | collective-permute-start | bytes 614408 | tf_op jit(solution)/shard_map/ppermute | solution.py:42
  39.7 1.7 %collective-permute-start.15 = (bf16[8,12672]{1,0:T(8,128)(2,1)S(1)}, bf16[8,12672]{1,0:T(8,128)(2,1)S(1)}, u32[]{:S(2)}, u32[]{:S(2)}) collective-permute-start(bf16[8,12672]{1,0:T(8,128)(2,1)S(1)} %collective-permute-done.11.near), channel_id=1, source_target_pairs={{0,4},{4,0},{8,12},{12,8},{16,20},{20,16},{24,28},{28,24},{32,36},... | collective-permute-start | bytes 608264 | tf_op jit(solution)/shard_map/ppermute | solution.py:42
  39.7 1.7 %collective-permute-start.16 = (bf16[4,12672]{1,0:T(4,128)(2,1)S(1)}, bf16[4,12672]{1,0:T(4,128)(2,1)S(1)}, u32[]{:S(2)}, u32[]{:S(2)}) collective-permute-start(bf16[4,12672]{1,0:T(4,128)(2,1)S(1)} %collective-permute-done.12.far), channel_id=1, source_target_pairs={{0,4},{4,0},{8,12},{12,8},{16,20},{20,16},{24,28},{28,24},{32,36},... | collective-permute-start | bytes 304136 | tf_op jit(solution)/shard_map/ppermute | solution.py:42
  43.8 2.6 %collective-permute-start.18 = (bf16[32,12672]{1,0:T(8,128)(2,1)S(1)}, bf16[32,12672]{1,0:T(8,128)(2,1)S(1)}, u32[]{:S(2)}, u32[]{:S(2)}) collective-permute-start(bf16[32,12672]{1,0:T(8,128)(2,1)S(1)} %collective-permute-done.17.refs_1_), channel_id=1, source_target_pairs={{0,4},{4,0},{8,12},{12,8},{16,20},{20,16},{24,28},{28,24},{32,36},... | collective-permute-start | bytes 2433032 | tf_op jit(solution)/shard_map/ppermute | solution.py:42

commit v4 on v3

--- a/solution.py
+++ b/solution.py
@@ -132,8 +132,8 @@
         project_kernel,
         in_specs=[pl.BlockSpec(memory_space=pltpu.VMEM)] * len(arguments),
         out_specs=[pl.BlockSpec(memory_space=pltpu.VMEM)] * (RING + 1),
-        out_shape=[jax.ShapeDtypeStruct((SEQS, RIGHT + LEFT), BF16)] * RING
-        + [jax.ShapeDtypeStruct((SEQS, RIGHT), BF16)],
+        out_shape=[pltpu.VMEM((SEQS, RIGHT + LEFT), BF16)] * RING
+        + [pltpu.VMEM((SEQS, RIGHT), BF16)],
         scratch_shapes=[
             pltpu.VMEM((2 * SIDE, EMBED), BF16),
             pltpu.VMEM((SEQS, SIDE, COLS), F32),
@@ -373,12 +373,12 @@
     near = both_ways(right, 1, 0)
     left_parts = [to_row_owner(left, k) for k in range(2)]
     far_parts = [both_ways(far_chip, 0, 1), res_shift(far, 0, 2, 0)]
-    left_parts, far_parts = lax.optimization_barrier((left_parts, far_parts))
+    left_parts, far_parts, near = lax.optimization_barrier((left_parts, far_parts, near))
     sides = arrange_left(left_parts + [core_swap(part) for part in left_parts])
+    sides, far_chip = lax.optimization_barrier((sides, far_chip))
     far_right = stack_far(
         far_chip, far_parts[0], core_swap(far_parts[0]), far_parts[1], core_swap(far_parts[1])
     )
-    sides, far_right, near = lax.optimization_barrier((sides, far_right, near))
     return pair(*sides, weight, [right, near, core_swap(near), far_right])
 
 

time: 64.5 us -> 60.9 us (0.944)
  waiting for transfers between devices: 12.9 us -> 11.5 us
  local copies, waits for them, and re-layouts: 1.85 us -> 0.95 us
  Pallas kernels: 24.8 us -> 24.1 us
    ppermute x15, waiting for transfers between devices: 8.65 us -> 7.26 us  [res_shift(): return lax.ppermute(value, 'res', pairs)]
    unnamed x4 -> x2, local copies, waits for them, and re-layouts: 1.85 us -> 0.95 us
    pallas_call x1, Pallas kernels: 3.68 us -> 2.98 us  [project(): pl.pallas_call(project_kernel, in_specs=[pl.BlockSpec(memory_space=pltpu....]
where the time goes in v4:
time: 60.9 us; the launch traced here: 60.7 us
  Pallas kernels  24.1 us (40%)
  starting transfers between devices  23.8 us (39%)
  waiting for transfers between devices  11.5 us (19%)
  local copies, waits for them, and re-layouts  0.95 us (2%)
    pallas_call x1, Pallas kernels, pair(): pl.pallas_call(functools.partial(pair_kernel, block, beside), grid=(ROWS...  17.8 us
    ppermute x15, starting transfers between devices, res_shift(): return lax.ppermute(value, 'res', pairs)  14.7 us
    ppermute x15, waiting for transfers between devices, res_shift(): return lax.ppermute(value, 'res', pairs)  7.26 us
    ppermute x2, starting transfers between devices, to_row_owner(): return lax.ppermute(value, ('res', 'col'), pairs)  5.2 us
    ppermute x2, waiting for transfers between devices, to_row_owner(): return lax.ppermute(value, ('res', 'col'), pairs)  4.27 us
    ppermute x2, starting transfers between devices, both_ways(): return lax.ppermute(value, 'res', pairs)  3.93 us
    pallas_call x1, Pallas kernels, project(): pl.pallas_call(project_kernel, in_specs=[pl.BlockSpec(memory_space=pltpu....  2.98 us
    pallas_call x1, Pallas kernels, arrange_left(): pl.pallas_call(left_kernel, in_specs=[pl.BlockSpec(memory_space=pl.ANY)]...  1.89 us
  transfers between devices with their start and end apart: 19, of which 6 were waited for; matrix products, arithmetic and copies ran while one was open for 0% of the time, Pallas kernels for 4%

profile of v4, /device:TPU:1, one launch (start us, length us, event | category | flops | bytes accessed | tf_op | source)
XLA Modules:
  0.0 60.7 jit_solution(10908116630012290140)
XLA Ops:
  0.0 3.0 %shard_map.82 = (bf16[4,15872]{1,0:T(4,128)(2,1)S(1)}, bf16[4,15872]{1,0:T(4,128)(2,1)S(1)}, bf16[4,15872]{1,0:T(4,128)(2,1)S(1)}, bf16[4,15872]{1,0:T(4,128)(2,1)S(1)}, bf16[4,12672]{1,0:T(4,128)(2,1)S(1)}) custom-call(bf16[4,384,256]{2,1,0:T(8,128)(2,1)} %refs_0_.1, bf16[4,8]{1,0:T(4,128)(2,1)} %refs_1_.1, s32[384]{0:T(512)} %refs_2_.1, f32[256]{0:T(256)} %refs_3_.1, ...), custom_call_target="tpu_custom_call" | custom-call | tf_op jit(solution)/shard_map/pallas_call | solution.py:131
  3.0 3.8 %collective-permute-start.1 = (bf16[4,15872]{1,0:T(4,128)(2,1)S(1)}, bf16[4,15872]{1,0:T(4,128)(2,1)S(1)}, u32[]{:S(2)}, u32[]{:S(2)}) collective-permute-start(bf16[4,15872]{1,0:T(4,128)(2,1)S(1)} %get-tuple-element.27), channel_id=1, source_target_pairs={{0,16},{4,20},{8,24},{12,28},{16,0},{20,4},{24,8},{28,12},{32,48},... | collective-permute-start | bytes 380936 | tf_op jit(solution)/shard_map/ppermute | solution.py:42
  6.8 0.4 collective-permute-start
  7.2 2.3 %collective-permute-start.2 = (bf16[4,15872]{1,0:T(4,128)(2,1)S(1)}, bf16[4,15872]{1,0:T(4,128)(2,1)S(1)}, u32[]{:S(2)}, u32[]{:S(2)}) collective-permute-start(bf16[4,15872]{1,0:T(4,128)(2,1)S(1)} %get-tuple-element.29), channel_id=1, source_target_pairs={{0,24},{4,28},{8,0},{12,4},{16,8},{20,12},{24,16},{28,20},{32,56},... | collective-permute-start | bytes 380936 | tf_op jit(solution)/shard_map/ppermute | solution.py:42
  9.5 3.6 %collective-permute-start.7 = (bf16[4,12672]{1,0:T(4,128)(2,1)S(1)}, bf16[4,12672]{1,0:T(4,128)(2,1)S(1)}, u32[]{:S(2)}, u32[]{:S(2)}) collective-permute-start(bf16[4,12672]{1,0:T(4,128)(2,1)S(1)} %get-tuple-element.30), channel_id=1, source_target_pairs={{0,64},{4,68},{8,72},{12,76},{16,80},{20,84},{24,88},{28,92},{32,9... | collective-permute-start | bytes 304136 | tf_op jit(solution)/shard_map/ppermute | solution.py:42
  13.1 1.8 %collective-permute-start.3 = (bf16[4,15872]{1,0:T(4,128)(2,1)S(1)}, bf16[4,15872]{1,0:T(4,128)(2,1)S(1)}, u32[]{:S(2)}, u32[]{:S(2)}) collective-permute-start(bf16[4,15872]{1,0:T(4,128)(2,1)S(1)} %get-tuple-element.25.refs_0_), channel_id=1, source_target_pairs={{0,4},{4,0},{8,12},{12,8},{16,20},{20,16},{24,28},{28,24},{32,36},... | collective-permute-start | bytes 380936 | tf_op jit(solution)/shard_map/ppermute | solution.py:42
  14.9 0.0 copy-start
  14.9 0.9 %copy-done = bf16[1024,128]{1,0:T(8,128)(2,1)S(1)} copy-done((bf16[1024,128]{1,0:T(8,128)(2,1)S(1)}, bf16[1024,128]{1,0:T(8,128)(2,1)}, u32[]{:S(2)}) %copy-start) | copy-done | bytes 262168
  15.8 0.4 shard_map.83.weight
  16.3 0.0 collective-permute-done.1.refs_2_
  16.3 0.1 collective-permute-start.5
  16.4 0.0 collective-permute-done.refs_1_
  16.4 0.5 collective-permute-start.4
  16.9 0.0 collective-permute-done.2.refs_3_
  16.9 0.1 collective-permute-start.6
  17.0 0.0 collective-permute-done.7.refs_8_
  17.0 0.5 collective-permute-start.8
  17.5 0.0 collective-permute-done.3.refs_4_
  17.5 0.9 %collective-permute-done.8.refs_9_ = bf16[4,12672]{1,0:T(4,128)(2,1)S(1)} collective-permute-done((bf16[4,12672]{1,0:T(4,128)(2,1)S(1)}, bf16[4,12672]{1,0:T(4,128)(2,1)S(1)}, u32[]{:S(2)}, u32[]{:S(2)}) %collective-permute-start.8) | collective-permute-done | bytes 101408 | tf_op jit(solution)/shard_map/ppermute | solution.py:42
  18.5 0.0 collective-permute-done.4.refs_5_
  18.5 0.0 collective-permute-done.5.refs_6_
  18.5 0.0 collective-permute-done.6.refs_7_
  18.5 0.6 %shard_map.84 = (bf16[32,12672]{1,0:T(8,128)(2,1)S(1)}, bf16[32,3200]{1,0:T(8,128)(2,1)S(1)}, bf16[8,12672]{1,0:T(8,128)(2,1)S(1)}) custom-call(bf16[4,15872]{1,0:T(4,128)(2,1)S(1)} %get-tuple-element.25.refs_0_, bf16[4,15872]{1,0:T(4,128)(2,1)S(1)} %collective-permute-done.refs_1_, bf16[4,15872]{1,0:T(4,128)(2,1)S(1)} %collective-permute-done.1.refs_2_, ...), custom_call_target="tpu_custom_call" | custom-call | tf_op jit(solution)/shard_map/pallas_call | solution.py:200
  19.1 3.5 %collective-permute-start.13 = (bf16[32,12672]{1,0:T(8,128)(2,1)S(1)}, bf16[32,12672]{1,0:T(8,128)(2,1)S(1)}, u32[]{:S(2)}, u32[]{:S(2)}) collective-permute-start(bf16[32,12672]{1,0:T(8,128)(2,1)S(1)} %get-tuple-element.33.refs_0_), channel_id=1, source_target_pairs={{0,32},{4,100},{8,40},{12,108},{16,48},{20,116},{24,56},{28,124},{... | collective-permute-start | bytes 2433032 | tf_op jit(solution)/shard_map/ppermute | solution.py:56
  22.6 2.5 %collective-permute-start.10 = (bf16[32,3200]{1,0:T(8,128)(2,1)S(1)}, bf16[32,3200]{1,0:T(8,128)(2,1)S(1)}, u32[]{:S(2)}, u32[]{:S(2)}) collective-permute-start(bf16[32,3200]{1,0:T(8,128)(2,1)S(1)} %get-tuple-element.31), channel_id=1, source_target_pairs={{0,1},{1,33},{2,65},{3,97},{4,7},{5,39},{6,71},{7,103},{8,9},{9,41... | collective-permute-start | bytes 614408 | tf_op jit(solution)/shard_map/ppermute | solution.py:68
  25.1 2.7 %collective-permute-start.9 = (bf16[32,3200]{1,0:T(8,128)(2,1)S(1)}, bf16[32,3200]{1,0:T(8,128)(2,1)S(1)}, u32[]{:S(2)}, u32[]{:S(2)}) collective-permute-start(bf16[32,3200]{1,0:T(8,128)(2,1)S(1)} %get-tuple-element.31), channel_id=1, source_target_pairs={{0,0},{1,32},{2,64},{3,96},{4,6},{5,38},{6,70},{7,102},{8,8},{9,40... | collective-permute-start | bytes 614408 | tf_op jit(solution)/shard_map/ppermute | solution.py:68
  27.8 0.4 collective-permute-start.11
  28.2 0.6 collective-permute-start.12
  28.8 4.4 %collective-permute-done.12.far = bf16[4,12672]{1,0:T(4,128)(2,1)S(1)} collective-permute-done((bf16[4,12672]{1,0:T(4,128)(2,1)S(1)}, bf16[4,12672]{1,0:T(4,128)(2,1)S(1)}, u32[]{:S(2)}, u32[]{:S(2)}) %collective-permute-start.12) | collective-permute-done | bytes 101408 | tf_op jit(solution)/shard_map/ppermute | solution.py:42
  33.2 0.0 collective-permute-done.11.near
  33.2 1.7 %collective-permute-done.10.refs_1_ = bf16[32,3200]{1,0:T(8,128)(2,1)S(1)} collective-permute-done((bf16[32,3200]{1,0:T(8,128)(2,1)S(1)}, bf16[32,3200]{1,0:T(8,128)(2,1)S(1)}, u32[]{:S(2)}, u32[]{:S(2)}) %collective-permute-start.10) | collective-permute-done | bytes 204832 | tf_op jit(solution)/shard_map/ppermute | solution.py:68
  35.0 2.5 %collective-permute-done.9.refs_0_ = bf16[32,3200]{1,0:T(8,128)(2,1)S(1)} collective-permute-done((bf16[32,3200]{1,0:T(8,128)(2,1)S(1)}, bf16[32,3200]{1,0:T(8,128)(2,1)S(1)}, u32[]{:S(2)}, u32[]{:S(2)}) %collective-permute-start.9) | collective-permute-done | bytes 204832 | tf_op jit(solution)/shard_map/ppermute | solution.py:68
  37.5 0.0 collective-permute-done.13.refs_1_
  37.5 0.0 collective-permute-start.16
  37.5 0.5 collective-permute-start.14
  38.0 0.0 collective-permute-start.15
  38.0 0.5 collective-permute-start.17
  38.5 0.0 collective-permute-start.18
  38.5 1.6 %collective-permute-done.14.refs_2_ = bf16[32,3200]{1,0:T(8,128)(2,1)S(1)} collective-permute-done((bf16[32,3200]{1,0:T(8,128)(2,1)S(1)}, bf16[32,3200]{1,0:T(8,128)(2,1)S(1)}, u32[]{:S(2)}, u32[]{:S(2)}) %collective-permute-start.14) | collective-permute-done | bytes 204832 | tf_op jit(solution)/shard_map/ppermute | solution.py:42
  40.1 0.3 collective-permute-done.15.refs_3_
  40.4 1.9 %shard_map.85 = (bf16[1536,128]{1,0:T(8,128)(2,1)S(1)}, bf16[48,128]{1,0:T(8,128)(2,1)S(1)}) custom-call(bf16[32,3200]{1,0:T(8,128)(2,1)S(1)} %collective-permute-done.9.refs_0_, bf16[32,3200]{1,0:T(8,128)(2,1)S(1)} %collective-permute-done.10.refs_1_, bf16[32,3200]{1,0:T(8,128)(2,1)S(1)} %collective-permute-done.14.refs_2_, ...), custom_call_target="tpu_custom_call" | custom-call | tf_op jit(solution)/shard_map/pallas_call | solution.py:272
  42.3 0.0 collective-permute-done.18.far_other
  42.3 0.0 collective-permute-done.17.near_other
  42.3 0.4 shard_map.86.refs_3_
  42.7 0.0 collective-permute-done.16.refs_2_
  42.7 17.8 %shard_map.87 = bf16[48,384,128]{2,1,0:T(8,128)(2,1)} custom-call(bf16[1536,128]{1,0:T(8,128)(2,1)S(1)} %get-tuple-element.38.left, bf16[48,128]{1,0:T(8,128)(2,1)S(1)} %get-tuple-element.39.left_mask, bf16[128,1024]{1,0:T(8,128)(2,1)S(1)} %shard_map.83.weight, bf16[32,12672]{1,0:T(8,128)(2,1)S(1)} %get-tuple-element.33.refs_0_, ...), custom_call_target="tpu_custom_call" | custom-call | tf_op jit(solution)/shard_map/pallas_call | solution.py:328
Async XLA Ops:
  3.0 13.3 %collective-permute-start.1 = (bf16[4,15872]{1,0:T(4,128)(2,1)S(1)}, bf16[4,15872]{1,0:T(4,128)(2,1)S(1)}, u32[]{:S(2)}, u32[]{:S(2)}) collective-permute-start(bf16[4,15872]{1,0:T(4,128)(2,1)S(1)} %get-tuple-element.27), channel_id=1, source_target_pairs={{0,16},{4,20},{8,24},{12,28},{16,0},{20,4},{24,8},{28,12},{32,48},... | collective-permute-start | bytes 380936 | tf_op jit(solution)/shard_map/ppermute | solution.py:42
  6.8 9.6 %collective-permute-start = (bf16[4,15872]{1,0:T(4,128)(2,1)S(1)}, bf16[4,15872]{1,0:T(4,128)(2,1)S(1)}, u32[]{:S(2)}, u32[]{:S(2)}) collective-permute-start(bf16[4,15872]{1,0:T(4,128)(2,1)S(1)} %get-tuple-element.26), channel_id=1, source_target_pairs={{0,8},{4,12},{8,16},{12,20},{16,24},{20,28},{24,0},{28,4},{32,40},... | collective-permute-start | bytes 380936 | tf_op jit(solution)/shard_map/ppermute | solution.py:42
  7.2 9.7 %collective-permute-start.2 = (bf16[4,15872]{1,0:T(4,128)(2,1)S(1)}, bf16[4,15872]{1,0:T(4,128)(2,1)S(1)}, u32[]{:S(2)}, u32[]{:S(2)}) collective-permute-start(bf16[4,15872]{1,0:T(4,128)(2,1)S(1)} %get-tuple-element.29), channel_id=1, source_target_pairs={{0,24},{4,28},{8,0},{12,4},{16,8},{20,12},{24,16},{28,20},{32,56},... | collective-permute-start | bytes 380936 | tf_op jit(solution)/shard_map/ppermute | solution.py:42
  9.5 7.5 %collective-permute-start.7 = (bf16[4,12672]{1,0:T(4,128)(2,1)S(1)}, bf16[4,12672]{1,0:T(4,128)(2,1)S(1)}, u32[]{:S(2)}, u32[]{:S(2)}) collective-permute-start(bf16[4,12672]{1,0:T(4,128)(2,1)S(1)} %get-tuple-element.30), channel_id=1, source_target_pairs={{0,64},{4,68},{8,72},{12,76},{16,80},{20,84},{24,88},{28,92},{32,9... | collective-permute-start | bytes 304136 | tf_op jit(solution)/shard_map/ppermute | solution.py:42
  13.1 4.4 %collective-permute-start.3 = (bf16[4,15872]{1,0:T(4,128)(2,1)S(1)}, bf16[4,15872]{1,0:T(4,128)(2,1)S(1)}, u32[]{:S(2)}, u32[]{:S(2)}) collective-permute-start(bf16[4,15872]{1,0:T(4,128)(2,1)S(1)} %get-tuple-element.25.refs_0_), channel_id=1, source_target_pairs={{0,4},{4,0},{8,12},{12,8},{16,20},{20,16},{24,28},{28,24},{32,36},... | collective-permute-start | bytes 380936 | tf_op jit(solution)/shard_map/ppermute | solution.py:42
  14.9 0.9 %copy-start = (bf16[1024,128]{1,0:T(8,128)(2,1)S(1)}, bf16[1024,128]{1,0:T(8,128)(2,1)}, u32[]{:S(2)}) copy-start(bf16[1024,128]{1,0:T(8,128)(2,1)} %weight_hbm.1) | copy-start | bytes 786436
  16.3 2.2 %collective-permute-start.5 = (bf16[4,15872]{1,0:T(4,128)(2,1)S(1)}, bf16[4,15872]{1,0:T(4,128)(2,1)S(1)}, u32[]{:S(2)}, u32[]{:S(2)}) collective-permute-start(bf16[4,15872]{1,0:T(4,128)(2,1)S(1)} %collective-permute-done.1.refs_2_), channel_id=1, source_target_pairs={{0,4},{4,0},{8,12},{12,8},{16,20},{20,16},{24,28},{28,24},{32,36},... | collective-permute-start | bytes 380936 | tf_op jit(solution)/shard_map/ppermute | solution.py:42
  16.4 2.1 %collective-permute-start.4 = (bf16[4,15872]{1,0:T(4,128)(2,1)S(1)}, bf16[4,15872]{1,0:T(4,128)(2,1)S(1)}, u32[]{:S(2)}, u32[]{:S(2)}) collective-permute-start(bf16[4,15872]{1,0:T(4,128)(2,1)S(1)} %collective-permute-done.refs_1_), channel_id=1, source_target_pairs={{0,4},{4,0},{8,12},{12,8},{16,20},{20,16},{24,28},{28,24},{32,36},... | collective-permute-start | bytes 380936 | tf_op jit(solution)/shard_map/ppermute | solution.py:42
  16.9 1.6 %collective-permute-start.6 = (bf16[4,15872]{1,0:T(4,128)(2,1)S(1)}, bf16[4,15872]{1,0:T(4,128)(2,1)S(1)}, u32[]{:S(2)}, u32[]{:S(2)}) collective-permute-start(bf16[4,15872]{1,0:T(4,128)(2,1)S(1)} %collective-permute-done.2.refs_3_), channel_id=1, source_target_pairs={{0,4},{4,0},{8,12},{12,8},{16,20},{20,16},{24,28},{28,24},{32,36},... | collective-permute-start | bytes 380936 | tf_op jit(solution)/shard_map/ppermute | solution.py:42
  17.0 1.5 %collective-permute-start.8 = (bf16[4,12672]{1,0:T(4,128)(2,1)S(1)}, bf16[4,12672]{1,0:T(4,128)(2,1)S(1)}, u32[]{:S(2)}, u32[]{:S(2)}) collective-permute-start(bf16[4,12672]{1,0:T(4,128)(2,1)S(1)} %collective-permute-done.7.refs_8_), channel_id=1, source_target_pairs={{0,4},{4,0},{8,12},{12,8},{16,20},{20,16},{24,28},{28,24},{32,36},... | collective-permute-start | bytes 304136 | tf_op jit(solution)/shard_map/ppermute | solution.py:42
  19.1 18.4 %collective-permute-start.13 = (bf16[32,12672]{1,0:T(8,128)(2,1)S(1)}, bf16[32,12672]{1,0:T(8,128)(2,1)S(1)}, u32[]{:S(2)}, u32[]{:S(2)}) collective-permute-start(bf16[32,12672]{1,0:T(8,128)(2,1)S(1)} %get-tuple-element.33.refs_0_), channel_id=1, source_target_pairs={{0,32},{4,100},{8,40},{12,108},{16,48},{20,116},{24,56},{28,124},{... | collective-permute-start | bytes 2433032 | tf_op jit(solution)/shard_map/ppermute | solution.py:56
  22.6 12.4 %collective-permute-start.10 = (bf16[32,3200]{1,0:T(8,128)(2,1)S(1)}, bf16[32,3200]{1,0:T(8,128)(2,1)S(1)}, u32[]{:S(2)}, u32[]{:S(2)}) collective-permute-start(bf16[32,3200]{1,0:T(8,128)(2,1)S(1)} %get-tuple-element.31), channel_id=1, source_target_pairs={{0,1},{1,33},{2,65},{3,97},{4,7},{5,39},{6,71},{7,103},{8,9},{9,41... | collective-permute-start | bytes 614408 | tf_op jit(solution)/shard_map/ppermute | solution.py:68
  25.1 12.4 %collective-permute-start.9 = (bf16[32,3200]{1,0:T(8,128)(2,1)S(1)}, bf16[32,3200]{1,0:T(8,128)(2,1)S(1)}, u32[]{:S(2)}, u32[]{:S(2)}) collective-permute-start(bf16[32,3200]{1,0:T(8,128)(2,1)S(1)} %get-tuple-element.31), channel_id=1, source_target_pairs={{0,0},{1,32},{2,64},{3,96},{4,6},{5,38},{6,70},{7,102},{8,8},{9,40... | collective-permute-start | bytes 614408 | tf_op jit(solution)/shard_map/ppermute | solution.py:68
  27.8 5.5 %collective-permute-start.11 = (bf16[8,12672]{1,0:T(8,128)(2,1)S(1)}, bf16[8,12672]{1,0:T(8,128)(2,1)S(1)}, u32[]{:S(2)}, u32[]{:S(2)}) collective-permute-start(bf16[8,12672]{1,0:T(8,128)(2,1)S(1)} %get-tuple-element.42.own), channel_id=1, source_target_pairs={{0,8},{4,28},{8,16},{12,4},{16,24},{20,12},{24,0},{28,20},{32,40},... | collective-permute-start | bytes 608264 | tf_op jit(solution)/shard_map/ppermute | solution.py:56
  28.2 5.0 %collective-permute-start.12 = (bf16[4,12672]{1,0:T(4,128)(2,1)S(1)}, bf16[4,12672]{1,0:T(4,128)(2,1)S(1)}, u32[]{:S(2)}, u32[]{:S(2)}) collective-permute-start(bf16[4,12672]{1,0:T(4,128)(2,1)S(1)} %collective-permute-done.7.refs_8_), channel_id=1, source_target_pairs={{0,16},{4,20},{8,24},{12,28},{16,0},{20,4},{24,8},{28,12},{32,48},... | collective-permute-start | bytes 304136 | tf_op jit(solution)/shard_map/ppermute | solution.py:42
  37.5 5.2 %collective-permute-start.16 = (bf16[32,12672]{1,0:T(8,128)(2,1)S(1)}, bf16[32,12672]{1,0:T(8,128)(2,1)S(1)}, u32[]{:S(2)}, u32[]{:S(2)}) collective-permute-start(bf16[32,12672]{1,0:T(8,128)(2,1)S(1)} %collective-permute-done.13.refs_1_), channel_id=1, source_target_pairs={{0,4},{4,0},{8,12},{12,8},{16,20},{20,16},{24,28},{28,24},{32,36},... | collective-permute-start | bytes 2433032 | tf_op jit(solution)/shard_map/ppermute | solution.py:42
  37.5 2.6 %collective-permute-start.14 = (bf16[32,3200]{1,0:T(8,128)(2,1)S(1)}, bf16[32,3200]{1,0:T(8,128)(2,1)S(1)}, u32[]{:S(2)}, u32[]{:S(2)}) collective-permute-start(bf16[32,3200]{1,0:T(8,128)(2,1)S(1)} %collective-permute-done.9.refs_0_), channel_id=1, source_target_pairs={{0,4},{4,0},{8,12},{12,8},{16,20},{20,16},{24,28},{28,24},{32,36},... | collective-permute-start | bytes 614408 | tf_op jit(solution)/shard_map/ppermute | solution.py:42
  38.0 2.4 %collective-permute-start.15 = (bf16[32,3200]{1,0:T(8,128)(2,1)S(1)}, bf16[32,3200]{1,0:T(8,128)(2,1)S(1)}, u32[]{:S(2)}, u32[]{:S(2)}) collective-permute-start(bf16[32,3200]{1,0:T(8,128)(2,1)S(1)} %collective-permute-done.10.refs_1_), channel_id=1, source_target_pairs={{0,4},{4,0},{8,12},{12,8},{16,20},{20,16},{24,28},{28,24},{32,36},... | collective-permute-start | bytes 614408 | tf_op jit(solution)/shard_map/ppermute | solution.py:42
  38.0 4.3 %collective-permute-start.17 = (bf16[8,12672]{1,0:T(8,128)(2,1)S(1)}, bf16[8,12672]{1,0:T(8,128)(2,1)S(1)}, u32[]{:S(2)}, u32[]{:S(2)}) collective-permute-start(bf16[8,12672]{1,0:T(8,128)(2,1)S(1)} %collective-permute-done.11.near), channel_id=1, source_target_pairs={{0,4},{4,0},{8,12},{12,8},{16,20},{20,16},{24,28},{28,24},{32,36},... | collective-permute-start | bytes 608264 | tf_op jit(solution)/shard_map/ppermute | solution.py:42
  38.5 3.8 %collective-permute-start.18 = (bf16[4,12672]{1,0:T(4,128)(2,1)S(1)}, bf16[4,12672]{1,0:T(4,128)(2,1)S(1)}, u32[]{:S(2)}, u32[]{:S(2)}) collective-permute-start(bf16[4,12672]{1,0:T(4,128)(2,1)S(1)} %collective-permute-done.12.far), channel_id=1, source_target_pairs={{0,4},{4,0},{8,12},{12,8},{16,20},{20,16},{24,28},{28,24},{32,36},... | collective-permute-start | bytes 304136 | tf_op jit(solution)/shard_map/ppermute | solution.py:42

commit v5 on v4

--- a/solution.py
+++ b/solution.py
@@ -177,9 +177,9 @@
 
 
 def stack_kernel(*refs):
-    parts, (far, far_other, right, left, far_chip, wide) = refs[: RING * CORES], refs[RING * CORES :]
+    parts, (right, left, wide) = refs[: RING * CORES], refs[RING * CORES :]
     _, _, core, _ = position()
-    for out, base in ((right, 0), (left, RIGHT)):
+    for out, base in ((left, RIGHT), (right, 0)):
         for at, width in chunks(out.shape[1]):
             lanes = slice(base + at, base + at + width)
             for c in range(CORES):
@@ -188,29 +188,46 @@
                 for d in range(RING):
                     half[d * SEQS : (d + 1) * SEQS, :width] = parts[c * RING + d][:, lanes].astype(F32)
             out[:, at : at + width] = wide[:, :width].astype(BF16)
+
+
+def stack(parts):
+    return pl.pallas_call(
+        stack_kernel,
+        out_shape=[
+            jax.ShapeDtypeStruct((CHIP, RIGHT), BF16),
+            jax.ShapeDtypeStruct((CHIP, LEFT), BF16),
+        ],
+        scratch_shapes=[pltpu.VMEM((CHIP, 2 * COLS), F32)],
+        compiler_params=pltpu.CompilerParams(vmem_limit_bytes=16 * MEGA),
+    )(*parts)
+
+
+def chip_kernel(far, far_other, after, out, wide):
+    _, _, core, _ = position()
     for at, width in chunks(RIGHT):
         lanes = slice(at, at + width)
         values = by_core(core, far[:, lanes].astype(F32), far_other[:, lanes].astype(F32))
         for c in range(CORES):
             wide[c * SEQS : (c + 1) * SEQS, :width] = values[c]
-        far_chip[:, lanes] = wide[: CORES * SEQS, :width].astype(BF16)
-
-
-def stack(parts, far, far_other):
-    return pl.pallas_call(
-        stack_kernel,
-        out_shape=[
-            jax.ShapeDtypeStruct((CHIP, RIGHT), BF16),
-            jax.ShapeDtypeStruct((CHIP, LEFT), BF16),
-            jax.ShapeDtypeStruct((CORES * SEQS, RIGHT), BF16),
-        ],
-        scratch_shapes=[pltpu.VMEM((CHIP, 2 * COLS), F32)],
+        out[:, lanes] = wide[:, :width].astype(BF16)
+
+
+def stack_chip(far, far_other, after):
+    vmem = pl.BlockSpec(memory_space=pltpu.VMEM)
+    return pl.pallas_call(
+        chip_kernel,
+        in_specs=[vmem, vmem, pl.BlockSpec(memory_space=pl.ANY)],
+        out_specs=vmem,
+        out_shape=jax.ShapeDtypeStruct((CORES * SEQS, RIGHT), BF16),
+        scratch_shapes=[pltpu.VMEM((CORES * SEQS, 2 * COLS), F32)],
         compiler_params=pltpu.CompilerParams(vmem_limit_bytes=16 * MEGA),
-    )(*parts, far, far_other)
-
-
-def far_kernel(own, near, near_other, far, far_other, out, wide):
+    )(far, far_other, after)
+
+
+def far_kernel(own, near, near_other, far, far_other, right_part, _, right, wide, sem):
     _, _, core, _ = position()
+    copy = pltpu.make_async_copy(right_part, right.at[rows_of(3 - 2 * core), :], sem)
+    copy.start()
     for at, width in chunks(RIGHT):
         lanes = slice(at, at + width)
         below, above = by_core(core, near[:, lanes].astype(F32), near_other[:, lanes].astype(F32))
@@ -221,30 +238,39 @@
             for d, value in enumerate((here[rows], below[rows], opposite[c], above[rows])):
                 start = c * GROUP + d * SEQS
                 wide[start : start + SEQS, :width] = value
-        out[:, lanes] = wide[:, :width].astype(BF16)
-
-
-def stack_far(*parts):
+        right[2 * CHIP : 3 * CHIP, lanes] = wide[:, :width].astype(BF16)
+    copy.wait()
+
+
+def finish_right(parts, right_part, right):
+    vmem, anywhere = (pl.BlockSpec(memory_space=m) for m in (pltpu.VMEM, pl.ANY))
     return pl.pallas_call(
         far_kernel,
-        out_shape=jax.ShapeDtypeStruct((CHIP, RIGHT), BF16),
-        scratch_shapes=[pltpu.VMEM((CHIP, 2 * COLS), F32)],
+        in_specs=[vmem] * len(parts) + [anywhere, vmem],
+        out_specs=vmem,
+        out_shape=pltpu.VMEM((TOTAL, RIGHT), BF16),
+        input_output_aliases={len(parts) + 1: 0},
+        scratch_shapes=[pltpu.VMEM((CHIP, 2 * COLS), F32), pltpu.SemaphoreType.DMA],
         compiler_params=pltpu.CompilerParams(vmem_limit_bytes=16 * MEGA),
-    )(*parts)
+    )(*parts, right_part, right)
+
+
+def rows_of(slot):
+    return pl.ds(pl.multiple_of(slot * CHIP, CHIP), CHIP)
 
 
 def left_kernel(*refs):
-    parts, (out, out_mask, stacked, turned, sem) = refs[:RING], refs[RING:]
+    parts, (own, near, out, out_mask, right, stacked, turned, sem) = refs[:RING], refs[RING:]
     z, _, core, x = position()
-    copies = []
+    copies = [
+        pltpu.make_async_copy(part, right.at[rows_of(slot), :], sem.at[k])
+        for k, (part, slot) in enumerate(((own, 0), (near, 1 + 2 * core)))
+    ]
+    for copy in copies:
+        copy.start()
     for at, part in enumerate(parts):
         group = lax.rem(z - x + at + 2 * core + RING, RING)
-        start = pl.multiple_of(group * CHIP, CHIP)
-        copies.append(pltpu.make_async_copy(part, stacked.at[pl.ds(start, CHIP), :], sem.at[at]))
-    for copy in copies:
-        copy.start()
-    for copy in copies:
-        copy.wait()
+        stacked[pl.ds(pl.multiple_of(group * CHIP, CHIP), CHIP), :] = part[...]
 
     def block_at(at):
         return stacked[:, at * LANES : (at + 1) * LANES].astype(F32).T
@@ -266,40 +292,33 @@
         out[i * SIDE : (i + 1) * SIDE, :] = rows.astype(BF16)
     start = pl.multiple_of(SIDE * PLANE + base, 8)
     out_mask[...] = turned[pl.ds(start, ROWS), :].astype(BF16)
-
-
-def arrange_left(parts):
+    for copy in copies:
+        copy.wait()
+
+
+def arrange_left(parts, own, near):
+    vmem, anywhere = (pl.BlockSpec(memory_space=m) for m in (pltpu.VMEM, pl.ANY))
     return pl.pallas_call(
         left_kernel,
-        in_specs=[pl.BlockSpec(memory_space=pl.ANY)] * len(parts),
-        out_specs=[pl.BlockSpec(memory_space=pltpu.VMEM)] * 2,
+        in_specs=[vmem] * len(parts) + [anywhere] * 2,
+        out_specs=[vmem] * 3,
         out_shape=[
             jax.ShapeDtypeStruct((ROWS * SIDE, TOTAL), BF16),
             jax.ShapeDtypeStruct((ROWS, TOTAL), BF16),
+            pltpu.VMEM((TOTAL, RIGHT), BF16),
         ],
         scratch_shapes=[
             pltpu.VMEM((TOTAL, LEFT), BF16),
             pltpu.VMEM(((SIDE + 1) * PLANE, TOTAL), F32),
-            pltpu.SemaphoreType.DMA((RING,)),
+            pltpu.SemaphoreType.DMA((2,)),
         ],
         compiler_params=pltpu.CompilerParams(vmem_limit_bytes=16 * MEGA),
-    )(*parts)
-
-
-def pair_kernel(block, beside, left, left_mask, weight, *refs):
-    parts, (out, right, outer, scale, sem) = refs[:RING], refs[RING:]
-    _, _, core, _ = position()
-
+    )(*parts, own, near)
+
+
+def pair_kernel(block, beside, left, left_mask, weight, right, out, outer, scale):
     @pl.when(pl.program_id(0) == 0)
     def _():
-        copies = []
-        for k, slot in enumerate((0, 1 + 2 * core, 3 - 2 * core, 2)):
-            rows = pl.ds(pl.multiple_of(slot * CHIP, CHIP), CHIP)
-            copies.append(pltpu.make_async_copy(parts[k], right.at[rows, :], sem.at[k]))
-        for copy in copies:
-            copy.start()
-        for copy in copies:
-            copy.wait()
         counts = jnp.dot(left_mask[...], right[:, SIDE * COLS :], preferred_element_type=F32)
         scale[...] = 1.0 / (counts + 0.001)
 
@@ -322,8 +341,8 @@
             out[i + k] = value.T.astype(BF16)
 
 
-def pair(left, left_mask, weight, parts):
-    block, beside = 8, 2
+def pair(left, left_mask, weight, right):
+    block, beside = 16, 2
     whole = lambda a: pl.BlockSpec(a.shape, lambda i: (0,) * a.ndim)
     return pl.pallas_call(
         functools.partial(pair_kernel, block, beside),
@@ -332,18 +351,16 @@
             pl.BlockSpec((block * SIDE, TOTAL), lambda i: (i, 0)),
             whole(left_mask),
             whole(weight),
-        ]
-        + [pl.BlockSpec(memory_space=pl.ANY)] * len(parts),
+            pl.BlockSpec(memory_space=pltpu.VMEM),
+        ],
         out_specs=pl.BlockSpec((block, COLS, PAIR), lambda i: (i, 0, 0)),
         out_shape=jax.ShapeDtypeStruct((ROWS, COLS, PAIR), BF16),
         scratch_shapes=[
-            pltpu.VMEM((TOTAL, RIGHT), BF16),
             pltpu.VMEM((block // beside, SIDE * SIDE, beside * COLS), BF16),
             pltpu.VMEM((ROWS, COLS), F32),
-            pltpu.SemaphoreType.DMA((RING,)),
         ],
         compiler_params=pltpu.CompilerParams(vmem_limit_bytes=40 * MEGA),
-    )(left, left_mask, weight, *parts)
+    )(left, left_mask, weight, right)
 
 
 def local(
@@ -369,17 +386,21 @@
     far = res_shift(own[RING], 2, 0, 0)
     weight = arrange_weight(output_weight)
     along_y[2], weight = lax.optimization_barrier((along_y[2], weight))
-    right, left, far_chip = stack(along_y + [core_swap(part) for part in along_y], far, core_swap(far))
+    along_y[3], far = lax.optimization_barrier((along_y[3], far))
+    swapped = [core_swap(part) for part in along_y]
+    right, left = stack(along_y + swapped)
+    left_parts = [to_row_owner(left, k) for k in range(2)]
     near = both_ways(right, 1, 0)
-    left_parts = [to_row_owner(left, k) for k in range(2)]
+    far_chip = stack_chip(far, core_swap(far), left)
     far_parts = [both_ways(far_chip, 0, 1), res_shift(far, 0, 2, 0)]
     left_parts, far_parts, near = lax.optimization_barrier((left_parts, far_parts, near))
-    sides = arrange_left(left_parts + [core_swap(part) for part in left_parts])
-    sides, far_chip = lax.optimization_barrier((sides, far_chip))
-    far_right = stack_far(
-        far_chip, far_parts[0], core_swap(far_parts[0]), far_parts[1], core_swap(far_parts[1])
-    )
-    return pair(*sides, weight, [right, near, core_swap(near), far_right])
+    left_others = [core_swap(part) for part in left_parts]
+    far_others = [core_swap(part) for part in far_parts]
+    left_others, far_others, near = lax.optimization_barrier((left_others, far_others, near))
+    left_all, left_mask, right_all = arrange_left(left_parts + left_others, right, near)
+    far_parts = [far_chip, far_parts[0], far_others[0], far_parts[1], far_others[1]]
+    right_all = finish_right(far_parts, core_swap(near), right_all)
+    return pair(left_all, left_mask, weight, right_all)
 
 
 def solution(mesh):

time: 60.9 us -> 59.8 us (0.982); the launches traced: 60.7 us -> 58.8 us
  waiting for transfers between devices: 11.5 us -> 9 us
  starting transfers between devices: 23.8 us -> 26.1 us
  Pallas kernels: 24.1 us -> 22.6 us
    ppermute x2, waiting for transfers between devices: 4.27 us -> 0.79 us  [to_row_owner(): return lax.ppermute(value, ('res', 'col'), pairs)]
    ppermute x2, starting transfers between devices: 5.2 us -> 6.91 us  [to_row_owner(): return lax.ppermute(value, ('res', 'col'), pairs)]
    ppermute x2, starting transfers between devices: 3.93 us -> 5.53 us  [both_ways(): return lax.ppermute(value, 'res', pairs)]
    ppermute x15, starting transfers between devices: 14.7 us -> 13.7 us  [res_shift(): return lax.ppermute(value, 'res', pairs)]
    ppermute x15, waiting for transfers between devices: 7.26 us -> 8.21 us  [res_shift(): return lax.ppermute(value, 'res', pairs)]
    pallas_call x1, Pallas kernels: 17.8 us -> 16.9 us  [pair(): pl.pallas_call(functools.partial(pair_kernel, block, beside), grid=(ROWS...]
    pallas_call x2 -> x3, Pallas kernels: 2.26 us -> 1.72 us  [the longest x1 1.13 us: arrange_left(): pl.pallas_call(left_kernel, in_specs=[vmem] * len(parts) + [anywhere] * 2...]
  transfers between devices with their start and end apart: 19 -> 19, of which waited for: 6 -> 6; matrix products, arithmetic and copies ran while one was open for 0% -> 0% of each run, Pallas kernels for 4% -> 3%
where the time goes in v5:
time: 59.8 us; the launch traced here: 58.8 us
  starting transfers between devices  26.1 us (44%)
  Pallas kernels  22.6 us (38%)
  waiting for transfers between devices  9 us (15%)
  local copies, waits for them, and re-layouts  0.95 us (2%)
    pallas_call x1, Pallas kernels, pair(): pl.pallas_call(functools.partial(pair_kernel, block, beside), grid=(ROWS...  16.9 us
    ppermute x15, starting transfers between devices, res_shift(): return lax.ppermute(value, 'res', pairs)  13.7 us
    ppermute x15, waiting for transfers between devices, res_shift(): return lax.ppermute(value, 'res', pairs)  8.21 us
    ppermute x2, starting transfers between devices, to_row_owner(): return lax.ppermute(value, ('res', 'col'), pairs)  6.91 us
    ppermute x2, starting transfers between devices, both_ways(): return lax.ppermute(value, 'res', pairs)  5.53 us
    pallas_call x1, Pallas kernels, project(): pl.pallas_call(project_kernel, in_specs=[pl.BlockSpec(memory_space=pltpu....  2.98 us
  transfers between devices with their start and end apart: 19, of which 6 were waited for; matrix products, arithmetic and copies ran while one was open for 0% of the time, Pallas kernels for 3%

profile of v5, /device:TPU:1, one launch (start us, length us, event | category | flops | bytes accessed | tf_op | source)
XLA Modules:
  0.0 58.8 jit_solution(16436716993688471571)
XLA Ops:
  0.0 3.0 %shard_map.82 = (bf16[4,15872]{1,0:T(4,128)(2,1)S(1)}, bf16[4,15872]{1,0:T(4,128)(2,1)S(1)}, bf16[4,15872]{1,0:T(4,128)(2,1)S(1)}, bf16[4,15872]{1,0:T(4,128)(2,1)S(1)}, bf16[4,12672]{1,0:T(4,128)(2,1)S(1)}) custom-call(bf16[4,384,256]{2,1,0:T(8,128)(2,1)} %refs_0_.1, bf16[4,8]{1,0:T(4,128)(2,1)} %refs_1_.1, s32[384]{0:T(512)} %refs_2_.1, f32[256]{0:T(256)} %refs_3_.1, ...), custom_call_target="tpu_custom_call" | custom-call | tf_op jit(solution)/shard_map/pallas_call | solution.py:131
  3.0 3.8 %collective-permute-start.1 = (bf16[4,15872]{1,0:T(4,128)(2,1)S(1)}, bf16[4,15872]{1,0:T(4,128)(2,1)S(1)}, u32[]{:S(2)}, u32[]{:S(2)}) collective-permute-start(bf16[4,15872]{1,0:T(4,128)(2,1)S(1)} %get-tuple-element.31), channel_id=1, source_target_pairs={{0,16},{4,20},{8,24},{12,28},{16,0},{20,4},{24,8},{28,12},{32,48},... | collective-permute-start | bytes 380936 | tf_op jit(solution)/shard_map/ppermute | solution.py:42
  6.8 0.8 %collective-permute-start.2 = (bf16[4,15872]{1,0:T(4,128)(2,1)S(1)}, bf16[4,15872]{1,0:T(4,128)(2,1)S(1)}, u32[]{:S(2)}, u32[]{:S(2)}) collective-permute-start(bf16[4,15872]{1,0:T(4,128)(2,1)S(1)} %get-tuple-element.33), channel_id=1, source_target_pairs={{0,24},{4,28},{8,0},{12,4},{16,8},{20,12},{24,16},{28,20},{32,56},... | collective-permute-start | bytes 380936 | tf_op jit(solution)/shard_map/ppermute | solution.py:42
  7.6 0.7 %collective-permute-start = (bf16[4,15872]{1,0:T(4,128)(2,1)S(1)}, bf16[4,15872]{1,0:T(4,128)(2,1)S(1)}, u32[]{:S(2)}, u32[]{:S(2)}) collective-permute-start(bf16[4,15872]{1,0:T(4,128)(2,1)S(1)} %get-tuple-element.30), channel_id=1, source_target_pairs={{0,8},{4,12},{8,16},{12,20},{16,24},{20,28},{24,0},{28,4},{32,40},... | collective-permute-start | bytes 380936 | tf_op jit(solution)/shard_map/ppermute | solution.py:42
  8.3 3.6 %collective-permute-start.3 = (bf16[4,12672]{1,0:T(4,128)(2,1)S(1)}, bf16[4,12672]{1,0:T(4,128)(2,1)S(1)}, u32[]{:S(2)}, u32[]{:S(2)}) collective-permute-start(bf16[4,12672]{1,0:T(4,128)(2,1)S(1)} %get-tuple-element.34), channel_id=1, source_target_pairs={{0,64},{4,68},{8,72},{12,76},{16,80},{20,84},{24,88},{28,92},{32,9... | collective-permute-start | bytes 304136 | tf_op jit(solution)/shard_map/ppermute | solution.py:42
  11.9 1.8 %collective-permute-start.4 = (bf16[4,15872]{1,0:T(4,128)(2,1)S(1)}, bf16[4,15872]{1,0:T(4,128)(2,1)S(1)}, u32[]{:S(2)}, u32[]{:S(2)}) collective-permute-start(bf16[4,15872]{1,0:T(4,128)(2,1)S(1)} %get-tuple-element.29.refs_0_), channel_id=1, source_target_pairs={{0,4},{4,0},{8,12},{12,8},{16,20},{20,16},{24,28},{28,24},{32,36},... | collective-permute-start | bytes 380936 | tf_op jit(solution)/shard_map/ppermute | solution.py:42
  13.7 0.0 copy-start
  13.7 0.9 %copy-done = bf16[1024,128]{1,0:T(8,128)(2,1)S(1)} copy-done((bf16[1024,128]{1,0:T(8,128)(2,1)S(1)}, bf16[1024,128]{1,0:T(8,128)(2,1)}, u32[]{:S(2)}) %copy-start) | copy-done | bytes 262168
  14.6 0.4 shard_map.83.weight
  15.1 0.0 collective-permute-done.1.refs_2_
  15.1 0.1 collective-permute-start.6
  15.2 0.0 collective-permute-done.3.far
  15.2 0.0 collective-permute-done.2.refs_3_
  15.2 0.0 collective-permute-done.refs_1_
  15.2 1.1 %collective-permute-start.5 = (bf16[4,15872]{1,0:T(4,128)(2,1)S(1)}, bf16[4,15872]{1,0:T(4,128)(2,1)S(1)}, u32[]{:S(2)}, u32[]{:S(2)}) collective-permute-start(bf16[4,15872]{1,0:T(4,128)(2,1)S(1)} %collective-permute-done.refs_1_), channel_id=1, source_target_pairs={{0,4},{4,0},{8,12},{12,8},{16,20},{20,16},{24,28},{28,24},{32,36},... | collective-permute-start | bytes 380936 | tf_op jit(solution)/shard_map/ppermute | solution.py:42
  16.3 0.1 collective-permute-start.7
  16.4 0.0 collective-permute-done.4.refs_4_
  16.4 0.9 %collective-permute-done.5.refs_5_ = bf16[4,15872]{1,0:T(4,128)(2,1)S(1)} collective-permute-done((bf16[4,15872]{1,0:T(4,128)(2,1)S(1)}, bf16[4,15872]{1,0:T(4,128)(2,1)S(1)}, u32[]{:S(2)}, u32[]{:S(2)}) %collective-permute-start.5) | collective-permute-done | bytes 127008 | tf_op jit(solution)/shard_map/ppermute | solution.py:42
  17.3 0.0 collective-permute-done.6.refs_6_
  17.3 0.4 collective-permute-done.7.refs_7_
  17.6 0.6 shard_map.84
  18.2 3.5 %collective-permute-start.13 = (bf16[32,12672]{1,0:T(8,128)(2,1)S(1)}, bf16[32,12672]{1,0:T(8,128)(2,1)S(1)}, u32[]{:S(2)}, u32[]{:S(2)}) collective-permute-start(bf16[32,12672]{1,0:T(8,128)(2,1)S(1)} %get-tuple-element.38.refs_4_), channel_id=1, source_target_pairs={{0,32},{4,100},{8,40},{12,108},{16,48},{20,116},{24,56},{28,124},{... | collective-permute-start | bytes 2433032 | tf_op jit(solution)/shard_map/ppermute | solution.py:56
  21.7 0.0 collective-permute-start.10
  21.7 2.5 %collective-permute-start.9 = (bf16[32,3200]{1,0:T(8,128)(2,1)S(1)}, bf16[32,3200]{1,0:T(8,128)(2,1)S(1)}, u32[]{:S(2)}, u32[]{:S(2)}) collective-permute-start(bf16[32,3200]{1,0:T(8,128)(2,1)S(1)} %get-tuple-element.36.after), channel_id=1, source_target_pairs={{0,1},{1,33},{2,65},{3,97},{4,7},{5,39},{6,71},{7,103},{8,9},{9,41... | collective-permute-start | bytes 614408 | tf_op jit(solution)/shard_map/ppermute | solution.py:68
  24.2 4.4 %collective-permute-start.8 = (bf16[32,3200]{1,0:T(8,128)(2,1)S(1)}, bf16[32,3200]{1,0:T(8,128)(2,1)S(1)}, u32[]{:S(2)}, u32[]{:S(2)}) collective-permute-start(bf16[32,3200]{1,0:T(8,128)(2,1)S(1)} %get-tuple-element.36.after), channel_id=1, source_target_pairs={{0,0},{1,32},{2,64},{3,96},{4,6},{5,38},{6,70},{7,102},{8,8},{9,40... | collective-permute-start | bytes 614408 | tf_op jit(solution)/shard_map/ppermute | solution.py:68
  28.6 0.0 collective-permute-done.10.far_other
  28.6 0.1 shard_map.85.own
  28.8 2.1 %collective-permute-start.11 = (bf16[8,12672]{1,0:T(8,128)(2,1)S(1)}, bf16[8,12672]{1,0:T(8,128)(2,1)S(1)}, u32[]{:S(2)}, u32[]{:S(2)}) collective-permute-start(bf16[8,12672]{1,0:T(8,128)(2,1)S(1)} %shard_map.85.own), channel_id=1, source_target_pairs={{0,8},{4,28},{8,16},{12,4},{16,24},{20,12},{24,0},{28,20},{32,40},... | collective-permute-start | bytes 608264 | tf_op jit(solution)/shard_map/ppermute | solution.py:56
  30.8 0.2 collective-permute-start.12
  31.0 4.8 %collective-permute-done.12.far = bf16[4,12672]{1,0:T(4,128)(2,1)S(1)} collective-permute-done((bf16[4,12672]{1,0:T(4,128)(2,1)S(1)}, bf16[4,12672]{1,0:T(4,128)(2,1)S(1)}, u32[]{:S(2)}, u32[]{:S(2)}) %collective-permute-start.12) | collective-permute-done | bytes 101408 | tf_op jit(solution)/shard_map/ppermute | solution.py:42
  35.8 0.0 collective-permute-done.11.near
  35.8 0.0 collective-permute-done.9.refs_1_
  35.8 0.8 %collective-permute-done.8.refs_0_ = bf16[32,3200]{1,0:T(8,128)(2,1)S(1)} collective-permute-done((bf16[32,3200]{1,0:T(8,128)(2,1)S(1)}, bf16[32,3200]{1,0:T(8,128)(2,1)S(1)}, u32[]{:S(2)}, u32[]{:S(2)}) %collective-permute-start.8) | collective-permute-done | bytes 204832 | tf_op jit(solution)/shard_map/ppermute | solution.py:68
  36.6 0.0 collective-permute-done.13.refs_5_
  36.6 0.0 collective-permute-start.14
  36.6 0.5 collective-permute-start.15
  37.1 0.0 collective-permute-start.16
  37.1 0.5 collective-permute-start.17
  37.6 1.2 %collective-permute-done.17.far_other = bf16[4,12672]{1,0:T(4,128)(2,1)S(1)} collective-permute-done((bf16[4,12672]{1,0:T(4,128)(2,1)S(1)}, bf16[4,12672]{1,0:T(4,128)(2,1)S(1)}, u32[]{:S(2)}, u32[]{:S(2)}) %collective-permute-start.17) | collective-permute-done | bytes 101408 | tf_op jit(solution)/shard_map/ppermute | solution.py:42
  38.8 0.0 collective-permute-done.16.near_other
  38.8 0.0 collective-permute-done.14.refs_2_
  38.8 0.0 collective-permute-done.15.refs_3_
  38.8 0.5 collective-permute-start.18
  39.3 1.1 %shard_map.86 = (bf16[1536,128]{1,0:T(8,128)(2,1)S(1)}, bf16[48,128]{1,0:T(8,128)(2,1)S(1)}, bf16[128,12672]{1,0:T(8,128)(2,1)S(1)}) custom-call(bf16[32,3200]{1,0:T(8,128)(2,1)S(1)} %collective-permute-done.8.refs_0_, bf16[32,3200]{1,0:T(8,128)(2,1)S(1)} %collective-permute-done.9.refs_1_, bf16[32,3200]{1,0:T(8,128)(2,1)S(1)} %collective-permute-done.14.refs_2_, ...), custom_call_target="tpu_custom_call" | custom-call | tf_op jit(solution)/shard_map/pallas_call | solution.py:301
  40.4 1.0 %collective-permute-done.18.right_part = bf16[32,12672]{1,0:T(8,128)(2,1)S(1)} collective-permute-done((bf16[32,12672]{1,0:T(8,128)(2,1)S(1)}, bf16[32,12672]{1,0:T(8,128)(2,1)S(1)}, u32[]{:S(2)}, u32[]{:S(2)}) %collective-permute-start.18) | collective-permute-done | bytes 811040 | tf_op jit(solution)/shard_map/ppermute | solution.py:42
  41.4 0.5 shard_map.87.right
  41.9 16.9 %shard_map.88 = bf16[48,384,128]{2,1,0:T(8,128)(2,1)} custom-call(bf16[1536,128]{1,0:T(8,128)(2,1)S(1)} %get-tuple-element.47.left, bf16[48,128]{1,0:T(8,128)(2,1)S(1)} %get-tuple-element.48.left_mask, bf16[128,1024]{1,0:T(8,128)(2,1)S(1)} %shard_map.83.weight, bf16[128,12672]{1,0:T(8,128)(2,1)S(1)} %shard_map.87.right), custom_call_target="tpu_custom_call" | custom-call | tf_op jit(solution)/shard_map/pallas_call | solution.py:347
Async XLA Ops:
  3.0 12.1 %collective-permute-start.1 = (bf16[4,15872]{1,0:T(4,128)(2,1)S(1)}, bf16[4,15872]{1,0:T(4,128)(2,1)S(1)}, u32[]{:S(2)}, u32[]{:S(2)}) collective-permute-start(bf16[4,15872]{1,0:T(4,128)(2,1)S(1)} %get-tuple-element.31), channel_id=1, source_target_pairs={{0,16},{4,20},{8,24},{12,28},{16,0},{20,4},{24,8},{28,12},{32,48},... | collective-permute-start | bytes 380936 | tf_op jit(solution)/shard_map/ppermute | solution.py:42
  6.8 8.4 %collective-permute-start.2 = (bf16[4,15872]{1,0:T(4,128)(2,1)S(1)}, bf16[4,15872]{1,0:T(4,128)(2,1)S(1)}, u32[]{:S(2)}, u32[]{:S(2)}) collective-permute-start(bf16[4,15872]{1,0:T(4,128)(2,1)S(1)} %get-tuple-element.33), channel_id=1, source_target_pairs={{0,24},{4,28},{8,0},{12,4},{16,8},{20,12},{24,16},{28,20},{32,56},... | collective-permute-start | bytes 380936 | tf_op jit(solution)/shard_map/ppermute | solution.py:42
  7.6 7.6 %collective-permute-start = (bf16[4,15872]{1,0:T(4,128)(2,1)S(1)}, bf16[4,15872]{1,0:T(4,128)(2,1)S(1)}, u32[]{:S(2)}, u32[]{:S(2)}) collective-permute-start(bf16[4,15872]{1,0:T(4,128)(2,1)S(1)} %get-tuple-element.30), channel_id=1, source_target_pairs={{0,8},{4,12},{8,16},{12,20},{16,24},{20,28},{24,0},{28,4},{32,40},... | collective-permute-start | bytes 380936 | tf_op jit(solution)/shard_map/ppermute | solution.py:42
  8.3 6.9 %collective-permute-start.3 = (bf16[4,12672]{1,0:T(4,128)(2,1)S(1)}, bf16[4,12672]{1,0:T(4,128)(2,1)S(1)}, u32[]{:S(2)}, u32[]{:S(2)}) collective-permute-start(bf16[4,12672]{1,0:T(4,128)(2,1)S(1)} %get-tuple-element.34), channel_id=1, source_target_pairs={{0,64},{4,68},{8,72},{12,76},{16,80},{20,84},{24,88},{28,92},{32,9... | collective-permute-start | bytes 304136 | tf_op jit(solution)/shard_map/ppermute | solution.py:42
  11.9 4.5 %collective-permute-start.4 = (bf16[4,15872]{1,0:T(4,128)(2,1)S(1)}, bf16[4,15872]{1,0:T(4,128)(2,1)S(1)}, u32[]{:S(2)}, u32[]{:S(2)}) collective-permute-start(bf16[4,15872]{1,0:T(4,128)(2,1)S(1)} %get-tuple-element.29.refs_0_), channel_id=1, source_target_pairs={{0,4},{4,0},{8,12},{12,8},{16,20},{20,16},{24,28},{28,24},{32,36},... | collective-permute-start | bytes 380936 | tf_op jit(solution)/shard_map/ppermute | solution.py:42
  13.7 0.9 %copy-start = (bf16[1024,128]{1,0:T(8,128)(2,1)S(1)}, bf16[1024,128]{1,0:T(8,128)(2,1)}, u32[]{:S(2)}) copy-start(bf16[1024,128]{1,0:T(8,128)(2,1)} %weight_hbm.1) | copy-start | bytes 786436
  15.1 2.2 %collective-permute-start.6 = (bf16[4,15872]{1,0:T(4,128)(2,1)S(1)}, bf16[4,15872]{1,0:T(4,128)(2,1)S(1)}, u32[]{:S(2)}, u32[]{:S(2)}) collective-permute-start(bf16[4,15872]{1,0:T(4,128)(2,1)S(1)} %collective-permute-done.1.refs_2_), channel_id=1, source_target_pairs={{0,4},{4,0},{8,12},{12,8},{16,20},{20,16},{24,28},{28,24},{32,36},... | collective-permute-start | bytes 380936 | tf_op jit(solution)/shard_map/ppermute | solution.py:42
  15.2 2.1 %collective-permute-start.5 = (bf16[4,15872]{1,0:T(4,128)(2,1)S(1)}, bf16[4,15872]{1,0:T(4,128)(2,1)S(1)}, u32[]{:S(2)}, u32[]{:S(2)}) collective-permute-start(bf16[4,15872]{1,0:T(4,128)(2,1)S(1)} %collective-permute-done.refs_1_), channel_id=1, source_target_pairs={{0,4},{4,0},{8,12},{12,8},{16,20},{20,16},{24,28},{28,24},{32,36},... | collective-permute-start | bytes 380936 | tf_op jit(solution)/shard_map/ppermute | solution.py:42
  16.3 1.3 %collective-permute-start.7 = (bf16[4,15872]{1,0:T(4,128)(2,1)S(1)}, bf16[4,15872]{1,0:T(4,128)(2,1)S(1)}, u32[]{:S(2)}, u32[]{:S(2)}) collective-permute-start(bf16[4,15872]{1,0:T(4,128)(2,1)S(1)} %collective-permute-done.2.refs_3_), channel_id=1, source_target_pairs={{0,4},{4,0},{8,12},{12,8},{16,20},{20,16},{24,28},{28,24},{32,36},... | collective-permute-start | bytes 380936 | tf_op jit(solution)/shard_map/ppermute | solution.py:42
  18.2 18.4 %collective-permute-start.13 = (bf16[32,12672]{1,0:T(8,128)(2,1)S(1)}, bf16[32,12672]{1,0:T(8,128)(2,1)S(1)}, u32[]{:S(2)}, u32[]{:S(2)}) collective-permute-start(bf16[32,12672]{1,0:T(8,128)(2,1)S(1)} %get-tuple-element.38.refs_4_), channel_id=1, source_target_pairs={{0,32},{4,100},{8,40},{12,108},{16,48},{20,116},{24,56},{28,124},{... | collective-permute-start | bytes 2433032 | tf_op jit(solution)/shard_map/ppermute | solution.py:56
  21.7 6.9 %collective-permute-start.10 = (bf16[4,12672]{1,0:T(4,128)(2,1)S(1)}, bf16[4,12672]{1,0:T(4,128)(2,1)S(1)}, u32[]{:S(2)}, u32[]{:S(2)}) collective-permute-start(bf16[4,12672]{1,0:T(4,128)(2,1)S(1)} %collective-permute-done.3.far), channel_id=1, source_target_pairs={{0,4},{4,0},{8,12},{12,8},{16,20},{20,16},{24,28},{28,24},{32,36},... | collective-permute-start | bytes 304136 | tf_op jit(solution)/shard_map/ppermute | solution.py:42
  21.7 14.1 %collective-permute-start.9 = (bf16[32,3200]{1,0:T(8,128)(2,1)S(1)}, bf16[32,3200]{1,0:T(8,128)(2,1)S(1)}, u32[]{:S(2)}, u32[]{:S(2)}) collective-permute-start(bf16[32,3200]{1,0:T(8,128)(2,1)S(1)} %get-tuple-element.36.after), channel_id=1, source_target_pairs={{0,1},{1,33},{2,65},{3,97},{4,7},{5,39},{6,71},{7,103},{8,9},{9,41... | collective-permute-start | bytes 614408 | tf_op jit(solution)/shard_map/ppermute | solution.py:68
  24.2 12.4 %collective-permute-start.8 = (bf16[32,3200]{1,0:T(8,128)(2,1)S(1)}, bf16[32,3200]{1,0:T(8,128)(2,1)S(1)}, u32[]{:S(2)}, u32[]{:S(2)}) collective-permute-start(bf16[32,3200]{1,0:T(8,128)(2,1)S(1)} %get-tuple-element.36.after), channel_id=1, source_target_pairs={{0,0},{1,32},{2,64},{3,96},{4,6},{5,38},{6,70},{7,102},{8,8},{9,40... | collective-permute-start | bytes 614408 | tf_op jit(solution)/shard_map/ppermute | solution.py:68
  28.8 7.1 %collective-permute-start.11 = (bf16[8,12672]{1,0:T(8,128)(2,1)S(1)}, bf16[8,12672]{1,0:T(8,128)(2,1)S(1)}, u32[]{:S(2)}, u32[]{:S(2)}) collective-permute-start(bf16[8,12672]{1,0:T(8,128)(2,1)S(1)} %shard_map.85.own), channel_id=1, source_target_pairs={{0,8},{4,28},{8,16},{12,4},{16,24},{20,12},{24,0},{28,20},{32,40},... | collective-permute-start | bytes 608264 | tf_op jit(solution)/shard_map/ppermute | solution.py:56
  30.8 5.0 %collective-permute-start.12 = (bf16[4,12672]{1,0:T(4,128)(2,1)S(1)}, bf16[4,12672]{1,0:T(4,128)(2,1)S(1)}, u32[]{:S(2)}, u32[]{:S(2)}) collective-permute-start(bf16[4,12672]{1,0:T(4,128)(2,1)S(1)} %collective-permute-done.3.far), channel_id=1, source_target_pairs={{0,16},{4,20},{8,24},{12,28},{16,0},{20,4},{24,8},{28,12},{32,48},... | collective-permute-start | bytes 304136 | tf_op jit(solution)/shard_map/ppermute | solution.py:42
  36.6 2.2 %collective-permute-start.14 = (bf16[32,3200]{1,0:T(8,128)(2,1)S(1)}, bf16[32,3200]{1,0:T(8,128)(2,1)S(1)}, u32[]{:S(2)}, u32[]{:S(2)}) collective-permute-start(bf16[32,3200]{1,0:T(8,128)(2,1)S(1)} %collective-permute-done.8.refs_0_), channel_id=1, source_target_pairs={{0,4},{4,0},{8,12},{12,8},{16,20},{20,16},{24,28},{28,24},{32,36},... | collective-permute-start | bytes 614408 | tf_op jit(solution)/shard_map/ppermute | solution.py:42
  36.6 2.2 %collective-permute-start.15 = (bf16[32,3200]{1,0:T(8,128)(2,1)S(1)}, bf16[32,3200]{1,0:T(8,128)(2,1)S(1)}, u32[]{:S(2)}, u32[]{:S(2)}) collective-permute-start(bf16[32,3200]{1,0:T(8,128)(2,1)S(1)} %collective-permute-done.9.refs_1_), channel_id=1, source_target_pairs={{0,4},{4,0},{8,12},{12,8},{16,20},{20,16},{24,28},{28,24},{32,36},... | collective-permute-start | bytes 614408 | tf_op jit(solution)/shard_map/ppermute | solution.py:42
  37.1 1.7 %collective-permute-start.16 = (bf16[8,12672]{1,0:T(8,128)(2,1)S(1)}, bf16[8,12672]{1,0:T(8,128)(2,1)S(1)}, u32[]{:S(2)}, u32[]{:S(2)}) collective-permute-start(bf16[8,12672]{1,0:T(8,128)(2,1)S(1)} %collective-permute-done.11.near), channel_id=1, source_target_pairs={{0,4},{4,0},{8,12},{12,8},{16,20},{20,16},{24,28},{28,24},{32,36},... | collective-permute-start | bytes 608264 | tf_op jit(solution)/shard_map/ppermute | solution.py:42
  37.1 1.7 %collective-permute-start.17 = (bf16[4,12672]{1,0:T(4,128)(2,1)S(1)}, bf16[4,12672]{1,0:T(4,128)(2,1)S(1)}, u32[]{:S(2)}, u32[]{:S(2)}) collective-permute-start(bf16[4,12672]{1,0:T(4,128)(2,1)S(1)} %collective-permute-done.12.far), channel_id=1, source_target_pairs={{0,4},{4,0},{8,12},{12,8},{16,20},{20,16},{24,28},{28,24},{32,36},... | collective-permute-start | bytes 304136 | tf_op jit(solution)/shard_map/ppermute | solution.py:42
  38.8 2.6 %collective-permute-start.18 = (bf16[32,12672]{1,0:T(8,128)(2,1)S(1)}, bf16[32,12672]{1,0:T(8,128)(2,1)S(1)}, u32[]{:S(2)}, u32[]{:S(2)}) collective-permute-start(bf16[32,12672]{1,0:T(8,128)(2,1)S(1)} %collective-permute-done.13.refs_5_), channel_id=1, source_target_pairs={{0,4},{4,0},{8,12},{12,8},{16,20},{20,16},{24,28},{28,24},{32,36},... | collective-permute-start | bytes 2433032 | tf_op jit(solution)/shard_map/ppermute | solution.py:42

commit v6 on v5

--- a/solution.py
+++ b/solution.py
@@ -224,10 +224,8 @@
     )(far, far_other, after)
 
 
-def far_kernel(own, near, near_other, far, far_other, right_part, _, right, wide, sem):
-    _, _, core, _ = position()
-    copy = pltpu.make_async_copy(right_part, right.at[rows_of(3 - 2 * core), :], sem)
-    copy.start()
+def stack_far(own, near, near_other, far, far_other, out, wide):
+    core = position()[2]
     for at, width in chunks(RIGHT):
         lanes = slice(at, at + width)
         below, above = by_core(core, near[:, lanes].astype(F32), near_other[:, lanes].astype(F32))
@@ -238,21 +236,27 @@
             for d, value in enumerate((here[rows], below[rows], opposite[c], above[rows])):
                 start = c * GROUP + d * SEQS
                 wide[start : start + SEQS, :width] = value
-        right[2 * CHIP : 3 * CHIP, lanes] = wide[:, :width].astype(BF16)
+        out[2 * CHIP : 3 * CHIP, lanes] = wide[:, :width].astype(BF16)
+
+
+def finish_kernel(right_part, _, right, sem):
+    core = position()[2]
+    copy = pltpu.make_async_copy(right_part, right.at[rows_of(3 - 2 * core), :], sem)
+    copy.start()
     copy.wait()
 
 
-def finish_right(parts, right_part, right):
+def finish_right(right_part, right):
     vmem, anywhere = (pl.BlockSpec(memory_space=m) for m in (pltpu.VMEM, pl.ANY))
     return pl.pallas_call(
-        far_kernel,
-        in_specs=[vmem] * len(parts) + [anywhere, vmem],
+        finish_kernel,
+        in_specs=[anywhere, vmem],
         out_specs=vmem,
         out_shape=pltpu.VMEM((TOTAL, RIGHT), BF16),
-        input_output_aliases={len(parts) + 1: 0},
-        scratch_shapes=[pltpu.VMEM((CHIP, 2 * COLS), F32), pltpu.SemaphoreType.DMA],
+        input_output_aliases={1: 0},
+        scratch_shapes=[pltpu.SemaphoreType.DMA],
         compiler_params=pltpu.CompilerParams(vmem_limit_bytes=16 * MEGA),
-    )(*parts, right_part, right)
+    )(right_part, right)
 
 
 def rows_of(slot):
@@ -260,7 +264,8 @@
 
 
 def left_kernel(*refs):
-    parts, (own, near, out, out_mask, right, stacked, turned, sem) = refs[:RING], refs[RING:]
+    parts, fars, refs = refs[:RING], refs[RING : RING + 5], refs[RING + 5 :]
+    own, near, out, out_mask, right, stacked, turned, wide, sem = refs
     z, _, core, x = position()
     copies = [
         pltpu.make_async_copy(part, right.at[rows_of(slot), :], sem.at[k])
@@ -292,15 +297,16 @@
         out[i * SIDE : (i + 1) * SIDE, :] = rows.astype(BF16)
     start = pl.multiple_of(SIDE * PLANE + base, 8)
     out_mask[...] = turned[pl.ds(start, ROWS), :].astype(BF16)
+    stack_far(*fars, right, wide)
     for copy in copies:
         copy.wait()
 
 
-def arrange_left(parts, own, near):
+def arrange_left(parts, fars, own, near):
     vmem, anywhere = (pl.BlockSpec(memory_space=m) for m in (pltpu.VMEM, pl.ANY))
     return pl.pallas_call(
         left_kernel,
-        in_specs=[vmem] * len(parts) + [anywhere] * 2,
+        in_specs=[vmem] * (len(parts) + len(fars)) + [anywhere] * 2,
         out_specs=[vmem] * 3,
         out_shape=[
             jax.ShapeDtypeStruct((ROWS * SIDE, TOTAL), BF16),
@@ -310,10 +316,11 @@
         scratch_shapes=[
             pltpu.VMEM((TOTAL, LEFT), BF16),
             pltpu.VMEM(((SIDE + 1) * PLANE, TOTAL), F32),
+            pltpu.VMEM((CHIP, 2 * COLS), F32),
             pltpu.SemaphoreType.DMA((2,)),
         ],
         compiler_params=pltpu.CompilerParams(vmem_limit_bytes=16 * MEGA),
-    )(*parts, own, near)
+    )(*parts, *fars, own, near)
 
 
 def pair_kernel(block, beside, left, left_mask, weight, right, out, outer, scale):
@@ -397,9 +404,10 @@
     left_others = [core_swap(part) for part in left_parts]
     far_others = [core_swap(part) for part in far_parts]
     left_others, far_others, near = lax.optimization_barrier((left_others, far_others, near))
-    left_all, left_mask, right_all = arrange_left(left_parts + left_others, right, near)
     far_parts = [far_chip, far_parts[0], far_others[0], far_parts[1], far_others[1]]
-    right_all = finish_right(far_parts, core_swap(near), right_all)
+    left_parts = left_parts + left_others
+    left_all, left_mask, right_all = arrange_left(left_parts, far_parts, right, near)
+    right_all = finish_right(core_swap(near), right_all)
     return pair(left_all, left_mask, weight, right_all)
 
 

time: 59.8 us -> 59.5 us (level)
  transfers between devices with their start and end apart: 19 -> 19, of which waited for: 6 -> 6; matrix products, arithmetic and copies ran while one was open for 0% -> 0% of each run, Pallas kernels for 3% -> 4%
where the time goes in v6:
time: 59.5 us; the launch traced here: 58.4 us
  starting transfers between devices  26.1 us (44%)
  Pallas kernels  22.6 us (38%)
  waiting for transfers between devices  8.64 us (15%)
  local copies, waits for them, and re-layouts  0.95 us (2%)
    pallas_call x1, Pallas kernels, pair(): pl.pallas_call(functools.partial(pair_kernel, block, beside), grid=(ROWS...  16.9 us
    ppermute x15, starting transfers between devices, res_shift(): return lax.ppermute(value, 'res', pairs)  13.7 us
    ppermute x15, waiting for transfers between devices, res_shift(): return lax.ppermute(value, 'res', pairs)  7.85 us
    ppermute x2, starting transfers between devices, to_row_owner(): return lax.ppermute(value, ('res', 'col'), pairs)  6.91 us
    ppermute x2, starting transfers between devices, both_ways(): return lax.ppermute(value, 'res', pairs)  5.53 us
    pallas_call x1, Pallas kernels, project(): pl.pallas_call(project_kernel, in_specs=[pl.BlockSpec(memory_space=pltpu....  2.98 us
    pallas_call x1, Pallas kernels, arrange_left(): pl.pallas_call(left_kernel, in_specs=[vmem] * (len(parts) + len(fars)) +...  1.49 us
  transfers between devices with their start and end apart: 19, of which 6 were waited for; matrix products, arithmetic and copies ran while one was open for 0% of the time, Pallas kernels for 4%

profile of v6, /device:TPU:1, one launch (start us, length us, event | category | flops | bytes accessed | tf_op | source)
XLA Modules:
  0.0 58.4 jit_solution(3212217943943345743)
XLA Ops:
  0.0 3.0 %shard_map.82 = (bf16[4,15872]{1,0:T(4,128)(2,1)S(1)}, bf16[4,15872]{1,0:T(4,128)(2,1)S(1)}, bf16[4,15872]{1,0:T(4,128)(2,1)S(1)}, bf16[4,15872]{1,0:T(4,128)(2,1)S(1)}, bf16[4,12672]{1,0:T(4,128)(2,1)S(1)}) custom-call(bf16[4,384,256]{2,1,0:T(8,128)(2,1)} %refs_0_.1, bf16[4,8]{1,0:T(4,128)(2,1)} %refs_1_.1, s32[384]{0:T(512)} %refs_2_.1, f32[256]{0:T(256)} %refs_3_.1, ...), custom_call_target="tpu_custom_call" | custom-call | tf_op jit(solution)/shard_map/pallas_call | solution.py:131
  3.0 3.8 %collective-permute-start.1 = (bf16[4,15872]{1,0:T(4,128)(2,1)S(1)}, bf16[4,15872]{1,0:T(4,128)(2,1)S(1)}, u32[]{:S(2)}, u32[]{:S(2)}) collective-permute-start(bf16[4,15872]{1,0:T(4,128)(2,1)S(1)} %get-tuple-element.31), channel_id=1, source_target_pairs={{0,16},{4,20},{8,24},{12,28},{16,0},{20,4},{24,8},{28,12},{32,48},... | collective-permute-start | bytes 380936 | tf_op jit(solution)/shard_map/ppermute | solution.py:42
  6.8 0.8 %collective-permute-start.2 = (bf16[4,15872]{1,0:T(4,128)(2,1)S(1)}, bf16[4,15872]{1,0:T(4,128)(2,1)S(1)}, u32[]{:S(2)}, u32[]{:S(2)}) collective-permute-start(bf16[4,15872]{1,0:T(4,128)(2,1)S(1)} %get-tuple-element.33), channel_id=1, source_target_pairs={{0,24},{4,28},{8,0},{12,4},{16,8},{20,12},{24,16},{28,20},{32,56},... | collective-permute-start | bytes 380936 | tf_op jit(solution)/shard_map/ppermute | solution.py:42
  7.6 0.7 %collective-permute-start = (bf16[4,15872]{1,0:T(4,128)(2,1)S(1)}, bf16[4,15872]{1,0:T(4,128)(2,1)S(1)}, u32[]{:S(2)}, u32[]{:S(2)}) collective-permute-start(bf16[4,15872]{1,0:T(4,128)(2,1)S(1)} %get-tuple-element.30), channel_id=1, source_target_pairs={{0,8},{4,12},{8,16},{12,20},{16,24},{20,28},{24,0},{28,4},{32,40},... | collective-permute-start | bytes 380936 | tf_op jit(solution)/shard_map/ppermute | solution.py:42
  8.3 3.6 %collective-permute-start.3 = (bf16[4,12672]{1,0:T(4,128)(2,1)S(1)}, bf16[4,12672]{1,0:T(4,128)(2,1)S(1)}, u32[]{:S(2)}, u32[]{:S(2)}) collective-permute-start(bf16[4,12672]{1,0:T(4,128)(2,1)S(1)} %get-tuple-element.34), channel_id=1, source_target_pairs={{0,64},{4,68},{8,72},{12,76},{16,80},{20,84},{24,88},{28,92},{32,9... | collective-permute-start | bytes 304136 | tf_op jit(solution)/shard_map/ppermute | solution.py:42
  11.9 1.8 %collective-permute-start.4 = (bf16[4,15872]{1,0:T(4,128)(2,1)S(1)}, bf16[4,15872]{1,0:T(4,128)(2,1)S(1)}, u32[]{:S(2)}, u32[]{:S(2)}) collective-permute-start(bf16[4,15872]{1,0:T(4,128)(2,1)S(1)} %get-tuple-element.29.refs_0_), channel_id=1, source_target_pairs={{0,4},{4,0},{8,12},{12,8},{16,20},{20,16},{24,28},{28,24},{32,36},... | collective-permute-start | bytes 380936 | tf_op jit(solution)/shard_map/ppermute | solution.py:42
  13.7 0.0 copy-start
  13.7 0.9 %copy-done = bf16[1024,128]{1,0:T(8,128)(2,1)S(1)} copy-done((bf16[1024,128]{1,0:T(8,128)(2,1)S(1)}, bf16[1024,128]{1,0:T(8,128)(2,1)}, u32[]{:S(2)}) %copy-start) | copy-done | bytes 262168
  14.6 0.4 shard_map.83.weight
  15.1 0.0 collective-permute-done.1.refs_2_
  15.1 0.1 collective-permute-start.6
  15.2 0.0 collective-permute-done.3.far
  15.2 0.0 collective-permute-done.2.refs_3_
  15.2 0.0 collective-permute-done.refs_1_
  15.2 1.1 %collective-permute-start.5 = (bf16[4,15872]{1,0:T(4,128)(2,1)S(1)}, bf16[4,15872]{1,0:T(4,128)(2,1)S(1)}, u32[]{:S(2)}, u32[]{:S(2)}) collective-permute-start(bf16[4,15872]{1,0:T(4,128)(2,1)S(1)} %collective-permute-done.refs_1_), channel_id=1, source_target_pairs={{0,4},{4,0},{8,12},{12,8},{16,20},{20,16},{24,28},{28,24},{32,36},... | collective-permute-start | bytes 380936 | tf_op jit(solution)/shard_map/ppermute | solution.py:42
  16.3 0.1 collective-permute-start.7
  16.4 0.0 collective-permute-done.4.refs_4_
  16.4 0.9 %collective-permute-done.5.refs_5_ = bf16[4,15872]{1,0:T(4,128)(2,1)S(1)} collective-permute-done((bf16[4,15872]{1,0:T(4,128)(2,1)S(1)}, bf16[4,15872]{1,0:T(4,128)(2,1)S(1)}, u32[]{:S(2)}, u32[]{:S(2)}) %collective-permute-start.5) | collective-permute-done | bytes 127008 | tf_op jit(solution)/shard_map/ppermute | solution.py:42
  17.3 0.0 collective-permute-done.6.refs_6_
  17.3 0.4 collective-permute-done.7.refs_7_
  17.6 0.6 shard_map.84
  18.2 3.5 %collective-permute-start.13 = (bf16[32,12672]{1,0:T(8,128)(2,1)S(1)}, bf16[32,12672]{1,0:T(8,128)(2,1)S(1)}, u32[]{:S(2)}, u32[]{:S(2)}) collective-permute-start(bf16[32,12672]{1,0:T(8,128)(2,1)S(1)} %get-tuple-element.38.refs_9_), channel_id=1, source_target_pairs={{0,32},{4,100},{8,40},{12,108},{16,48},{20,116},{24,56},{28,124},{... | collective-permute-start | bytes 2433032 | tf_op jit(solution)/shard_map/ppermute | solution.py:56
  21.7 0.0 collective-permute-start.10
  21.7 2.5 %collective-permute-start.9 = (bf16[32,3200]{1,0:T(8,128)(2,1)S(1)}, bf16[32,3200]{1,0:T(8,128)(2,1)S(1)}, u32[]{:S(2)}, u32[]{:S(2)}) collective-permute-start(bf16[32,3200]{1,0:T(8,128)(2,1)S(1)} %get-tuple-element.36.after), channel_id=1, source_target_pairs={{0,1},{1,33},{2,65},{3,97},{4,7},{5,39},{6,71},{7,103},{8,9},{9,41... | collective-permute-start | bytes 614408 | tf_op jit(solution)/shard_map/ppermute | solution.py:68
  24.2 4.4 %collective-permute-start.8 = (bf16[32,3200]{1,0:T(8,128)(2,1)S(1)}, bf16[32,3200]{1,0:T(8,128)(2,1)S(1)}, u32[]{:S(2)}, u32[]{:S(2)}) collective-permute-start(bf16[32,3200]{1,0:T(8,128)(2,1)S(1)} %get-tuple-element.36.after), channel_id=1, source_target_pairs={{0,0},{1,32},{2,64},{3,96},{4,6},{5,38},{6,70},{7,102},{8,8},{9,40... | collective-permute-start | bytes 614408 | tf_op jit(solution)/shard_map/ppermute | solution.py:68
  28.6 0.0 collective-permute-done.10.far_other
  28.6 0.1 shard_map.85.refs_4_
  28.8 2.1 %collective-permute-start.11 = (bf16[8,12672]{1,0:T(8,128)(2,1)S(1)}, bf16[8,12672]{1,0:T(8,128)(2,1)S(1)}, u32[]{:S(2)}, u32[]{:S(2)}) collective-permute-start(bf16[8,12672]{1,0:T(8,128)(2,1)S(1)} %shard_map.85.refs_4_), channel_id=1, source_target_pairs={{0,8},{4,28},{8,16},{12,4},{16,24},{20,12},{24,0},{28,20},{32,40},... | collective-permute-start | bytes 608264 | tf_op jit(solution)/shard_map/ppermute | solution.py:56
  30.8 0.2 collective-permute-start.12
  31.0 4.8 %collective-permute-done.12.refs_7_ = bf16[4,12672]{1,0:T(4,128)(2,1)S(1)} collective-permute-done((bf16[4,12672]{1,0:T(4,128)(2,1)S(1)}, bf16[4,12672]{1,0:T(4,128)(2,1)S(1)}, u32[]{:S(2)}, u32[]{:S(2)}) %collective-permute-start.12) | collective-permute-done | bytes 101408 | tf_op jit(solution)/shard_map/ppermute | solution.py:42
  35.8 0.0 collective-permute-done.11.refs_5_
  35.8 0.0 collective-permute-done.9.refs_1_
  35.8 0.8 %collective-permute-done.8.refs_0_ = bf16[32,3200]{1,0:T(8,128)(2,1)S(1)} collective-permute-done((bf16[32,3200]{1,0:T(8,128)(2,1)S(1)}, bf16[32,3200]{1,0:T(8,128)(2,1)S(1)}, u32[]{:S(2)}, u32[]{:S(2)}) %collective-permute-start.8) | collective-permute-done | bytes 204832 | tf_op jit(solution)/shard_map/ppermute | solution.py:68
  36.6 0.0 collective-permute-done.13.refs_10_
  36.6 0.0 collective-permute-start.14
  36.6 0.5 collective-permute-start.15
  37.1 0.0 collective-permute-start.16
  37.1 0.5 collective-permute-start.17
  37.6 1.2 %collective-permute-done.17.refs_8_ = bf16[4,12672]{1,0:T(4,128)(2,1)S(1)} collective-permute-done((bf16[4,12672]{1,0:T(4,128)(2,1)S(1)}, bf16[4,12672]{1,0:T(4,128)(2,1)S(1)}, u32[]{:S(2)}, u32[]{:S(2)}) %collective-permute-start.17) | collective-permute-done | bytes 101408 | tf_op jit(solution)/shard_map/ppermute | solution.py:42
  38.8 0.0 collective-permute-done.16.refs_6_
  38.8 0.0 collective-permute-done.14.refs_2_
  38.8 0.0 collective-permute-done.15.refs_3_
  38.8 0.5 collective-permute-start.18
  39.3 1.5 %shard_map.86 = (bf16[1536,128]{1,0:T(8,128)(2,1)S(1)}, bf16[48,128]{1,0:T(8,128)(2,1)S(1)}, bf16[128,12672]{1,0:T(8,128)(2,1)S(1)}) custom-call(bf16[32,3200]{1,0:T(8,128)(2,1)S(1)} %collective-permute-done.8.refs_0_, bf16[32,3200]{1,0:T(8,128)(2,1)S(1)} %collective-permute-done.9.refs_1_, bf16[32,3200]{1,0:T(8,128)(2,1)S(1)} %collective-permute-done.14.refs_2_, ...), custom_call_target="tpu_custom_call" | custom-call | tf_op jit(solution)/shard_map/pallas_call | solution.py:307
  40.8 0.6 %collective-permute-done.18.right_part = bf16[32,12672]{1,0:T(8,128)(2,1)S(1)} collective-permute-done((bf16[32,12672]{1,0:T(8,128)(2,1)S(1)}, bf16[32,12672]{1,0:T(8,128)(2,1)S(1)}, u32[]{:S(2)}, u32[]{:S(2)}) %collective-permute-start.18) | collective-permute-done | bytes 811040 | tf_op jit(solution)/shard_map/ppermute | solution.py:42
  41.4 0.1 shard_map.87.right
  41.5 16.9 %shard_map.88 = bf16[48,384,128]{2,1,0:T(8,128)(2,1)} custom-call(bf16[1536,128]{1,0:T(8,128)(2,1)S(1)} %get-tuple-element.49.left, bf16[48,128]{1,0:T(8,128)(2,1)S(1)} %get-tuple-element.50.left_mask, bf16[128,1024]{1,0:T(8,128)(2,1)S(1)} %shard_map.83.weight, bf16[128,12672]{1,0:T(8,128)(2,1)S(1)} %shard_map.87.right), custom_call_target="tpu_custom_call" | custom-call | tf_op jit(solution)/shard_map/pallas_call | solution.py:354
Async XLA Ops:
  3.0 12.1 %collective-permute-start.1 = (bf16[4,15872]{1,0:T(4,128)(2,1)S(1)}, bf16[4,15872]{1,0:T(4,128)(2,1)S(1)}, u32[]{:S(2)}, u32[]{:S(2)}) collective-permute-start(bf16[4,15872]{1,0:T(4,128)(2,1)S(1)} %get-tuple-element.31), channel_id=1, source_target_pairs={{0,16},{4,20},{8,24},{12,28},{16,0},{20,4},{24,8},{28,12},{32,48},... | collective-permute-start | bytes 380936 | tf_op jit(solution)/shard_map/ppermute | solution.py:42
  6.8 8.4 %collective-permute-start.2 = (bf16[4,15872]{1,0:T(4,128)(2,1)S(1)}, bf16[4,15872]{1,0:T(4,128)(2,1)S(1)}, u32[]{:S(2)}, u32[]{:S(2)}) collective-permute-start(bf16[4,15872]{1,0:T(4,128)(2,1)S(1)} %get-tuple-element.33), channel_id=1, source_target_pairs={{0,24},{4,28},{8,0},{12,4},{16,8},{20,12},{24,16},{28,20},{32,56},... | collective-permute-start | bytes 380936 | tf_op jit(solution)/shard_map/ppermute | solution.py:42
  7.6 7.6 %collective-permute-start = (bf16[4,15872]{1,0:T(4,128)(2,1)S(1)}, bf16[4,15872]{1,0:T(4,128)(2,1)S(1)}, u32[]{:S(2)}, u32[]{:S(2)}) collective-permute-start(bf16[4,15872]{1,0:T(4,128)(2,1)S(1)} %get-tuple-element.30), channel_id=1, source_target_pairs={{0,8},{4,12},{8,16},{12,20},{16,24},{20,28},{24,0},{28,4},{32,40},... | collective-permute-start | bytes 380936 | tf_op jit(solution)/shard_map/ppermute | solution.py:42
  8.3 6.9 %collective-permute-start.3 = (bf16[4,12672]{1,0:T(4,128)(2,1)S(1)}, bf16[4,12672]{1,0:T(4,128)(2,1)S(1)}, u32[]{:S(2)}, u32[]{:S(2)}) collective-permute-start(bf16[4,12672]{1,0:T(4,128)(2,1)S(1)} %get-tuple-element.34), channel_id=1, source_target_pairs={{0,64},{4,68},{8,72},{12,76},{16,80},{20,84},{24,88},{28,92},{32,9... | collective-permute-start | bytes 304136 | tf_op jit(solution)/shard_map/ppermute | solution.py:42
  11.9 4.5 %collective-permute-start.4 = (bf16[4,15872]{1,0:T(4,128)(2,1)S(1)}, bf16[4,15872]{1,0:T(4,128)(2,1)S(1)}, u32[]{:S(2)}, u32[]{:S(2)}) collective-permute-start(bf16[4,15872]{1,0:T(4,128)(2,1)S(1)} %get-tuple-element.29.refs_0_), channel_id=1, source_target_pairs={{0,4},{4,0},{8,12},{12,8},{16,20},{20,16},{24,28},{28,24},{32,36},... | collective-permute-start | bytes 380936 | tf_op jit(solution)/shard_map/ppermute | solution.py:42
  13.7 0.9 %copy-start = (bf16[1024,128]{1,0:T(8,128)(2,1)S(1)}, bf16[1024,128]{1,0:T(8,128)(2,1)}, u32[]{:S(2)}) copy-start(bf16[1024,128]{1,0:T(8,128)(2,1)} %weight_hbm.1) | copy-start | bytes 786436
  15.1 2.2 %collective-permute-start.6 = (bf16[4,15872]{1,0:T(4,128)(2,1)S(1)}, bf16[4,15872]{1,0:T(4,128)(2,1)S(1)}, u32[]{:S(2)}, u32[]{:S(2)}) collective-permute-start(bf16[4,15872]{1,0:T(4,128)(2,1)S(1)} %collective-permute-done.1.refs_2_), channel_id=1, source_target_pairs={{0,4},{4,0},{8,12},{12,8},{16,20},{20,16},{24,28},{28,24},{32,36},... | collective-permute-start | bytes 380936 | tf_op jit(solution)/shard_map/ppermute | solution.py:42
  15.2 2.1 %collective-permute-start.5 = (bf16[4,15872]{1,0:T(4,128)(2,1)S(1)}, bf16[4,15872]{1,0:T(4,128)(2,1)S(1)}, u32[]{:S(2)}, u32[]{:S(2)}) collective-permute-start(bf16[4,15872]{1,0:T(4,128)(2,1)S(1)} %collective-permute-done.refs_1_), channel_id=1, source_target_pairs={{0,4},{4,0},{8,12},{12,8},{16,20},{20,16},{24,28},{28,24},{32,36},... | collective-permute-start | bytes 380936 | tf_op jit(solution)/shard_map/ppermute | solution.py:42
  16.3 1.3 %collective-permute-start.7 = (bf16[4,15872]{1,0:T(4,128)(2,1)S(1)}, bf16[4,15872]{1,0:T(4,128)(2,1)S(1)}, u32[]{:S(2)}, u32[]{:S(2)}) collective-permute-start(bf16[4,15872]{1,0:T(4,128)(2,1)S(1)} %collective-permute-done.2.refs_3_), channel_id=1, source_target_pairs={{0,4},{4,0},{8,12},{12,8},{16,20},{20,16},{24,28},{28,24},{32,36},... | collective-permute-start | bytes 380936 | tf_op jit(solution)/shard_map/ppermute | solution.py:42
  18.2 18.4 %collective-permute-start.13 = (bf16[32,12672]{1,0:T(8,128)(2,1)S(1)}, bf16[32,12672]{1,0:T(8,128)(2,1)S(1)}, u32[]{:S(2)}, u32[]{:S(2)}) collective-permute-start(bf16[32,12672]{1,0:T(8,128)(2,1)S(1)} %get-tuple-element.38.refs_9_), channel_id=1, source_target_pairs={{0,32},{4,100},{8,40},{12,108},{16,48},{20,116},{24,56},{28,124},{... | collective-permute-start | bytes 2433032 | tf_op jit(solution)/shard_map/ppermute | solution.py:56
  21.7 6.9 %collective-permute-start.10 = (bf16[4,12672]{1,0:T(4,128)(2,1)S(1)}, bf16[4,12672]{1,0:T(4,128)(2,1)S(1)}, u32[]{:S(2)}, u32[]{:S(2)}) collective-permute-start(bf16[4,12672]{1,0:T(4,128)(2,1)S(1)} %collective-permute-done.3.far), channel_id=1, source_target_pairs={{0,4},{4,0},{8,12},{12,8},{16,20},{20,16},{24,28},{28,24},{32,36},... | collective-permute-start | bytes 304136 | tf_op jit(solution)/shard_map/ppermute | solution.py:42
  21.7 14.1 %collective-permute-start.9 = (bf16[32,3200]{1,0:T(8,128)(2,1)S(1)}, bf16[32,3200]{1,0:T(8,128)(2,1)S(1)}, u32[]{:S(2)}, u32[]{:S(2)}) collective-permute-start(bf16[32,3200]{1,0:T(8,128)(2,1)S(1)} %get-tuple-element.36.after), channel_id=1, source_target_pairs={{0,1},{1,33},{2,65},{3,97},{4,7},{5,39},{6,71},{7,103},{8,9},{9,41... | collective-permute-start | bytes 614408 | tf_op jit(solution)/shard_map/ppermute | solution.py:68
  24.2 12.4 %collective-permute-start.8 = (bf16[32,3200]{1,0:T(8,128)(2,1)S(1)}, bf16[32,3200]{1,0:T(8,128)(2,1)S(1)}, u32[]{:S(2)}, u32[]{:S(2)}) collective-permute-start(bf16[32,3200]{1,0:T(8,128)(2,1)S(1)} %get-tuple-element.36.after), channel_id=1, source_target_pairs={{0,0},{1,32},{2,64},{3,96},{4,6},{5,38},{6,70},{7,102},{8,8},{9,40... | collective-permute-start | bytes 614408 | tf_op jit(solution)/shard_map/ppermute | solution.py:68
  28.8 7.1 %collective-permute-start.11 = (bf16[8,12672]{1,0:T(8,128)(2,1)S(1)}, bf16[8,12672]{1,0:T(8,128)(2,1)S(1)}, u32[]{:S(2)}, u32[]{:S(2)}) collective-permute-start(bf16[8,12672]{1,0:T(8,128)(2,1)S(1)} %shard_map.85.refs_4_), channel_id=1, source_target_pairs={{0,8},{4,28},{8,16},{12,4},{16,24},{20,12},{24,0},{28,20},{32,40},... | collective-permute-start | bytes 608264 | tf_op jit(solution)/shard_map/ppermute | solution.py:56
  30.8 5.0 %collective-permute-start.12 = (bf16[4,12672]{1,0:T(4,128)(2,1)S(1)}, bf16[4,12672]{1,0:T(4,128)(2,1)S(1)}, u32[]{:S(2)}, u32[]{:S(2)}) collective-permute-start(bf16[4,12672]{1,0:T(4,128)(2,1)S(1)} %collective-permute-done.3.far), channel_id=1, source_target_pairs={{0,16},{4,20},{8,24},{12,28},{16,0},{20,4},{24,8},{28,12},{32,48},... | collective-permute-start | bytes 304136 | tf_op jit(solution)/shard_map/ppermute | solution.py:42
  36.6 2.2 %collective-permute-start.14 = (bf16[32,3200]{1,0:T(8,128)(2,1)S(1)}, bf16[32,3200]{1,0:T(8,128)(2,1)S(1)}, u32[]{:S(2)}, u32[]{:S(2)}) collective-permute-start(bf16[32,3200]{1,0:T(8,128)(2,1)S(1)} %collective-permute-done.8.refs_0_), channel_id=1, source_target_pairs={{0,4},{4,0},{8,12},{12,8},{16,20},{20,16},{24,28},{28,24},{32,36},... | collective-permute-start | bytes 614408 | tf_op jit(solution)/shard_map/ppermute | solution.py:42
  36.6 2.2 %collective-permute-start.15 = (bf16[32,3200]{1,0:T(8,128)(2,1)S(1)}, bf16[32,3200]{1,0:T(8,128)(2,1)S(1)}, u32[]{:S(2)}, u32[]{:S(2)}) collective-permute-start(bf16[32,3200]{1,0:T(8,128)(2,1)S(1)} %collective-permute-done.9.refs_1_), channel_id=1, source_target_pairs={{0,4},{4,0},{8,12},{12,8},{16,20},{20,16},{24,28},{28,24},{32,36},... | collective-permute-start | bytes 614408 | tf_op jit(solution)/shard_map/ppermute | solution.py:42
  37.1 1.7 %collective-permute-start.16 = (bf16[8,12672]{1,0:T(8,128)(2,1)S(1)}, bf16[8,12672]{1,0:T(8,128)(2,1)S(1)}, u32[]{:S(2)}, u32[]{:S(2)}) collective-permute-start(bf16[8,12672]{1,0:T(8,128)(2,1)S(1)} %collective-permute-done.11.refs_5_), channel_id=1, source_target_pairs={{0,4},{4,0},{8,12},{12,8},{16,20},{20,16},{24,28},{28,24},{32,36},... | collective-permute-start | bytes 608264 | tf_op jit(solution)/shard_map/ppermute | solution.py:42
  37.1 1.7 %collective-permute-start.17 = (bf16[4,12672]{1,0:T(4,128)(2,1)S(1)}, bf16[4,12672]{1,0:T(4,128)(2,1)S(1)}, u32[]{:S(2)}, u32[]{:S(2)}) collective-permute-start(bf16[4,12672]{1,0:T(4,128)(2,1)S(1)} %collective-permute-done.12.refs_7_), channel_id=1, source_target_pairs={{0,4},{4,0},{8,12},{12,8},{16,20},{20,16},{24,28},{28,24},{32,36},... | collective-permute-start | bytes 304136 | tf_op jit(solution)/shard_map/ppermute | solution.py:42
  38.8 2.6 %collective-permute-start.18 = (bf16[32,12672]{1,0:T(8,128)(2,1)S(1)}, bf16[32,12672]{1,0:T(8,128)(2,1)S(1)}, u32[]{:S(2)}, u32[]{:S(2)}) collective-permute-start(bf16[32,12672]{1,0:T(8,128)(2,1)S(1)} %collective-permute-done.13.refs_10_), channel_id=1, source_target_pairs={{0,4},{4,0},{8,12},{12,8},{16,20},{20,16},{24,28},{28,24},{32,36},... | collective-permute-start | bytes 2433032 | tf_op jit(solution)/shard_map/ppermute | solution.py:42

commit v7 on v6

--- a/solution.py
+++ b/solution.py
@@ -63,7 +63,7 @@
             for c in range(CORES):
                 for x in range(RING):
                     source = ((z * RING + y) * CORES + c) * RING + x
-                    target = ((x * RING + y) * CORES + c) * RING + (z + k + 2 * c) % RING
+                    target = ((x * RING + y) * CORES + c) * RING + (z ^ x ^ (k + 2 * c))
                     pairs.append((source, target))
     return lax.ppermute(value, ("res", "col"), pairs)
 
@@ -274,7 +274,8 @@
     for copy in copies:
         copy.start()
     for at, part in enumerate(parts):
-        group = lax.rem(z - x + at + 2 * core + RING, RING)
+        source = z ^ x ^ lax.rem(at + 2 * core, RING)
+        group = lax.rem(z - source + RING, RING)
         stacked[pl.ds(pl.multiple_of(group * CHIP, CHIP), CHIP), :] = part[...]
 
     def block_at(at):

time: 59.5 us -> 59.9 us (level)
  starting transfers between devices: 26.1 us -> 27.4 us
  waiting for transfers between devices: 8.64 us -> 7.85 us
    ppermute x2, starting transfers between devices: 6.91 us -> 8.16 us  [to_row_owner(): return lax.ppermute(value, ('res', 'col'), pairs)]
    ppermute x2, waiting for transfers between devices: 0.79 us -> 0.01 us  [to_row_owner(): return lax.ppermute(value, ('res', 'col'), pairs)]
  transfers between devices with their start and end apart: 19 -> 19, of which waited for: 6 -> 5; matrix products, arithmetic and copies ran while one was open for 0% -> 0% of each run, Pallas kernels for 4% -> 3%
where the time goes in v7:
time: 59.9 us; the launch traced here: 59 us
  starting transfers between devices  27.4 us (46%)
  Pallas kernels  22.6 us (38%)
  waiting for transfers between devices  7.85 us (13%)
  local copies, waits for them, and re-layouts  0.95 us (2%)
    pallas_call x1, Pallas kernels, pair(): pl.pallas_call(functools.partial(pair_kernel, block, beside), grid=(ROWS...  16.9 us
    ppermute x15, starting transfers between devices, res_shift(): return lax.ppermute(value, 'res', pairs)  13.7 us
    ppermute x2, starting transfers between devices, to_row_owner(): return lax.ppermute(value, ('res', 'col'), pairs)  8.16 us
    ppermute x15, waiting for transfers between devices, res_shift(): return lax.ppermute(value, 'res', pairs)  7.84 us
    ppermute x2, starting transfers between devices, both_ways(): return lax.ppermute(value, 'res', pairs)  5.53 us
    pallas_call x1, Pallas kernels, project(): pl.pallas_call(project_kernel, in_specs=[pl.BlockSpec(memory_space=pltpu....  2.98 us
    pallas_call x1, Pallas kernels, arrange_left(): pl.pallas_call(left_kernel, in_specs=[vmem] * (len(parts) + len(fars)) +...  1.49 us
  transfers between devices with their start and end apart: 19, of which 5 were waited for; matrix products, arithmetic and copies ran while one was open for 0% of the time, Pallas kernels for 3%

profile of v7, /device:TPU:1, one launch (start us, length us, event | category | flops | bytes accessed | tf_op | source)
XLA Modules:
  0.0 59.0 jit_solution(5815007642992362761)
XLA Ops:
  0.0 3.0 %shard_map.82 = (bf16[4,15872]{1,0:T(4,128)(2,1)S(1)}, bf16[4,15872]{1,0:T(4,128)(2,1)S(1)}, bf16[4,15872]{1,0:T(4,128)(2,1)S(1)}, bf16[4,15872]{1,0:T(4,128)(2,1)S(1)}, bf16[4,12672]{1,0:T(4,128)(2,1)S(1)}) custom-call(bf16[4,384,256]{2,1,0:T(8,128)(2,1)} %refs_0_.1, bf16[4,8]{1,0:T(4,128)(2,1)} %refs_1_.1, s32[384]{0:T(512)} %refs_2_.1, f32[256]{0:T(256)} %refs_3_.1, ...), custom_call_target="tpu_custom_call" | custom-call | tf_op jit(solution)/shard_map/pallas_call | solution.py:131
  3.0 3.8 %collective-permute-start.1 = (bf16[4,15872]{1,0:T(4,128)(2,1)S(1)}, bf16[4,15872]{1,0:T(4,128)(2,1)S(1)}, u32[]{:S(2)}, u32[]{:S(2)}) collective-permute-start(bf16[4,15872]{1,0:T(4,128)(2,1)S(1)} %get-tuple-element.31), channel_id=1, source_target_pairs={{0,16},{4,20},{8,24},{12,28},{16,0},{20,4},{24,8},{28,12},{32,48},... | collective-permute-start | bytes 380936 | tf_op jit(solution)/shard_map/ppermute | solution.py:42
  6.8 0.8 %collective-permute-start.2 = (bf16[4,15872]{1,0:T(4,128)(2,1)S(1)}, bf16[4,15872]{1,0:T(4,128)(2,1)S(1)}, u32[]{:S(2)}, u32[]{:S(2)}) collective-permute-start(bf16[4,15872]{1,0:T(4,128)(2,1)S(1)} %get-tuple-element.33), channel_id=1, source_target_pairs={{0,24},{4,28},{8,0},{12,4},{16,8},{20,12},{24,16},{28,20},{32,56},... | collective-permute-start | bytes 380936 | tf_op jit(solution)/shard_map/ppermute | solution.py:42
  7.6 0.7 %collective-permute-start = (bf16[4,15872]{1,0:T(4,128)(2,1)S(1)}, bf16[4,15872]{1,0:T(4,128)(2,1)S(1)}, u32[]{:S(2)}, u32[]{:S(2)}) collective-permute-start(bf16[4,15872]{1,0:T(4,128)(2,1)S(1)} %get-tuple-element.30), channel_id=1, source_target_pairs={{0,8},{4,12},{8,16},{12,20},{16,24},{20,28},{24,0},{28,4},{32,40},... | collective-permute-start | bytes 380936 | tf_op jit(solution)/shard_map/ppermute | solution.py:42
  8.3 3.6 %collective-permute-start.3 = (bf16[4,12672]{1,0:T(4,128)(2,1)S(1)}, bf16[4,12672]{1,0:T(4,128)(2,1)S(1)}, u32[]{:S(2)}, u32[]{:S(2)}) collective-permute-start(bf16[4,12672]{1,0:T(4,128)(2,1)S(1)} %get-tuple-element.34), channel_id=1, source_target_pairs={{0,64},{4,68},{8,72},{12,76},{16,80},{20,84},{24,88},{28,92},{32,9... | collective-permute-start | bytes 304136 | tf_op jit(solution)/shard_map/ppermute | solution.py:42
  11.9 1.8 %collective-permute-start.4 = (bf16[4,15872]{1,0:T(4,128)(2,1)S(1)}, bf16[4,15872]{1,0:T(4,128)(2,1)S(1)}, u32[]{:S(2)}, u32[]{:S(2)}) collective-permute-start(bf16[4,15872]{1,0:T(4,128)(2,1)S(1)} %get-tuple-element.29.refs_0_), channel_id=1, source_target_pairs={{0,4},{4,0},{8,12},{12,8},{16,20},{20,16},{24,28},{28,24},{32,36},... | collective-permute-start | bytes 380936 | tf_op jit(solution)/shard_map/ppermute | solution.py:42
  13.7 0.0 copy-start
  13.7 0.9 %copy-done = bf16[1024,128]{1,0:T(8,128)(2,1)S(1)} copy-done((bf16[1024,128]{1,0:T(8,128)(2,1)S(1)}, bf16[1024,128]{1,0:T(8,128)(2,1)}, u32[]{:S(2)}) %copy-start) | copy-done | bytes 262168
  14.6 0.4 shard_map.83.weight
  15.1 0.0 collective-permute-done.1.refs_2_
  15.1 0.1 collective-permute-start.6
  15.2 0.0 collective-permute-done.3.far
  15.2 0.0 collective-permute-done.2.refs_3_
  15.2 0.0 collective-permute-done.refs_1_
  15.2 1.1 %collective-permute-start.5 = (bf16[4,15872]{1,0:T(4,128)(2,1)S(1)}, bf16[4,15872]{1,0:T(4,128)(2,1)S(1)}, u32[]{:S(2)}, u32[]{:S(2)}) collective-permute-start(bf16[4,15872]{1,0:T(4,128)(2,1)S(1)} %collective-permute-done.refs_1_), channel_id=1, source_target_pairs={{0,4},{4,0},{8,12},{12,8},{16,20},{20,16},{24,28},{28,24},{32,36},... | collective-permute-start | bytes 380936 | tf_op jit(solution)/shard_map/ppermute | solution.py:42
  16.3 0.1 collective-permute-start.7
  16.4 0.0 collective-permute-done.4.refs_4_
  16.4 0.9 %collective-permute-done.5.refs_5_ = bf16[4,15872]{1,0:T(4,128)(2,1)S(1)} collective-permute-done((bf16[4,15872]{1,0:T(4,128)(2,1)S(1)}, bf16[4,15872]{1,0:T(4,128)(2,1)S(1)}, u32[]{:S(2)}, u32[]{:S(2)}) %collective-permute-start.5) | collective-permute-done | bytes 127008 | tf_op jit(solution)/shard_map/ppermute | solution.py:42
  17.3 0.0 collective-permute-done.6.refs_6_
  17.3 0.4 collective-permute-done.7.refs_7_
  17.6 0.6 shard_map.84
  18.2 3.5 %collective-permute-start.13 = (bf16[32,12672]{1,0:T(8,128)(2,1)S(1)}, bf16[32,12672]{1,0:T(8,128)(2,1)S(1)}, u32[]{:S(2)}, u32[]{:S(2)}) collective-permute-start(bf16[32,12672]{1,0:T(8,128)(2,1)S(1)} %get-tuple-element.38.refs_9_), channel_id=1, source_target_pairs={{0,32},{4,100},{8,40},{12,108},{16,48},{20,116},{24,56},{28,124},{... | collective-permute-start | bytes 2433032 | tf_op jit(solution)/shard_map/ppermute | solution.py:56
  21.7 0.0 collective-permute-start.10
  21.7 4.4 %collective-permute-start.9 = (bf16[32,3200]{1,0:T(8,128)(2,1)S(1)}, bf16[32,3200]{1,0:T(8,128)(2,1)S(1)}, u32[]{:S(2)}, u32[]{:S(2)}) collective-permute-start(bf16[32,3200]{1,0:T(8,128)(2,1)S(1)} %get-tuple-element.36.after), channel_id=1, source_target_pairs={{0,1},{1,32},{2,67},{3,98},{4,7},{5,38},{6,69},{7,100},{8,9},{9,40... | collective-permute-start | bytes 614408 | tf_op jit(solution)/shard_map/ppermute | solution.py:68
  26.1 3.8 %collective-permute-start.8 = (bf16[32,3200]{1,0:T(8,128)(2,1)S(1)}, bf16[32,3200]{1,0:T(8,128)(2,1)S(1)}, u32[]{:S(2)}, u32[]{:S(2)}) collective-permute-start(bf16[32,3200]{1,0:T(8,128)(2,1)S(1)} %get-tuple-element.36.after), channel_id=1, source_target_pairs={{0,0},{1,33},{2,66},{3,99},{4,6},{5,39},{6,68},{7,101},{8,8},{9,41... | collective-permute-start | bytes 614408 | tf_op jit(solution)/shard_map/ppermute | solution.py:68
  29.9 0.0 collective-permute-done.10.far_other
  29.9 0.1 shard_map.85.refs_4_
  30.0 2.1 %collective-permute-start.11 = (bf16[8,12672]{1,0:T(8,128)(2,1)S(1)}, bf16[8,12672]{1,0:T(8,128)(2,1)S(1)}, u32[]{:S(2)}, u32[]{:S(2)}) collective-permute-start(bf16[8,12672]{1,0:T(8,128)(2,1)S(1)} %shard_map.85.refs_4_), channel_id=1, source_target_pairs={{0,8},{4,28},{8,16},{12,4},{16,24},{20,12},{24,0},{28,20},{32,40},... | collective-permute-start | bytes 608264 | tf_op jit(solution)/shard_map/ppermute | solution.py:56
  32.1 0.2 collective-permute-start.12
  32.3 4.8 %collective-permute-done.12.refs_7_ = bf16[4,12672]{1,0:T(4,128)(2,1)S(1)} collective-permute-done((bf16[4,12672]{1,0:T(4,128)(2,1)S(1)}, bf16[4,12672]{1,0:T(4,128)(2,1)S(1)}, u32[]{:S(2)}, u32[]{:S(2)}) %collective-permute-start.12) | collective-permute-done | bytes 101408 | tf_op jit(solution)/shard_map/ppermute | solution.py:42
  37.1 0.0 collective-permute-done.11.refs_5_
  37.1 0.0 collective-permute-done.9.refs_1_
  37.1 0.0 collective-permute-done.8.refs_0_
  37.1 0.0 collective-permute-done.13.refs_10_
  37.1 0.1 collective-permute-start.14
  37.2 0.5 collective-permute-start.15
  37.7 0.1 collective-permute-start.16
  37.8 0.4 collective-permute-start.17
  38.2 1.2 %collective-permute-done.17.refs_8_ = bf16[4,12672]{1,0:T(4,128)(2,1)S(1)} collective-permute-done((bf16[4,12672]{1,0:T(4,128)(2,1)S(1)}, bf16[4,12672]{1,0:T(4,128)(2,1)S(1)}, u32[]{:S(2)}, u32[]{:S(2)}) %collective-permute-start.17) | collective-permute-done | bytes 101408 | tf_op jit(solution)/shard_map/ppermute | solution.py:42
  39.4 0.0 collective-permute-done.16.refs_6_
  39.4 0.0 collective-permute-done.14.refs_2_
  39.4 0.0 collective-permute-done.15.refs_3_
  39.4 0.5 collective-permute-start.18
  39.8 1.5 %shard_map.86 = (bf16[1536,128]{1,0:T(8,128)(2,1)S(1)}, bf16[48,128]{1,0:T(8,128)(2,1)S(1)}, bf16[128,12672]{1,0:T(8,128)(2,1)S(1)}) custom-call(bf16[32,3200]{1,0:T(8,128)(2,1)S(1)} %collective-permute-done.8.refs_0_, bf16[32,3200]{1,0:T(8,128)(2,1)S(1)} %collective-permute-done.9.refs_1_, bf16[32,3200]{1,0:T(8,128)(2,1)S(1)} %collective-permute-done.14.refs_2_, ...), custom_call_target="tpu_custom_call" | custom-call | tf_op jit(solution)/shard_map/pallas_call | solution.py:308
  41.3 0.6 %collective-permute-done.18.right_part = bf16[32,12672]{1,0:T(8,128)(2,1)S(1)} collective-permute-done((bf16[32,12672]{1,0:T(8,128)(2,1)S(1)}, bf16[32,12672]{1,0:T(8,128)(2,1)S(1)}, u32[]{:S(2)}, u32[]{:S(2)}) %collective-permute-start.18) | collective-permute-done | bytes 811040 | tf_op jit(solution)/shard_map/ppermute | solution.py:42
  41.9 0.1 shard_map.87.right
  42.0 16.9 %shard_map.88 = bf16[48,384,128]{2,1,0:T(8,128)(2,1)} custom-call(bf16[1536,128]{1,0:T(8,128)(2,1)S(1)} %get-tuple-element.49.left, bf16[48,128]{1,0:T(8,128)(2,1)S(1)} %get-tuple-element.50.left_mask, bf16[128,1024]{1,0:T(8,128)(2,1)S(1)} %shard_map.83.weight, bf16[128,12672]{1,0:T(8,128)(2,1)S(1)} %shard_map.87.right), custom_call_target="tpu_custom_call" | custom-call | tf_op jit(solution)/shard_map/pallas_call | solution.py:355
Async XLA Ops:
  3.0 12.1 %collective-permute-start.1 = (bf16[4,15872]{1,0:T(4,128)(2,1)S(1)}, bf16[4,15872]{1,0:T(4,128)(2,1)S(1)}, u32[]{:S(2)}, u32[]{:S(2)}) collective-permute-start(bf16[4,15872]{1,0:T(4,128)(2,1)S(1)} %get-tuple-element.31), channel_id=1, source_target_pairs={{0,16},{4,20},{8,24},{12,28},{16,0},{20,4},{24,8},{28,12},{32,48},... | collective-permute-start | bytes 380936 | tf_op jit(solution)/shard_map/ppermute | solution.py:42
  6.8 8.4 %collective-permute-start.2 = (bf16[4,15872]{1,0:T(4,128)(2,1)S(1)}, bf16[4,15872]{1,0:T(4,128)(2,1)S(1)}, u32[]{:S(2)}, u32[]{:S(2)}) collective-permute-start(bf16[4,15872]{1,0:T(4,128)(2,1)S(1)} %get-tuple-element.33), channel_id=1, source_target_pairs={{0,24},{4,28},{8,0},{12,4},{16,8},{20,12},{24,16},{28,20},{32,56},... | collective-permute-start | bytes 380936 | tf_op jit(solution)/shard_map/ppermute | solution.py:42
  7.6 7.6 %collective-permute-start = (bf16[4,15872]{1,0:T(4,128)(2,1)S(1)}, bf16[4,15872]{1,0:T(4,128)(2,1)S(1)}, u32[]{:S(2)}, u32[]{:S(2)}) collective-permute-start(bf16[4,15872]{1,0:T(4,128)(2,1)S(1)} %get-tuple-element.30), channel_id=1, source_target_pairs={{0,8},{4,12},{8,16},{12,20},{16,24},{20,28},{24,0},{28,4},{32,40},... | collective-permute-start | bytes 380936 | tf_op jit(solution)/shard_map/ppermute | solution.py:42
  8.3 6.9 %collective-permute-start.3 = (bf16[4,12672]{1,0:T(4,128)(2,1)S(1)}, bf16[4,12672]{1,0:T(4,128)(2,1)S(1)}, u32[]{:S(2)}, u32[]{:S(2)}) collective-permute-start(bf16[4,12672]{1,0:T(4,128)(2,1)S(1)} %get-tuple-element.34), channel_id=1, source_target_pairs={{0,64},{4,68},{8,72},{12,76},{16,80},{20,84},{24,88},{28,92},{32,9... | collective-permute-start | bytes 304136 | tf_op jit(solution)/shard_map/ppermute | solution.py:42
  11.9 4.5 %collective-permute-start.4 = (bf16[4,15872]{1,0:T(4,128)(2,1)S(1)}, bf16[4,15872]{1,0:T(4,128)(2,1)S(1)}, u32[]{:S(2)}, u32[]{:S(2)}) collective-permute-start(bf16[4,15872]{1,0:T(4,128)(2,1)S(1)} %get-tuple-element.29.refs_0_), channel_id=1, source_target_pairs={{0,4},{4,0},{8,12},{12,8},{16,20},{20,16},{24,28},{28,24},{32,36},... | collective-permute-start | bytes 380936 | tf_op jit(solution)/shard_map/ppermute | solution.py:42
  13.7 0.9 %copy-start = (bf16[1024,128]{1,0:T(8,128)(2,1)S(1)}, bf16[1024,128]{1,0:T(8,128)(2,1)}, u32[]{:S(2)}) copy-start(bf16[1024,128]{1,0:T(8,128)(2,1)} %weight_hbm.1) | copy-start | bytes 786436
  15.1 2.2 %collective-permute-start.6 = (bf16[4,15872]{1,0:T(4,128)(2,1)S(1)}, bf16[4,15872]{1,0:T(4,128)(2,1)S(1)}, u32[]{:S(2)}, u32[]{:S(2)}) collective-permute-start(bf16[4,15872]{1,0:T(4,128)(2,1)S(1)} %collective-permute-done.1.refs_2_), channel_id=1, source_target_pairs={{0,4},{4,0},{8,12},{12,8},{16,20},{20,16},{24,28},{28,24},{32,36},... | collective-permute-start | bytes 380936 | tf_op jit(solution)/shard_map/ppermute | solution.py:42
  15.2 2.1 %collective-permute-start.5 = (bf16[4,15872]{1,0:T(4,128)(2,1)S(1)}, bf16[4,15872]{1,0:T(4,128)(2,1)S(1)}, u32[]{:S(2)}, u32[]{:S(2)}) collective-permute-start(bf16[4,15872]{1,0:T(4,128)(2,1)S(1)} %collective-permute-done.refs_1_), channel_id=1, source_target_pairs={{0,4},{4,0},{8,12},{12,8},{16,20},{20,16},{24,28},{28,24},{32,36},... | collective-permute-start | bytes 380936 | tf_op jit(solution)/shard_map/ppermute | solution.py:42
  16.3 1.3 %collective-permute-start.7 = (bf16[4,15872]{1,0:T(4,128)(2,1)S(1)}, bf16[4,15872]{1,0:T(4,128)(2,1)S(1)}, u32[]{:S(2)}, u32[]{:S(2)}) collective-permute-start(bf16[4,15872]{1,0:T(4,128)(2,1)S(1)} %collective-permute-done.2.refs_3_), channel_id=1, source_target_pairs={{0,4},{4,0},{8,12},{12,8},{16,20},{20,16},{24,28},{28,24},{32,36},... | collective-permute-start | bytes 380936 | tf_op jit(solution)/shard_map/ppermute | solution.py:42
  18.2 18.9 %collective-permute-start.13 = (bf16[32,12672]{1,0:T(8,128)(2,1)S(1)}, bf16[32,12672]{1,0:T(8,128)(2,1)S(1)}, u32[]{:S(2)}, u32[]{:S(2)}) collective-permute-start(bf16[32,12672]{1,0:T(8,128)(2,1)S(1)} %get-tuple-element.38.refs_9_), channel_id=1, source_target_pairs={{0,32},{4,100},{8,40},{12,108},{16,48},{20,116},{24,56},{28,124},{... | collective-permute-start | bytes 2433032 | tf_op jit(solution)/shard_map/ppermute | solution.py:56
  21.7 8.2 %collective-permute-start.10 = (bf16[4,12672]{1,0:T(4,128)(2,1)S(1)}, bf16[4,12672]{1,0:T(4,128)(2,1)S(1)}, u32[]{:S(2)}, u32[]{:S(2)}) collective-permute-start(bf16[4,12672]{1,0:T(4,128)(2,1)S(1)} %collective-permute-done.3.far), channel_id=1, source_target_pairs={{0,4},{4,0},{8,12},{12,8},{16,20},{20,16},{24,28},{28,24},{32,36},... | collective-permute-start | bytes 304136 | tf_op jit(solution)/shard_map/ppermute | solution.py:42
  21.7 15.4 %collective-permute-start.9 = (bf16[32,3200]{1,0:T(8,128)(2,1)S(1)}, bf16[32,3200]{1,0:T(8,128)(2,1)S(1)}, u32[]{:S(2)}, u32[]{:S(2)}) collective-permute-start(bf16[32,3200]{1,0:T(8,128)(2,1)S(1)} %get-tuple-element.36.after), channel_id=1, source_target_pairs={{0,1},{1,32},{2,67},{3,98},{4,7},{5,38},{6,69},{7,100},{8,9},{9,40... | collective-permute-start | bytes 614408 | tf_op jit(solution)/shard_map/ppermute | solution.py:68
  26.1 11.0 %collective-permute-start.8 = (bf16[32,3200]{1,0:T(8,128)(2,1)S(1)}, bf16[32,3200]{1,0:T(8,128)(2,1)S(1)}, u32[]{:S(2)}, u32[]{:S(2)}) collective-permute-start(bf16[32,3200]{1,0:T(8,128)(2,1)S(1)} %get-tuple-element.36.after), channel_id=1, source_target_pairs={{0,0},{1,33},{2,66},{3,99},{4,6},{5,39},{6,68},{7,101},{8,8},{9,41... | collective-permute-start | bytes 614408 | tf_op jit(solution)/shard_map/ppermute | solution.py:68
  30.0 7.1 %collective-permute-start.11 = (bf16[8,12672]{1,0:T(8,128)(2,1)S(1)}, bf16[8,12672]{1,0:T(8,128)(2,1)S(1)}, u32[]{:S(2)}, u32[]{:S(2)}) collective-permute-start(bf16[8,12672]{1,0:T(8,128)(2,1)S(1)} %shard_map.85.refs_4_), channel_id=1, source_target_pairs={{0,8},{4,28},{8,16},{12,4},{16,24},{20,12},{24,0},{28,20},{32,40},... | collective-permute-start | bytes 608264 | tf_op jit(solution)/shard_map/ppermute | solution.py:56
  32.1 5.0 %collective-permute-start.12 = (bf16[4,12672]{1,0:T(4,128)(2,1)S(1)}, bf16[4,12672]{1,0:T(4,128)(2,1)S(1)}, u32[]{:S(2)}, u32[]{:S(2)}) collective-permute-start(bf16[4,12672]{1,0:T(4,128)(2,1)S(1)} %collective-permute-done.3.far), channel_id=1, source_target_pairs={{0,16},{4,20},{8,24},{12,28},{16,0},{20,4},{24,8},{28,12},{32,48},... | collective-permute-start | bytes 304136 | tf_op jit(solution)/shard_map/ppermute | solution.py:42
  37.1 2.3 %collective-permute-start.14 = (bf16[32,3200]{1,0:T(8,128)(2,1)S(1)}, bf16[32,3200]{1,0:T(8,128)(2,1)S(1)}, u32[]{:S(2)}, u32[]{:S(2)}) collective-permute-start(bf16[32,3200]{1,0:T(8,128)(2,1)S(1)} %collective-permute-done.8.refs_0_), channel_id=1, source_target_pairs={{0,4},{4,0},{8,12},{12,8},{16,20},{20,16},{24,28},{28,24},{32,36},... | collective-permute-start | bytes 614408 | tf_op jit(solution)/shard_map/ppermute | solution.py:42
  37.2 2.2 %collective-permute-start.15 = (bf16[32,3200]{1,0:T(8,128)(2,1)S(1)}, bf16[32,3200]{1,0:T(8,128)(2,1)S(1)}, u32[]{:S(2)}, u32[]{:S(2)}) collective-permute-start(bf16[32,3200]{1,0:T(8,128)(2,1)S(1)} %collective-permute-done.9.refs_1_), channel_id=1, source_target_pairs={{0,4},{4,0},{8,12},{12,8},{16,20},{20,16},{24,28},{28,24},{32,36},... | collective-permute-start | bytes 614408 | tf_op jit(solution)/shard_map/ppermute | solution.py:42
  37.7 1.7 %collective-permute-start.16 = (bf16[8,12672]{1,0:T(8,128)(2,1)S(1)}, bf16[8,12672]{1,0:T(8,128)(2,1)S(1)}, u32[]{:S(2)}, u32[]{:S(2)}) collective-permute-start(bf16[8,12672]{1,0:T(8,128)(2,1)S(1)} %collective-permute-done.11.refs_5_), channel_id=1, source_target_pairs={{0,4},{4,0},{8,12},{12,8},{16,20},{20,16},{24,28},{28,24},{32,36},... | collective-permute-start | bytes 608264 | tf_op jit(solution)/shard_map/ppermute | solution.py:42
  37.8 1.6 %collective-permute-start.17 = (bf16[4,12672]{1,0:T(4,128)(2,1)S(1)}, bf16[4,12672]{1,0:T(4,128)(2,1)S(1)}, u32[]{:S(2)}, u32[]{:S(2)}) collective-permute-start(bf16[4,12672]{1,0:T(4,128)(2,1)S(1)} %collective-permute-done.12.refs_7_), channel_id=1, source_target_pairs={{0,4},{4,0},{8,12},{12,8},{16,20},{20,16},{24,28},{28,24},{32,36},... | collective-permute-start | bytes 304136 | tf_op jit(solution)/shard_map/ppermute | solution.py:42
  39.4 2.6 %collective-permute-start.18 = (bf16[32,12672]{1,0:T(8,128)(2,1)S(1)}, bf16[32,12672]{1,0:T(8,128)(2,1)S(1)}, u32[]{:S(2)}, u32[]{:S(2)}) collective-permute-start(bf16[32,12672]{1,0:T(8,128)(2,1)S(1)} %collective-permute-done.13.refs_10_), channel_id=1, source_target_pairs={{0,4},{4,0},{8,12},{12,8},{16,20},{20,16},{24,28},{28,24},{32,36},... | collective-permute-start | bytes 2433032 | tf_op jit(solution)/shard_map/ppermute | solution.py:42
